TPU v7x, 32 devices: a whole 2x2x4 slice. The times are simulated.
32 devices in a mesh: region: 4 (over x, core), dom: 8 (over z, y).
Axes of the slice: x: 2, y: 2, z: 4, core: 2. Of those that a mesh axis runs over, the one named last changes fastest.
Arguments:
- embeds: bfloat16 [65536, 256], P(('region', 'dom')), may hold values from -6 to 6
- neighbours: int32 [65536, 8], P(('region', 'dom')), may hold values from 0 to 3071
- halo_send: int32 [256, 128], P(('region', 'dom')), may hold values from 0 to 2047
- gnn_weight: bfloat16 [512, 256], replicated, may hold values from -0.25 to 0.25
- pair_local: int32 [128, 512], P(('region', 'dom')), may hold values from 0 to 2047
- pair_remote: int32 [128, 512], P(('region', 'dom')), may hold values from 0 to 2047
- pair_count: int32 [32, 4], P(('region', 'dom')), may hold values from 1 to 512, as said below
- targets: float32 [128, 512], P(('region', 'dom')), may hold values from -6 to 6
- pair_w1: bfloat16 [512, 256], replicated, may hold values from -0.25 to 0.25
- pair_w2: bfloat16 [256], replicated, may hold values from -0.375 to 0.375
Outputs:
- embeds_grad: bfloat16 [65536, 256], P(('region', 'dom'))
- gnn_grad: float32 [512, 256], replicated
- pair_w1_grad: float32 [512, 256], replicated
- pair_w2_grad: float32 [256], replicated
- loss: float32 [], replicated
Inputs may be any that keep to these rules, and one draw needn't show every extreme that they name: `pair_count`: some partition has 512 live slots for some owner region in every draw.
All inputs are finite; a program needn't handle non-finite values.
Results may differ from a plain program's by a relative error of at most 0.0061.
Values may be sent and summed in bfloat16 or wider, within the bound.
No kernel may reach another device: no remote copies, remote signals or barrier semaphores. Data moves between devices by JAX's collectives and lax.ppermute only.
A program may use at most 128 MiB of HBM per device.

v0:
```python
import jax
import jax.numpy as jnp
from jax import lax
from jax.sharding import PartitionSpec as P

gelu_coef = 0.7978845608


def gelu_tanh(value):
    inner = jnp.tanh(gelu_coef * (value + 0.044715 * value * value * value))
    return 0.5 * value * (1.0 + inner)


def gelu_slope(value):
    inner = jnp.tanh(gelu_coef * (value + 0.044715 * value * value * value))
    return 0.5 * (1.0 + inner) + 0.5 * value * (1.0 - inner * inner) * gelu_coef * (
        1.0 + 3.0 * 0.044715 * value * value
    )


def local(
    embeds,
    neighbours,
    halo_send,
    gnn_weight,
    pair_local,
    pair_remote,
    pair_count,
    targets,
    pair_w1,
    pair_w2,
):
    net_rows = embeds.shape[0]
    feat_width = embeds.shape[1]
    degree = neighbours.shape[1]
    regions = pair_local.shape[0]
    slot_cap = pair_local.shape[1]
    peers = halo_send.shape[0]
    halo_rows = halo_send.shape[1]
    table_rows = net_rows + peers * halo_rows
    nets_total = net_rows * lax.axis_size("region") * lax.axis_size("dom")
    contract_rows = (((0,), (0,)), ((), ()))
    contract_cols = (((1,), (1,)), ((), ()))
    net_ids = jnp.arange(net_rows, dtype=jnp.int32)
    selector = (halo_send.reshape(-1)[:, None] == net_ids[None, :]).astype(jnp.bfloat16)
    outgoing = (
        jnp.dot(selector, embeds, preferred_element_type=jnp.float32)
        .astype(jnp.bfloat16)
        .reshape(peers, halo_rows, feat_width)
    )
    received = lax.all_to_all(outgoing, "dom", split_axis=0, concat_axis=0, tiled=True)
    table = jnp.concatenate([embeds, received.reshape(-1, feat_width)], 0)
    table_ids = jnp.arange(table_rows, dtype=jnp.int32)
    adjacency = jnp.zeros((net_rows, table_rows), jnp.bfloat16)
    for column in range(degree):
        adjacency = adjacency + (neighbours[:, column][:, None] == table_ids[None, :]).astype(
            jnp.bfloat16
        )
    agg_sum = jnp.dot(adjacency, table, preferred_element_type=jnp.float32)
    aggregate = (agg_sum / degree).astype(jnp.bfloat16)
    joined = jnp.concatenate([embeds, aggregate], 1)
    pre = jnp.dot(joined, gnn_weight, preferred_element_type=jnp.float32)
    nets = (embeds.astype(jnp.float32) + gelu_tanh(pre)).astype(jnp.bfloat16)
    local_count = jnp.sum(pair_count).astype(jnp.float32)
    total_count = lax.psum(local_count, ("region", "dom"))
    asked = lax.all_to_all(pair_remote, "region", split_axis=0, concat_axis=0, tiled=True)
    partner = lax.all_to_all(nets[asked], "region", split_axis=0, concat_axis=0, tiled=True)
    victim = nets[pair_local]
    pairs_in = jnp.concatenate([victim, partner], 2).reshape(regions * slot_cap, 2 * feat_width)
    linear = jnp.dot(pairs_in, pair_w1, preferred_element_type=jnp.float32)
    activated = gelu_tanh(linear).astype(jnp.bfloat16)
    scores = jnp.dot(activated, pair_w2, preferred_element_type=jnp.float32)
    slot_ids = jnp.arange(slot_cap, dtype=jnp.int32)
    valid_mask = (
        (slot_ids[None, :] < pair_count.reshape(-1)[:, None]).astype(jnp.float32).reshape(-1)
    )
    errors = (scores - targets.reshape(-1)) * valid_mask
    sq_local = jnp.sum(errors * errors)
    residual = 2.0 * errors
    lin_grad = (
        residual[:, None] * pair_w2.astype(jnp.float32)[None, :] * gelu_slope(linear)
    ).astype(jnp.bfloat16)
    grad_w1 = lax.dot_general(pairs_in, lin_grad, contract_rows, preferred_element_type=jnp.float32)
    grad_w2 = jnp.sum(residual[:, None] * activated.astype(jnp.float32), 0)
    pair_grad = lax.dot_general(
        lin_grad, pair_w1, contract_cols, preferred_element_type=jnp.float32
    )
    victim_grad = pair_grad[:, :feat_width]
    partner_grad = (
        pair_grad[:, feat_width:].astype(jnp.bfloat16).reshape(regions, slot_cap, feat_width)
    )
    nets_grad = (
        jnp.zeros((net_rows, feat_width), jnp.float32).at[pair_local.reshape(-1)].add(victim_grad)
    )
    returned_pairs = lax.all_to_all(partner_grad, "region", split_axis=0, concat_axis=0, tiled=True)
    nets_grad = nets_grad.at[asked.reshape(-1)].add(
        returned_pairs.reshape(-1, feat_width).astype(jnp.float32)
    )
    pre_grad = (nets_grad * gelu_slope(pre)).astype(jnp.bfloat16)
    grad_gnn = lax.dot_general(joined, pre_grad, contract_rows, preferred_element_type=jnp.float32)
    cat_grad = lax.dot_general(
        pre_grad, gnn_weight, contract_cols, preferred_element_type=jnp.float32
    )
    agg_grad = (cat_grad[:, feat_width:] / degree).astype(jnp.bfloat16)
    table_grad = lax.dot_general(
        adjacency, agg_grad, contract_rows, preferred_element_type=jnp.float32
    )
    halo_back = table_grad[net_rows:].astype(jnp.bfloat16).reshape(peers, halo_rows, feat_width)
    returned_halo = lax.all_to_all(halo_back, "dom", split_axis=0, concat_axis=0, tiled=True)
    embeds_sum = nets_grad + cat_grad[:, :feat_width] + table_grad[:net_rows]
    embeds_sum = embeds_sum + lax.dot_general(
        selector,
        returned_halo.reshape(-1, feat_width),
        contract_rows,
        preferred_element_type=jnp.float32,
    )
    gnn_sum, w1_sum, w2_sum, sq_sum = lax.psum(
        (grad_gnn, grad_w1, grad_w2, sq_local), ("region", "dom")
    )
    root_count = jnp.sqrt(total_count)
    embeds_grad = (embeds_sum * (8.0 * nets_total / total_count)).astype(jnp.bfloat16)
    return (
        embeds_grad,
        8.0 * gnn_sum / root_count,
        8.0 * w1_sum / root_count,
        8.0 * w2_sum / root_count,
        sq_sum / total_count,
    )


def solution(mesh):
    in_specs = (
        P(("region", "dom"), None),
        P(("region", "dom"), None),
        P(("region", "dom"), None),
        P(),
        P(("region", "dom"), None),
        P(("region", "dom"), None),
        P(("region", "dom"), None),
        P(("region", "dom"), None),
        P(),
        P(),
    )
    out_specs = (P(("region", "dom"), None), P(), P(), P(), P())
    return jax.shard_map(local, mesh=mesh, in_specs=in_specs, out_specs=out_specs, check_vma=False)
```

profile of v0, /device:TPU:0, one launch (start us, length us, event | category | flops | bytes accessed | tf_op | source)
XLA Modules:
  0.0 338.2 jit_solution(2831680173835258016)
XLA Ops:
  7.2 0.0 copy-start
  7.2 1.3 all_to_all.21
  8.5 4.2 %all-to-all-start.1 = ((s32[4,1,512]{2,1,0:T(1,128)}), s32[4,1,512]{2,1,0:T(1,128)S(1)}, u32[]{:S(2)}, u32[]{:S(2)}) async-start(s32[4,1,512]{2,1,0:T(1,128)} %all_to_all.21), calls=%async_computation.1 | async-start | bytes 16384 | tf_op jit(solution)/shard_map/all_to_all | solution.py:66
  12.7 3.6 %fusion.55 = bf16[1024,256]{1,0:T(8,128)(2,1)} fusion(bf16[2048,256]{1,0:T(8,128)(2,1)} %param.10, s32[1024]{0:T(1024)} %bitcast.87), kind=kOutput, calls=%fused_computation.75 | convolution fusion | flops 1076101120 | bytes 1576960 | tf_op jit(solution)/shard_map/dot_general | solution.py:47
  16.3 0.2 all-to-all-done.1
  16.5 6.3 %all-to-all-start = ((bf16[8,128,256]{2,1,0:T(8,128)(2,1)}), bf16[8,128,256]{2,1,0:T(8,128)(2,1)S(1)}, u32[]{:S(2)}, u32[]{:S(2)}) async-start(bf16[8,128,256]{2,1,0:T(8,128)(2,1)} %bitcast.11), calls=%async_computation | async-start | bytes 1048576 | tf_op jit(solution)/shard_map/all_to_all | solution.py:51
  22.8 0.6 copy.17
  23.6 14.3 %all-to-all-done = bf16[8,128,256]{2,1,0:T(8,128)(2,1)S(1)} async-done(((bf16[8,128,256]{2,1,0:T(8,128)(2,1)}), bf16[8,128,256]{2,1,0:T(8,128)(2,1)S(1)}, u32[]{:S(2)}, u32[]{:S(2)}) %all-to-all-start) | async-done | bytes 524320 | tf_op jit(solution)/shard_map/all_to_all | solution.py:51
  37.9 27.2 %fusion.29 = bf16[2048,256]{0,1:T(8,128)(2,1)S(1)} fusion(s32[2048]{0:T(1024)S(1)} %bitcast.78, s32[2048]{0:T(1024)S(1)} %bitcast.80, s32[2048]{0:T(1024)S(1)} %bitcast.68, s32[2048]{0:T(1024)S(1)} %bitcast.70, s32[2048]{0:T(1024)S(1)} %bitcast.72, s32[2048]{0:T(1024)S(1)} %bitcast.74, s32[2048]{0:T(1024)S(1)} %bitcast.76, s32[2048]{0:T(1024)S(1)} %bitcast.66, ...), kind=kOutput, calls=%fused_computation.42 | convolution fusion | flops 3426746368 | bytes 2686976 | tf_op jit(solution)/shard_map/dot_general | solution.py:59
  65.2 2.5 add_convert_fusion
  67.7 9.0 %gather_fusion.1 = bf16[2048,256]{1,0:T(8,128)(2,1)} fusion(bf16[2048,256]{1,0:T(8,128)(2,1)S(1)} %get-tuple-element.22, s32[2048]{0:T(1024)S(1)} %broadcast_clamp_fusion), kind=kCustom, calls=%fused_computation.1 | custom fusion | bytes 2105344 | tf_op jit(solution)/shard_map/gather | solution.py:67
  76.7 3.7 %all-to-all-start.2 = ((bf16[4,512,256]{2,1,0:T(8,128)(2,1)}), bf16[4,512,256]{2,1,0:T(8,128)(2,1)S(1)}, u32[]{:S(2)}, u32[]{:S(2)}) async-start(bf16[4,512,256]{2,1,0:T(8,128)(2,1)} %bitcast.16), calls=%async_computation.2 | async-start | bytes 2097152 | tf_op jit(solution)/shard_map/all_to_all | solution.py:67
  80.5 0.1 fusion.59
  80.6 9.0 %gather_fusion = bf16[2048,256]{1,0:T(8,128)(2,1)} fusion(bf16[2048,256]{1,0:T(8,128)(2,1)S(1)} %get-tuple-element.22, s32[2048]{0:T(1024)S(1)} %broadcast_clamp_fusion.1), kind=kCustom, calls=%fused_computation | custom fusion | bytes 2105344 | tf_op jit(solution)/shard_map/gather | solution.py:68
  89.6 5.2 %all-to-all-done.2 = bf16[4,512,256]{2,1,0:T(8,128)(2,1)S(1)} async-done(((bf16[4,512,256]{2,1,0:T(8,128)(2,1)}), bf16[4,512,256]{2,1,0:T(8,128)(2,1)S(1)}, u32[]{:S(2)}, u32[]{:S(2)}) %all-to-all-start.2) | async-done | bytes 1048608 | tf_op jit(solution)/shard_map/all_to_all | solution.py:67
  94.8 1.4 pad_maximum_fusion.1
  96.2 0.9 multiply_convert_fusion.1
  97.2 0.4 fusion.65
  97.5 0.6 multiply_reduce_fusion.1
  98.2 1.6 multiply_reduce_fusion
  99.8 0.7 fusion.66
  100.5 1.9 copy-done.1
  102.5 1.1 slice.78
  103.6 4.3 %all-to-all-start.3 = ((bf16[4,512,256]{2,1,0:T(8,128)(2,1)}), bf16[4,512,256]{2,1,0:T(8,128)(2,1)}, u32[]{:S(2)}, u32[]{:S(2)}) async-start(bf16[4,512,256]{2,1,0:T(8,128)(2,1)} %bitcast.55), calls=%async_computation.3 | async-start | bytes 2097152 | tf_op jit(solution)/shard_map/all_to_all | solution.py:95
  107.9 13.6 %scatter_custom_fusion = f32[2048,256]{1,0:T(8,128)} fusion(s32[2048]{0:T(1024)S(1)} %bitcast.84, f32[2048,512]{1,0:T(8,128)} %copy-done.1, f32[]{:T(128)} %constant.12.clone.1), kind=kCustom, calls=%fused_computation.60 | custom fusion | flops 524288 | bytes 4194816 | tf_op jit(solution)/shard_map/scatter-add | solution.py:93
  121.5 1.5 fusion.68
  123.0 0.0 all-to-all-done.3
  123.0 15.3 %scatter_custom_fusion.1 = f32[2048,256]{1,0:T(8,128)} fusion(f32[2048,256]{1,0:T(8,128)} %scatter_custom_fusion, s32[2048]{0:T(1024)S(1)} %bitcast.83, bf16[2048,256]{1,0:T(8,128)(2,1)} %bitcast.25), kind=kCustom, calls=%fused_computation.64 | custom fusion | flops 1048576 | bytes 3145728 | tf_op jit(solution)/shard_map/scatter-add | solution.py:96
  138.4 0.0 copy-start.9
  138.4 3.0 fusion.45
  141.4 0.7 fusion.67
  142.1 1.9 copy-done.2
  144.1 0.2 slice.65
  144.3 1.9 copy.19
  146.2 30.3 %fusion.17 = f32[3072,256]{1,0:T(8,128)S(1)} fusion(s32[2048]{0:T(1024)S(1)} %bitcast.79, s32[2048]{0:T(1024)S(1)} %bitcast.81, s32[2048]{0:T(1024)S(1)} %bitcast.69, s32[2048]{0:T(1024)S(1)} %bitcast.71, s32[2048]{0:T(1024)S(1)} %bitcast.73, s32[2048]{0:T(1024)S(1)} %bitcast.75, s32[2048]{0:T(1024)S(1)} %bitcast.77, s32[2048]{0:T(1024)S(1)} %bitcast.67, ...), kind=kOutput, calls=%fused_computation.30 | convolution fusion | flops 3423600640 | bytes 5308416 | tf_op jit(solution)/shard_map/dot_general | solution.py:105
  176.5 1.7 copy-done.10
  178.2 0.8 slice.79
  179.0 3.6 %all-to-all-start.4 = ((bf16[8,128,256]{2,1,0:T(8,128)(2,1)}), bf16[8,128,256]{2,1,0:T(8,128)(2,1)S(1)}, u32[]{:S(2)}, u32[]{:S(2)}) async-start(bf16[8,128,256]{2,1,0:T(8,128)(2,1)} %bitcast.23), calls=%async_computation.4 | async-start | bytes 1048576 | tf_op jit(solution)/shard_map/all_to_all | solution.py:109
  182.7 0.0 all-reduce.4.cloned.1.call-start
  182.7 2.7 fusion.53
  185.5 0.0 all-reduce.4.cloned.1.call-update
  185.5 0.6 reduce_sum.27
  186.8 41.8 %all-reduce = (f32[]{:T(128)}, f32[256]{0:T(256)S(1)}, f32[]{:T(128)}) all-reduce(f32[]{:T(128)S(6)} %convert_element_type.90, f32[256]{0:T(256)S(1)} %get-tuple-element.20, f32[]{:T(128)} %get-tuple-element.18), channel_id=1, replica_groups=mesh['region'=4,'dom'=8] {'region','dom'}, use_global_device_ids=true, to_apply=%region_3.0 | all-reduce | flops 258 | bytes 2064 | tf_op jit(solution)/shard_map/psum | solution.py:65
  231.2 0.6 multiply_divide_fusion.2
  231.8 89.9 %all-reduce.4.cloned.1.call-done = (f32[512,256]{1,0:T(8,128)}, f32[512,256]{1,0:T(8,128)}) async-done(((f32[512,256]{1,0:T(8,128)}, f32[512,256]{1,0:T(8,128)}), (f32[512,256]{1,0:T(8,128)}, f32[512,256]{1,0:T(8,128)})) %all-reduce.4.cloned.1.call-update) | async-done | bytes 1048592 | tf_op jit(solution)/shard_map/psum | solution.py:117
  321.7 2.3 multiply_divide_fusion
  324.0 0.0 all-to-all-done.4
  324.0 5.8 %fusion.28 = bf16[2048,256]{1,0:T(8,128)(2,1)} fusion(bf16[1024,256]{1,0:T(8,128)(2,1)S(1)} %bitcast.57, s32[1024]{0:T(1024)S(1)} %bitcast.88, f32[3072,256]{1,0:T(8,128)} %copy-done.10, f32[2048,256]{1,0:T(8,128)S(1)} %copy-done.3, f32[2048,512]{1,0:T(8,128)} %copy-done.2, f32[]{:T(128)S(6)} %div.30), kind=kOutput, calls=%fused_computation.41 | convolution fusion | flops 1078460416 | bytes 7868420 | tf_op jit(solution)/shard_map/dot_general | solution.py:111
  (44 shorter events, 0.2 us)
Async XLA Ops:
  7.2 89.1 %copy-start = (bf16[512,256]{1,0:T(8,128)(2,1)S(1)}, bf16[512,256]{1,0:T(8,128)(2,1)}, u32[]{:S(2)}) copy-start(bf16[512,256]{1,0:T(8,128)(2,1)} %param.18) | copy-start | bytes 786436
  8.5 8.0 %all-to-all-start.1 = ((s32[4,1,512]{2,1,0:T(1,128)}), s32[4,1,512]{2,1,0:T(1,128)S(1)}, u32[]{:S(2)}, u32[]{:S(2)}) async-start(s32[4,1,512]{2,1,0:T(1,128)} %all_to_all.21), calls=%async_computation.1 | async-start | bytes 16384 | tf_op jit(solution)/shard_map/all_to_all | solution.py:66
  12.7 10.1 %copy-start.5 = (bf16[2048,256]{1,0:T(8,128)(2,1)S(1)}, bf16[2048,256]{1,0:T(8,128)(2,1)}, u32[]{:S(2)}) copy-start(bf16[2048,256]{1,0:T(8,128)(2,1)} %param.10) | copy-start | bytes 3145732
  16.3 7.2 %copy-start.11 = (s32[2048,8]{0,1:T(8,128)S(1)}, s32[2048,8]{0,1:T(8,128)}, u32[]{:S(2)}) copy-start(s32[2048,8]{0,1:T(8,128)} %param.11) | copy-start | bytes 196612
  16.5 21.4 %all-to-all-start = ((bf16[8,128,256]{2,1,0:T(8,128)(2,1)}), bf16[8,128,256]{2,1,0:T(8,128)(2,1)S(1)}, u32[]{:S(2)}, u32[]{:S(2)}) async-start(bf16[8,128,256]{2,1,0:T(8,128)(2,1)} %bitcast.11), calls=%async_computation | async-start | bytes 1048576 | tf_op jit(solution)/shard_map/all_to_all | solution.py:51
  23.5 41.7 %copy-start.6 = (bf16[2048,256]{0,1:T(8,128)(2,1)}, bf16[2048,256]{0,1:T(8,128)(2,1)S(1)}, u32[]{:S(2)}) copy-start(bf16[2048,256]{0,1:T(8,128)(2,1)S(1)} %copy.17) | copy-start | bytes 3145732
  37.9 27.3 %copy-start.8 = (bf16[512,256]{1,0:T(8,128)(2,1)S(1)}, bf16[512,256]{1,0:T(8,128)(2,1)}, u32[]{:S(2)}) copy-start(bf16[512,256]{1,0:T(8,128)(2,1)} %param.13) | copy-start | bytes 786436
  65.2 2.5 copy-start.17
  76.7 3.7 %copy-start.16 = (bf16[256]{0:T(256)(128)(2,1)S(1)}, bf16[256]{0:T(256)(128)(2,1)}, u32[]{:S(2)}) copy-start(bf16[256]{0:T(256)(128)(2,1)} %param.19) | copy-start | bytes 1540
  76.7 3.7 %copy-start.14 = (s32[1,4]{1,0:T(1,128)S(1)}, s32[1,4]{1,0:T(1,128)}, u32[]{:S(2)}) copy-start(s32[1,4]{1,0:T(1,128)} %param.16) | copy-start | bytes 52
  76.7 3.8 %copy-start.13 = (f32[4,512]{1,0:T(4,128)S(1)}, f32[4,512]{1,0:T(4,128)}, u32[]{:S(2)}) copy-start(f32[4,512]{1,0:T(4,128)} %param.17) | copy-start | bytes 24580
  76.7 3.8 %copy-start.12 = (s32[4,512]{1,0:T(4,128)S(1)}, s32[4,512]{1,0:T(4,128)}, u32[]{:S(2)}) copy-start(s32[4,512]{1,0:T(4,128)} %param.14) | copy-start | bytes 24580
  76.7 18.1 %all-to-all-start.2 = ((bf16[4,512,256]{2,1,0:T(8,128)(2,1)}), bf16[4,512,256]{2,1,0:T(8,128)(2,1)S(1)}, u32[]{:S(2)}, u32[]{:S(2)}) async-start(bf16[4,512,256]{2,1,0:T(8,128)(2,1)} %bitcast.16), calls=%async_computation.2 | async-start | bytes 2097152 | tf_op jit(solution)/shard_map/all_to_all | solution.py:67
  100.5 2.0 copy-start.1
  103.6 19.4 %all-to-all-start.3 = ((bf16[4,512,256]{2,1,0:T(8,128)(2,1)}), bf16[4,512,256]{2,1,0:T(8,128)(2,1)}, u32[]{:S(2)}, u32[]{:S(2)}) async-start(bf16[4,512,256]{2,1,0:T(8,128)(2,1)} %bitcast.55), calls=%async_computation.3 | async-start | bytes 2097152 | tf_op jit(solution)/shard_map/all_to_all | solution.py:95
  123.0 15.3 %copy-start.4 = (f32[2048,256]{1,0:T(8,128)S(1)}, f32[2048,256]{1,0:T(8,128)}, u32[]{:S(2)}) copy-start(f32[2048,256]{1,0:T(8,128)} %get-tuple-element.23) | copy-start | bytes 6291460
  138.4 3.0 copy-start.9
  142.1 2.0 copy-start.2
  176.5 1.7 copy-start.10
  178.2 4.5 %copy-start.7 = (bf16[2048,256]{0,1:T(8,128)(2,1)S(1)}, bf16[2048,256]{0,1:T(8,128)(2,1)}, u32[]{:S(2)}) copy-start(bf16[2048,256]{0,1:T(8,128)(2,1)} %copy-done.6) | copy-start | bytes 3145732
  179.0 144.9 %all-to-all-start.4 = ((bf16[8,128,256]{2,1,0:T(8,128)(2,1)}), bf16[8,128,256]{2,1,0:T(8,128)(2,1)S(1)}, u32[]{:S(2)}, u32[]{:S(2)}) async-start(bf16[8,128,256]{2,1,0:T(8,128)(2,1)} %bitcast.23), calls=%async_computation.4 | async-start | bytes 1048576 | tf_op jit(solution)/shard_map/all_to_all | solution.py:109
  182.7 139.1 %all-reduce.4.cloned.1.call-start = ((), (), s32[]{:S(2)}) async-start(), calls=%async_computation.5 | async-start | bytes 2097152 | tf_op jit(solution)/shard_map/psum | solution.py:117
  185.5 138.5 %copy-start.3 = (f32[2048,256]{1,0:T(8,128)S(1)}, f32[2048,256]{1,0:T(8,128)}, u32[]{:S(2)}) copy-start(f32[2048,256]{1,0:T(8,128)} %scatter_custom_fusion.1) | copy-start | bytes 6291460
  185.5 138.5 %copy-start.15 = (s32[8,128]{1,0:T(8,128)S(1)}, s32[8,128]{1,0:T(8,128)}, u32[]{:S(2)}) copy-start(s32[8,128]{1,0:T(8,128)} %param.12) | copy-start | bytes 12292
Sparse Core Ops, SparseCore 0:
  189.5 132.2 all-reduce.3
where the time goes:
time: 341 us; the launch traced here: 338 us
  waiting for transfers between devices  110 us (32%)
  matrix products  76.5 us (22%)
  blocking collectives  41.8 us (12%)
  other arithmetic  39.1 us (11%)
  local copies, waits for them, and re-layouts  29.8 us (9%)
  starting transfers between devices  22.1 us (6%)
  between operations  19.3 us (6%)
    psum x1, waiting for transfers between devices, local(): lax.psum((grad_gnn, grad_w1, grad_w2, sq_local), ('region', 'dom'))  89.9 us
    psum x1, blocking collectives, local(): total_count = lax.psum(local_count, ('region', 'dom'))  41.8 us
    dot_general x1, matrix products, local(): lax.dot_general(adjacency, agg_grad, contract_rows, preferred_element_typ...  30.3 us
    dot_general x1, matrix products, local(): agg_sum = jnp.dot(adjacency, table, preferred_element_type=jnp.float32)  27.2 us
    scatter-add x1, other arithmetic, local(): nets_grad.at[asked.reshape(-1)]  15.3 us
    all_to_all x1, waiting for transfers between devices, local(): lax.all_to_all(outgoing, 'dom', split_axis=0, concat_axis=0, tiled=True)  14.3 us
    scatter-add x1, other arithmetic, local(): jnp.zeros((net_rows, feat_width), jnp.float32).at[pair_local.reshape(-1)]  13.6 us
    gather x1, local copies, waits for them, and re-layouts, local(): nets[asked]  9.05 us
  transfers between devices with their start and end apart: 6, of which 4 were waited for; matrix products, arithmetic and copies ran while one was open for 10% of the time, Pallas kernels for 0%

commit v1 on v0

v1 whole, which is shorter than its diff:
```python
import functools

import jax
import jax.numpy as jnp
from jax import lax
from jax.experimental import pallas as pl
from jax.experimental.pallas import tpu as pltpu
from jax.sharding import PartitionSpec as P

bf16 = jnp.bfloat16
f32 = jnp.float32
i32 = jnp.int32
i16 = jnp.int16
gelu_coef = 0.7978845608
BOTH = ("region", "dom")
BLOCK = 256
TT = (((0,), (0,)), ((), ()))
NT = (((1,), (1,)), ((), ()))


def mm(a, b):
    return jnp.dot(a, b, preferred_element_type=f32)


def mm_dims(a, b, dims):
    return lax.dot_general(a, b, dims, preferred_element_type=f32)


def gelu_inner(value):
    return jnp.tanh(gelu_coef * (value + 0.044715 * value * value * value))


def slope_of(value, inner):
    return 0.5 * (1.0 + inner) + 0.5 * value * (1.0 - inner * inner) * gelu_coef * (
        1.0 + 3.0 * 0.044715 * value * value
    )


def column_of(row):
    return jnp.broadcast_to(row, (128, row.shape[1])).T


def onehot_rows(row, width):
    column = column_of(row).astype(i16)
    lane = lax.broadcasted_iota(i32, column.shape, 1).astype(i16)
    one = jnp.ones(column.shape, bf16)
    zero = jnp.zeros(column.shape, bf16)
    return jnp.concatenate(
        [jnp.where(column == lane + jnp.int16(128 * j), one, zero) for j in range(width // 128)], 1
    )


def onehot_cols(row, first, height):
    shape = (height, row.shape[1])
    wide = jnp.broadcast_to(row - first, shape).astype(i16)
    sub = lax.broadcasted_iota(i32, shape, 0).astype(i16)
    return jnp.where(wide == sub, jnp.ones(shape, bf16), jnp.zeros(shape, bf16))


def halo_gather_kernel(send_ref, embeds_ref, out_ref):
    peers, halo = send_ref.shape
    nets = embeds_ref.shape[0]
    for p in range(peers):
        hot = onehot_rows(send_ref[p : p + 1, :], nets)
        out_ref[p * halo : (p + 1) * halo, :] = mm(hot, embeds_ref[...]).astype(bf16)


def adjacency_kernel(
    neigh_ref, embeds_ref, block_ref, gnn_ref, own_ref, halo_ref, sum_ref, pre_ref
):
    degree = neigh_ref.shape[0]
    rows, nets = own_ref.shape
    feat = embeds_ref.shape[1]
    listed = [neigh_ref[c : c + 1, :] for c in range(degree)]
    columns, counts = [], []
    for c in range(degree):
        count = jnp.ones_like(listed[c])
        seen = None
        for e in range(degree):
            if e != c:
                same = listed[e] == listed[c]
                if e > c:
                    count = count + same.astype(i32)
                else:
                    seen = same if seen is None else (seen | same)
        index = listed[c] if seen is None else jnp.where(seen, -1, listed[c])
        columns.append(column_of(index).astype(i16))
        counts.append(column_of(count).astype(f32).astype(bf16))
    lane = lax.broadcasted_iota(i32, (rows, 128), 1).astype(i16)
    zero = jnp.zeros((rows, 128), bf16)

    def tile(at):
        acc = zero
        here = lane + jnp.int16(at)
        for c in range(degree):
            acc = jnp.where(columns[c] == here, counts[c], acc)
        return acc

    for at in range(0, nets, 128):
        own_ref[:, at : at + 128] = tile(at)
    for at in range(0, halo_ref.shape[1], 128):
        halo_ref[:, at : at + 128] = tile(nets + at)
    sum_ref[...] = mm(own_ref[...], embeds_ref[...])
    pre_ref[...] = mm(block_ref[...], gnn_ref[:feat, :])


def asked_kernel(asked_ref, hot_ref):
    regions, slots = asked_ref.shape
    for q in range(regions):
        hot_ref[q] = onehot_rows(asked_ref[q : q + 1, :], hot_ref.shape[2])


def layer_kernel(
    rid_ref,
    halo_ref,
    received_ref,
    sum_ref,
    pre_own_ref,
    embeds_ref,
    gnn_ref,
    hot_ref,
    pre_ref,
    agg_ref,
    nets_ref,
    *send_refs,
    degree,
):
    nets, feat = embeds_ref.shape
    regions = hot_ref.shape[0]
    for at in range(0, nets, BLOCK):
        rows = slice(at, at + BLOCK)
        total = sum_ref[rows, :] + mm(halo_ref[rows, :], received_ref[...])
        agg = (total / degree).astype(bf16)
        agg_ref[rows, :] = agg
        pre = pre_own_ref[rows, :] + mm(agg, gnn_ref[feat:, :])
        pre_ref[rows, :] = pre
        gelu = 0.5 * pre * (1.0 + gelu_inner(pre))
        nets_ref[rows, :] = (embeds_ref[rows, :].astype(f32) + gelu).astype(bf16)
    me = rid_ref[0]
    for k in [*range(1, regions), 0]:
        send_refs[k][...] = mm(hot_ref[me ^ k], nets_ref[...]).astype(bf16)


def victim_kernel(rid_ref, local_ref, nets_ref, w1_ref, pre_ref, victim_ref, linear_ref, slope_ref):
    regions, slots = local_ref.shape
    nets, feat = nets_ref.shape
    me = rid_ref[0]
    for k in range(regions):
        hot = onehot_rows(local_ref[pl.ds(me ^ k, 1), :], nets)
        victim = mm(hot, nets_ref[...]).astype(bf16)
        victim_ref[k] = victim
        linear_ref[k] = mm(victim, w1_ref[:feat, :])
    for at in range(0, nets, BLOCK):
        pre = pre_ref[at : at + BLOCK, :]
        slope_ref[at : at + BLOCK, :] = slope_of(pre, gelu_inner(pre))


def pair_kernel(rid_ref, count_ref, target_ref, linear_ref, w1_ref, w2_ref, *refs, ks):
    some = len(ks)
    partner_refs, (lin_grad_ref, w2_sum_ref, sq_ref), back_refs = (
        refs[:some],
        refs[some : some + 3],
        refs[some + 3 :],
    )
    me = rid_ref[0]
    slots, hid = linear_ref.shape[1:]
    feat = partner_refs[0].shape[1]
    w2_row = w2_ref[...].astype(f32)
    w2_column = column_of(w2_row).astype(bf16)
    w2_sum = jnp.zeros((1, hid), f32)
    sq_sum = jnp.zeros((1, 128), f32)
    slot = lax.broadcasted_iota(i32, (slots, 128), 0)
    for at, k in enumerate(ks):
        linear = linear_ref[k] + mm(partner_refs[at][...], w1_ref[feat:, :])
        inner = gelu_inner(linear)
        activated = (0.5 * linear * (1.0 + inner)).astype(bf16)
        scores = mm(activated, w2_column)
        live = slot < count_ref[0, me ^ k]
        errors = jnp.where(live, scores - column_of(target_ref[pl.ds(me ^ k, 1), :]), 0.0)
        sq_sum = sq_sum + jnp.sum(errors * errors, 0, keepdims=True)
        residual = 2.0 * errors
        residual = jnp.concatenate([residual] * (hid // 128), 1)
        w2_sum = w2_sum + jnp.sum(residual * activated.astype(f32), 0, keepdims=True)
        lin_grad = (residual * w2_row * slope_of(linear, inner)).astype(bf16)
        lin_grad_ref[at] = lin_grad
        back_refs[at][...] = mm_dims(lin_grad, w1_ref[feat:, :], NT).astype(bf16)
    w2_sum_ref[...] = jnp.broadcast_to(w2_sum, w2_sum_ref.shape)
    sq_ref[...] = jnp.broadcast_to(sq_sum, sq_ref.shape)


def local_grad_kernel(
    rid_ref, local_ref, asked_ref, w1_ref, victim_ref, *refs, regions, groups, near
):
    partner_refs, refs = refs[:regions], refs[regions:]
    lin_refs, refs = refs[: len(groups)], refs[len(groups) :]
    near_refs, refs = refs[:near], refs[near:]
    grad_ref, hot_ref, w1_grad_ref, vg_ref = refs
    me = rid_ref[0]
    slots, feat = victim_ref.shape[1:]
    nets = grad_ref.shape[0]
    top = jnp.zeros((feat, w1_ref.shape[1]), f32)
    low = jnp.zeros((feat, w1_ref.shape[1]), f32)
    for ref, ks in zip(lin_refs, groups, strict=True):
        for at, k in enumerate(ks):
            lin_grad = ref[at]
            vg_ref[k * slots : (k + 1) * slots, :] = mm_dims(lin_grad, w1_ref[:feat, :], NT).astype(
                bf16
            )
            top = top + mm_dims(victim_ref[k], lin_grad, TT)
            low = low + mm_dims(partner_refs[k][...], lin_grad, TT)
    w1_grad_ref[:feat, :] = top.astype(bf16)
    w1_grad_ref[feat:, :] = low.astype(bf16)
    local = [local_ref[pl.ds(me ^ k, 1), :] for k in range(regions)]
    asked = [asked_ref[pl.ds(me ^ k, 1), :] for k in range(regions)]
    for at in range(0, nets, BLOCK):
        hot = jnp.concatenate([onehot_cols(row, at, BLOCK) for row in local], 1)
        total = mm(hot, vg_ref[...])
        for k in range(near):
            total = total + mm(onehot_cols(asked[k], at, BLOCK), near_refs[k][...])
        grad_ref[at : at + BLOCK, :] = total
        for k in range(near, regions):
            hot_ref[at : at + BLOCK, (k - near) * slots : (k - near + 1) * slots] = onehot_cols(
                asked[k], at, BLOCK
            )


def layer_grad_kernel(
    grad_ref, hot_ref, slope_ref, gnn_ref, halo_ref, *refs, far, degree
):
    far_refs, (total_ref, pre_grad_ref, agg_grad_ref, back_ref) = refs[:far], refs[far:]
    nets, feat = grad_ref.shape
    slots = far_refs[0].shape[0]
    for at in range(0, nets, BLOCK):
        rows = slice(at, at + BLOCK)
        total = grad_ref[rows, :]
        for k in range(far):
            total = total + mm(hot_ref[rows, k * slots : (k + 1) * slots], far_refs[k][...])
        total_ref[rows, :] = total
        pre_grad = (total * slope_ref[rows, :]).astype(bf16)
        pre_grad_ref[rows, :] = pre_grad
        agg_grad_ref[:, rows] = (mm_dims(gnn_ref[feat:, :], pre_grad, NT) / degree).astype(bf16)
    for at in range(0, halo_ref.shape[1], BLOCK):
        back = mm(agg_grad_ref[...], halo_ref[:, at : at + BLOCK])
        back_ref[at : at + BLOCK, :] = back.T.astype(bf16)


def gnn_grad_kernel(embeds_ref, agg_ref, pre_grad_ref, out_ref):
    feat = embeds_ref.shape[1]
    out_ref[:feat, :] = mm_dims(embeds_ref[...], pre_grad_ref[...], TT).astype(bf16)
    out_ref[feat:, :] = mm_dims(agg_ref[...], pre_grad_ref[...], TT).astype(bf16)


def own_grad_kernel(total_ref, pre_grad_ref, gnn_ref, agg_grad_ref, own_ref, out_ref):
    feat = agg_grad_ref.shape[0]
    out_ref[...] = (
        total_ref[...]
        + mm_dims(pre_grad_ref[...], gnn_ref[:feat, :], NT)
        + mm(agg_grad_ref[...], own_ref[...]).T
    )


def final_kernel(scale_ref, send_ref, own_ref, returned_ref, out_ref):
    nets = out_ref.shape[0]
    peers = send_ref.shape[0]
    scale = scale_ref[0]
    for at in range(0, nets, BLOCK):
        hot = jnp.concatenate(
            [onehot_cols(send_ref[p : p + 1, :], at, BLOCK) for p in range(peers)], 1
        )
        total = own_ref[at : at + BLOCK, :] + mm(hot, returned_ref[...])
        out_ref[at : at + BLOCK, :] = (total * scale).astype(bf16)


VM = pl.BlockSpec(memory_space=pltpu.VMEM)
SM = pl.BlockSpec(memory_space=pltpu.SMEM)


def params(mib):
    return pltpu.CompilerParams(vmem_limit_bytes=mib << 20)


def cost(flops, moved):
    return pl.CostEstimate(flops=flops, bytes_accessed=moved, transcendentals=0)


def shape(dims, dtype):
    return jax.ShapeDtypeStruct(dims, dtype)


def exchange(value, axis):
    return lax.all_to_all(value, axis, split_axis=0, concat_axis=0, tiled=True)


def two_parts(value):
    high = value.astype(bf16)
    return high, (value - high.astype(f32)).astype(bf16)


def local(
    embeds,
    neighbours,
    halo_send,
    gnn_weight,
    pair_local,
    pair_remote,
    pair_count,
    targets,
    pair_w1,
    pair_w2,
):
    nets, feat = embeds.shape
    hid = pair_w1.shape[1]
    degree = neighbours.shape[1]
    regions, slots = pair_local.shape
    peers, halo = halo_send.shape
    halo_rows = peers * halo
    devices = lax.axis_size("region") * lax.axis_size("dom")
    rid = lax.axis_index("region").astype(i32).reshape(1)
    near = 2

    def permute(value, k):
        return lax.ppermute(value, "region", [(i, i ^ k) for i in range(regions)])

    outgoing = pl.pallas_call(
        halo_gather_kernel,
        out_shape=shape((halo_rows, feat), bf16),
        in_specs=[VM, VM],
        out_specs=VM,
        compiler_params=params(24),
        cost_estimate=cost(2 * halo_rows * nets * feat, 2 << 20),
        name="halo_gather",
    )(halo_send, embeds)
    received = exchange(outgoing.reshape(peers, halo, feat), "dom").reshape(halo_rows, feat)
    asked = exchange(pair_remote.reshape(regions, 1, slots), "region").reshape(regions, slots)

    own, from_halo, agg_sum, pre_own = pl.pallas_call(
        adjacency_kernel,
        grid=(nets // BLOCK,),
        in_specs=[
            pl.BlockSpec((degree, BLOCK), lambda i: (0, i)),
            pl.BlockSpec((nets, feat), lambda i: (0, 0)),
            pl.BlockSpec((BLOCK, feat), lambda i: (i, 0)),
            pl.BlockSpec((2 * feat, feat), lambda i: (0, 0)),
        ],
        out_specs=[
            pl.BlockSpec((BLOCK, nets), lambda i: (i, 0)),
            pl.BlockSpec((BLOCK, halo_rows), lambda i: (i, 0)),
            pl.BlockSpec((BLOCK, feat), lambda i: (i, 0)),
            pl.BlockSpec((BLOCK, feat), lambda i: (i, 0)),
        ],
        out_shape=[
            shape((nets, nets), bf16),
            shape((nets, halo_rows), bf16),
            shape((nets, feat), f32),
            shape((nets, feat), f32),
        ],
        compiler_params=params(24),
        cost_estimate=cost(20 * nets * (nets + halo_rows) * feat // 2, 20 << 20),
        name="adjacency",
    )(neighbours.T, embeds, embeds, gnn_weight)

    asked_hot = pl.pallas_call(
        asked_kernel,
        out_shape=shape((regions, slots, nets), bf16),
        in_specs=[VM],
        out_specs=VM,
        compiler_params=params(40),
        cost_estimate=cost(2 * nets * nets * feat, 8 << 20),
        name="asked_onehot",
    )(asked)

    pre, aggregate, net_values, *sends = pl.pallas_call(
        functools.partial(layer_kernel, degree=degree),
        out_shape=[
            shape((nets, feat), f32),
            shape((nets, feat), bf16),
            shape((nets, feat), bf16),
        ]
        + [shape((slots, feat), bf16)] * regions,
        in_specs=[SM] + [VM] * 7,
        out_specs=[VM] * (3 + regions),
        compiler_params=params(40),
        cost_estimate=cost(2 * nets * nets * feat * 2, 20 << 20),
        name="layer",
    )(rid, from_halo, received, agg_sum, pre_own, embeds, gnn_weight, asked_hot)

    partners = [sends[0]] + [permute(sends[k], k) for k in range(1, regions)]

    victim, linear_own, slope = pl.pallas_call(
        victim_kernel,
        out_shape=[
            shape((regions, slots, feat), bf16),
            shape((regions, slots, hid), f32),
            shape((nets, feat), f32),
        ],
        in_specs=[SM] + [VM] * 4,
        out_specs=[VM] * 3,
        compiler_params=params(40),
        cost_estimate=cost(2 * nets * nets * feat * 2, 8 << 20),
        name="victims",
    )(rid, pair_local, net_values, pair_w1, pre)

    groups = [tuple(range(near))] + [(k,) for k in range(near, regions)]
    w2_row = pair_w2.reshape(1, hid)
    lin_grads, backs, w2_sums, sq_sums = [], [], [], []
    for ks in groups:
        lin_grad, w2_sum, sq_sum, *back = pl.pallas_call(
            functools.partial(pair_kernel, ks=ks),
            out_shape=[
                shape((len(ks), slots, hid), bf16),
                shape((8, hid), f32),
                shape((8, 128), f32),
            ]
            + [shape((slots, feat), bf16)] * len(ks),
            in_specs=[SM, SM] + [VM] * (4 + len(ks)),
            out_specs=[VM] * (3 + len(ks)),
            compiler_params=params(24),
            cost_estimate=cost(len(ks) * 2 * slots * hid * feat * 16, 2 << 20),
            name="pairs",
        )(rid, pair_count, targets, linear_own, pair_w1, w2_row, *[partners[k] for k in ks])
        lin_grads.append(lin_grad)
        backs += back
        w2_sums.append(w2_sum[0])
        sq_sums.append(sq_sum[0, 0])
    returned = [backs[0]] + [permute(backs[k], k) for k in range(1, regions)]

    far = regions - near
    local_grad, far_hot, w1_part = pl.pallas_call(
        functools.partial(local_grad_kernel, regions=regions, groups=groups, near=near),
        out_shape=[
            shape((nets, feat), f32),
            shape((nets, far * slots), bf16),
            shape((2 * feat, hid), bf16),
        ],
        in_specs=[SM] + [VM] * (4 + regions + len(groups) + near),
        out_specs=[VM] * 3,
        scratch_shapes=[pltpu.VMEM((regions * slots, feat), bf16)],
        compiler_params=params(40),
        cost_estimate=cost(2 * nets * nets * feat * 3, 12 << 20),
        name="local_grads",
    )(rid, pair_local, asked, pair_w1, victim, *partners, *lin_grads, *returned[:near])

    share = 2 * feat * hid // devices
    scalars = jnp.zeros((2, 128), f32)
    scalars = scalars.at[0, 0].set(sum(sq_sums)).at[1, 0].set(jnp.sum(pair_count).astype(f32))
    short = jnp.concatenate([sum(w2_sums).reshape(-1, 128), scalars], 0)
    short = jnp.concatenate(two_parts(short), 0)
    short_rows = short.shape[0]
    w1_parts = jnp.concatenate(
        [
            w1_part.reshape(devices, share // 128, 128),
            jnp.broadcast_to(short[None], (devices, short_rows, 128)),
        ],
        1,
    )
    w1_got = jnp.sum(exchange(w1_parts, BOTH).astype(f32), 0)
    short_sum = w1_got[share // 128 :]
    short_sum = short_sum[: short_rows // 2] + short_sum[short_rows // 2 :]
    w2_total = short_sum[: hid // 128].reshape(hid)
    sq_total = short_sum[hid // 128, 0]
    total_count = short_sum[hid // 128 + 1, 0]
    root_count = jnp.sqrt(total_count)

    def spread(value):
        value = (8.0 * value / root_count).astype(bf16)
        wide = jnp.broadcast_to(value[None], (devices,) + value.shape)
        return exchange(wide, BOTH).reshape(2 * feat, hid).astype(f32)

    w1_grad = spread(w1_got[: share // 128])

    total_grad, pre_grad, agg_grad, halo_back = pl.pallas_call(
        functools.partial(layer_grad_kernel, far=far, degree=degree),
        out_shape=[
            shape((nets, feat), f32),
            shape((nets, feat), bf16),
            shape((feat, nets), bf16),
            shape((halo_rows, feat), bf16),
        ],
        in_specs=[VM] * (5 + far),
        out_specs=[VM] * 4,
        compiler_params=params(40),
        cost_estimate=cost(2 * nets * nets * feat * 2, 16 << 20),
        name="layer_grad",
    )(local_grad, far_hot, slope, gnn_weight, from_halo, *returned[near:])
    returned_halo = exchange(halo_back.reshape(peers, halo, feat), "dom").reshape(halo_rows, feat)

    gnn_part = pl.pallas_call(
        gnn_grad_kernel,
        out_shape=shape((2 * feat, feat), bf16),
        in_specs=[VM] * 3,
        out_specs=VM,
        compiler_params=params(24),
        cost_estimate=cost(2 * nets * 2 * feat * feat * 3, 4 << 20),
        name="gnn_grads",
    )(embeds, aggregate, pre_grad)
    gnn_got = jnp.sum(exchange(gnn_part.reshape(devices, share // 128, 128), BOTH).astype(f32), 0)
    gnn_grad = spread(gnn_got)

    own_grad = pl.pallas_call(
        own_grad_kernel,
        grid=(nets // BLOCK,),
        in_specs=[
            pl.BlockSpec((BLOCK, feat), lambda i: (i, 0)),
            pl.BlockSpec((BLOCK, feat), lambda i: (i, 0)),
            pl.BlockSpec((2 * feat, feat), lambda i: (0, 0)),
            pl.BlockSpec((feat, nets), lambda i: (0, 0)),
            pl.BlockSpec((nets, BLOCK), lambda i: (0, i)),
        ],
        out_specs=pl.BlockSpec((BLOCK, feat), lambda i: (i, 0)),
        out_shape=shape((nets, feat), f32),
        compiler_params=params(24),
        cost_estimate=cost(2 * nets * nets * feat * 2, 12 << 20),
        name="own_grads",
    )(total_grad, pre_grad, gnn_weight, agg_grad, own)

    scale = (8.0 * nets * devices / total_count).reshape(1)
    embeds_grad = pl.pallas_call(
        final_kernel,
        out_shape=shape((nets, feat), bf16),
        in_specs=[SM] + [VM] * 3,
        out_specs=VM,
        compiler_params=params(24),
        cost_estimate=cost(2 * nets * halo_rows * feat * 2, 6 << 20),
        name="embeds_grads",
    )(scale, halo_send, own_grad, returned_halo)
    return (
        embeds_grad,
        gnn_grad,
        w1_grad,
        8.0 * w2_total / root_count,
        sq_total / total_count,
    )


def solution(mesh):
    split = P(BOTH, None)
    in_specs = (split, split, split, P(), split, split, split, split, P(), P())
    out_specs = (split, P(), P(), P(), P())
    return jax.shard_map(local, mesh=mesh, in_specs=in_specs, out_specs=out_specs, check_vma=False)
```

time: 341 us -> 188 us (0.55)
  matrix products: 76.5 us -> 0 us
  waiting for transfers between devices: 110 us -> 37 us
  Pallas kernels: 0 us -> 60.4 us
  other arithmetic: 39.1 us -> 1.4 us
  blocking collectives: 41.8 us -> 14.3 us
  between operations: 19.3 us -> 7.43 us
  starting transfers between devices: 22.1 us -> 30.6 us
  local copies, waits for them, and re-layouts: 29.8 us -> 36.1 us
    psum x1 -> x0, waiting for transfers between devices: 89.9 us -> none  [local(): lax.psum((grad_gnn, grad_w1, grad_w2, sq_local), ('region', 'dom'))]
    dot_general x11 -> x0, matrix products: 76.5 us -> none  [the longest x1 30.3 us: local(): lax.dot_general(adjacency, agg_grad, contract_rows, preferred_element_typ...]
    pallas_call x0 -> x13, Pallas kernels: none -> 60.4 us  [the longest x1 12.6 us: local(): pl.pallas_call(adjacency_kernel, grid=(nets // BLOCK,), in_specs=[pl.Bloc...]
    psum x1 -> x0, blocking collectives: 41.8 us -> none  [local(): total_count = lax.psum(local_count, ('region', 'dom'))]
    scatter-add x2 -> x0, other arithmetic: 28.9 us -> none  [the longest x1 15.3 us: local(): nets_grad.at[asked.reshape(-1)]]
    unnamed x43 -> x71, local copies, waits for them, and re-layouts: 8.17 us -> 28.5 us
    gather x2 -> x0, local copies, waits for them, and re-layouts: 18 us -> none  [the longest x1 9.05 us: local(): nets[asked]]
    all_to_all x0 -> x1, blocking collectives: none -> 14.3 us  [exchange(): return lax.all_to_all(value, axis, split_axis=0, concat_axis=0, tiled=True)]
  transfers between devices with their start and end apart: 6 -> 12, of which waited for: 4 -> 5; matrix products, arithmetic and copies ran while one was open for 10% -> 2% of each run, Pallas kernels for 0% -> 22%
where the time goes in v1:
time: 188 us; the launch traced here: 187 us
  Pallas kernels  60.4 us (32%)
  waiting for transfers between devices  37 us (20%)
  local copies, waits for them, and re-layouts  36.1 us (19%)
  starting transfers between devices  30.6 us (16%)
  blocking collectives  14.3 us (8%)
  between operations  7.43 us (4%)
    all_to_all x6, waiting for transfers between devices, exchange(): return lax.all_to_all(value, axis, split_axis=0, concat_axis=0, tiled=True)  30.7 us
    unnamed x71, local copies, waits for them, and re-layouts  28.5 us
    all_to_all x6, starting transfers between devices, exchange(): return lax.all_to_all(value, axis, split_axis=0, concat_axis=0, tiled=True)  26.1 us
    all_to_all x1, blocking collectives, exchange(): return lax.all_to_all(value, axis, split_axis=0, concat_axis=0, tiled=True)  14.3 us
    pallas_call x1, Pallas kernels, local(): pl.pallas_call(adjacency_kernel, grid=(nets // BLOCK,), in_specs=[pl.Bloc...  12.6 us
    pallas_call x1, Pallas kernels, local(): pl.pallas_call(functools.partial(layer_kernel, degree=degree), out_shape=...  11.1 us
    pallas_call x1, Pallas kernels, local(): pl.pallas_call(functools.partial(layer_grad_kernel, far=far, degree=degre...  8.2 us
    pallas_call x1, Pallas kernels, local(): pl.pallas_call(victim_kernel, out_shape=[shape((regions, slots, feat), bf...  6.76 us
  transfers between devices with their start and end apart: 12, of which 5 were waited for; matrix products, arithmetic and copies ran while one was open for 2% of the time, Pallas kernels for 22%

profile of v1, /device:TPU:0, one launch (start us, length us, event | category | flops | bytes accessed | tf_op | source)
XLA Modules:
  0.0 187.1 jit_solution(9601429220454553116)
XLA Ops:
  0.6 1.3 reshape.136
  1.9 4.2 %all-to-all-start = ((s32[4,1,512]{2,1,0:T(1,128)}), s32[4,1,512]{2,1,0:T(1,128)S(1)}, u32[]{:S(2)}, u32[]{:S(2)}) async-start(s32[4,1,512]{2,1,0:T(1,128)} %reshape.136), calls=%async_computation | async-start | bytes 16384 | tf_op jit(solution)/shard_map/all_to_all | solution.py:291
  6.1 1.2 copy-done.4
  8.1 2.1 %halo_gather.1 = bf16[1024,256]{1,0:T(8,128)(2,1)} custom-call(s32[8,128]{1,0:T(8,128)S(1)} %copy-done.15, bf16[2048,256]{1,0:T(8,128)(2,1)S(1)} %copy-done.4), custom_call_target="tpu_custom_call" | custom-call | flops 1073741824 | bytes 2097152 | tf_op jit(solution)/shard_map/halo_gather/pallas_call | solution.py:324
  10.1 6.3 %all-to-all-start.1 = ((bf16[8,128,256]{2,1,0:T(8,128)(2,1)}), bf16[8,128,256]{2,1,0:T(8,128)(2,1)S(1)}, u32[]{:S(2)}, u32[]{:S(2)}) async-start(bf16[8,128,256]{2,1,0:T(8,128)(2,1)} %bitcast.2), calls=%async_computation.1 | async-start | bytes 1048576 | tf_op jit(solution)/shard_map/all_to_all | solution.py:291
  16.5 1.2 copy-done.5
  17.7 12.6 %adjacency.1 = (bf16[2048,2048]{1,0:T(8,128)(2,1)S(1)}, bf16[2048,1024]{1,0:T(8,128)(2,1)S(1)}, f32[2048,256]{1,0:T(8,128)S(1)}, f32[2048,256]{1,0:T(8,128)S(1)}) custom-call(s32[8,2048]{1,0:T(8,128)S(1)} %bitcast.20, bf16[2048,256]{1,0:T(8,128)(2,1)S(1)} %copy-done.5, bf16[2048,256]{1,0:T(8,128)(2,1)S(1)} %copy-done.5, bf16[512,256]{1,0:T(8,128)(2,1)S(1)} %copy-done.8), custom_call_target="tpu_custom_call" | custom-call | flops 16106127360 | bytes 20971520 | tf_op jit(solution)/shard_map/adjacency/pallas_call | solution.py:336
  30.3 2.0 %copy-done.1 = bf16[2048,1024]{1,0:T(8,128)(2,1)} copy-done((bf16[2048,1024]{1,0:T(8,128)(2,1)}, bf16[2048,1024]{1,0:T(8,128)(2,1)S(1)}, u32[]{:S(2)}) %copy-start.1) | copy-done | bytes 4194328
  32.3 1.4 copy-done.2
  33.7 3.3 %copy-done.18 = bf16[2048,2048]{1,0:T(8,128)(2,1)} copy-done((bf16[2048,2048]{1,0:T(8,128)(2,1)}, bf16[2048,2048]{1,0:T(8,128)(2,1)S(1)}, u32[]{:S(2)}) %copy-start.18) | copy-done | bytes 8388632
  37.0 0.9 asked_onehot.1.hot_ref
  37.9 3.3 %copy-done = bf16[4,512,2048]{2,1,0:T(8,128)(2,1)} copy-done((bf16[4,512,2048]{2,1,0:T(8,128)(2,1)}, bf16[4,512,2048]{2,1,0:T(8,128)(2,1)S(1)}, u32[]{:S(2)}) %copy-start) | copy-done | bytes 8388632
  41.2 1.6 copy-done.3
  42.8 1.2 copy-done.6
  44.0 11.1 %layer.1 = (f32[2048,256]{1,0:T(8,128)S(1)}, bf16[2048,256]{1,0:T(8,128)(2,1)S(1)}, bf16[2048,256]{1,0:T(8,128)(2,1)S(1)}, bf16[512,256]{1,0:T(8,128)(2,1)S(1)},...) custom-call(s32[1]{0:T(128)} %bitcast.rid_ref, bf16[2048,1024]{1,0:T(8,128)(2,1)} %copy-done.1, ...), custom_call_target="tpu_custom_call" | custom-call | flops 4294967296 | bytes 20971520 | tf_op jit(solution)/shard_map/layer/pallas_call | solution.py:372
  55.1 1.0 copy-done.9
  56.3 1.9 %collective-permute-start.2 = (bf16[512,256]{1,0:T(8,128)(2,1)}, bf16[512,256]{1,0:T(8,128)(2,1)S(1)}, u32[]{:S(2)}, u32[]{:S(2)}) collective-permute-start(bf16[512,256]{1,0:T(8,128)(2,1)} %get-tuple-element.72), channel_id=1, source_target_pairs={{0,24},{8,16},{16,8},{24,0},{1,25},{9,17},{17,9},{25,1},{2,26},{10... | collective-permute-start | bytes 786440 | tf_op jit(solution)/shard_map/ppermute | solution.py:322
  58.3 6.8 %victims.1 = (bf16[4,512,256]{2,1,0:T(8,128)(2,1)S(1)}, f32[4,512,256]{2,1,0:T(8,128)S(1)}, f32[2048,256]{1,0:T(8,128)S(1)}) custom-call(s32[1]{0:T(128)} %bitcast.rid_ref, s32[4,512]{1,0:T(4,128)S(1)} %copy-done.14, bf16[2048,256]{1,0:T(8,128)(2,1)S(1)} %get-tuple-element.66.nets_ref, bf16[512,256]{1,0:T(8,128)(2,1)S(1)} %copy-done.11, ...), custom_call_target="tpu_custom_call" | custom-call | flops 4294967296 | bytes 8388608 | tf_op jit(solution)/shard_map/victims/pallas_call | solution.py:389
  65.0 1.0 copy-done.32
  66.0 2.0 %pairs.3 = (bf16[2,512,256]{2,1,0:T(8,128)(2,1)S(1)}, f32[8,256]{1,0:T(8,128)S(1)}, f32[8,128]{1,0:T(8,128)S(1)}, bf16[512,256]{1,0:T(8,128)(2,1)S(1)}, bf16[512,256]{1,0:T(8,128)(2,1)S(1)}) custom-call(s32[1]{0:T(128)} %bitcast.rid_ref, s32[1,4]{1,0:T(1,128)S(1)} %copy-done.17, f32[4,512]{1,0:T(4,128)S(1)} %copy-done.13, ...), custom_call_target="tpu_custom_call" | custom-call | flops 2147483648 | bytes 2097152 | tf_op jit(solution)/shard_map/pairs/pallas_call | solution.py:407
  69.5 1.6 copy-done.23
  71.1 1.6 pairs.5
  72.7 2.0 %collective-permute-start.5 = (bf16[512,256]{1,0:T(8,128)(2,1)S(1)}, bf16[512,256]{1,0:T(8,128)(2,1)S(1)}, u32[]{:S(2)}, u32[]{:S(2)}) collective-permute-start(bf16[512,256]{1,0:T(8,128)(2,1)S(1)} %get-tuple-element.90), channel_id=1, source_target_pairs={{0,24},{8,16},{16,8},{24,0},{1,25},{9,17},{17,9},{25,1},{2,26},{10... | collective-permute-start | bytes 786440 | tf_op jit(solution)/shard_map/ppermute | solution.py:322
  74.7 1.4 pairs.4
  76.3 4.7 %local_grads.1 = (f32[2048,256]{1,0:T(8,128)S(1)}, bf16[2048,1024]{1,0:T(8,128)(2,1)S(1)}, bf16[512,256]{1,0:T(8,128)(2,1)S(1)}) custom-call(s32[1]{0:T(128)} %bitcast.rid_ref, s32[4,512]{1,0:T(4,128)S(1)} %copy-done.14, s32[4,512]{1,0:T(4,128)S(1)} %bitcast.19, bf16[512,256]{1,0:T(8,128)(2,1)S(1)} %copy-done.11, bf16[4,512,256]{2,1,0:T(8,128)(2,1)S(1)} %copy-done.33, ...), custom_call_target="tpu_custom_call" | custom-call | flops 6442450944 | bytes 12582912 | tf_op jit(solution)/shard_map/local_grads/pallas_call | solution.py:428
  81.4 5.8 %collective-permute-done.4.refs_0_ = bf16[512,256]{1,0:T(8,128)(2,1)S(1)} collective-permute-done((bf16[512,256]{1,0:T(8,128)(2,1)S(1)}, bf16[512,256]{1,0:T(8,128)(2,1)S(1)}, u32[]{:S(2)}, u32[]{:S(2)}) %collective-permute-start.4) | collective-permute-done | bytes 262176 | tf_op jit(solution)/shard_map/ppermute | solution.py:322
  87.2 8.2 %layer_grad.1 = (f32[2048,256]{1,0:T(8,128)S(1)}, bf16[2048,256]{1,0:T(8,128)(2,1)S(1)}, bf16[256,2048]{1,0:T(8,128)(2,1)S(1)}, bf16[1024,256]{1,0:T(8,128)(2,1)}) custom-call(f32[2048,256]{1,0:T(8,128)S(1)} %get-tuple-element.86.grad_ref, bf16[2048,1024]{1,0:T(8,128)(2,1)S(1)} %get-tuple-element.87.hot_ref, f32[2048,256]{1,0:T(8,128)S(1)} %copy-done.29, ...), custom_call_target="tpu_custom_call" | custom-call | flops 4294967296 | bytes 16777216 | tf_op jit(solution)/shard_map/layer_grad/pallas_call | solution.py:471
  95.4 1.3 copy-done.20
  96.7 1.0 copy-done.26
  97.7 0.8 gnn_grads.1
  98.5 1.0 copy-done.24
  99.5 0.8 reshape.146
  100.2 6.2 %all-to-all-start.4 = ((bf16[32,32,128]{2,1,0:T(8,128)(2,1)}), bf16[32,32,128]{2,1,0:T(8,128)(2,1)S(1)}, u32[]{:S(2)}, u32[]{:S(2)}) async-start(bf16[32,32,128]{2,1,0:T(8,128)(2,1)} %reshape.146), calls=%async_computation.4 | async-start | bytes 524288 | tf_op jit(solution)/shard_map/all_to_all | solution.py:291
  110.2 6.9 %all-to-all-done.4 = bf16[32,32,128]{2,1,0:T(8,128)(2,1)S(1)} async-done(((bf16[32,32,128]{2,1,0:T(8,128)(2,1)}), bf16[32,32,128]{2,1,0:T(8,128)(2,1)S(1)}, u32[]{:S(2)}, u32[]{:S(2)}) %all-to-all-start.4) | async-done | bytes 262176 | tf_op jit(solution)/shard_map/all_to_all | solution.py:291
  117.1 14.3 %all_to_all.35 = bf16[32,40,128]{2,1,0:T(8,128)(2,1)S(1)} all-to-all(bf16[32,40,128]{2,1,0:T(8,128)(2,1)S(1)} %pad_maximum_fusion), channel_id=1, replica_groups=mesh['region'=4,'dom'=8] {'region','dom'}, dimensions={0} | all-to-all | bytes 655360 | tf_op jit(solution)/shard_map/all_to_all | solution.py:291
  131.4 3.5 %all-to-all-start.3 = ((bf16[8,128,256]{2,1,0:T(8,128)(2,1)}), bf16[8,128,256]{2,1,0:T(8,128)(2,1)S(1)}, u32[]{:S(2)}, u32[]{:S(2)}) async-start(bf16[8,128,256]{2,1,0:T(8,128)(2,1)} %bitcast.7), calls=%async_computation.3 | async-start | bytes 1048576 | tf_op jit(solution)/shard_map/all_to_all | solution.py:291
  136.2 13.2 %all-to-all-done.3 = bf16[8,128,256]{2,1,0:T(8,128)(2,1)S(1)} async-done(((bf16[8,128,256]{2,1,0:T(8,128)(2,1)}), bf16[8,128,256]{2,1,0:T(8,128)(2,1)S(1)}, u32[]{:S(2)}, u32[]{:S(2)}) %all-to-all-start.3) | async-done | bytes 524320 | tf_op jit(solution)/shard_map/all_to_all | solution.py:291
  150.1 3.3 %all-to-all-start.6 = ((bf16[32,32,128]{2,1,0:T(8,128)(2,1)}), bf16[32,32,128]{2,1,0:T(8,128)(2,1)S(1)}, u32[]{:S(2)}, u32[]{:S(2)}) async-start(bf16[32,32,128]{2,1,0:T(8,128)(2,1)} %broadcast_in_dim.8), calls=%async_computation.6 | async-start | bytes 524288 | tf_op jit(solution)/shard_map/all_to_all | solution.py:291
  153.5 10.6 %all-to-all-done.6 = bf16[32,32,128]{2,1,0:T(8,128)(2,1)S(1)} async-done(((bf16[32,32,128]{2,1,0:T(8,128)(2,1)}), bf16[32,32,128]{2,1,0:T(8,128)(2,1)S(1)}, u32[]{:S(2)}, u32[]{:S(2)}) %all-to-all-start.6) | async-done | bytes 262176 | tf_op jit(solution)/shard_map/all_to_all | solution.py:291
  164.1 0.7 broadcast_in_dim.7
  164.9 2.6 %all-to-all-start.5 = ((bf16[32,32,128]{2,1,0:T(8,128)(2,1)}), bf16[32,32,128]{2,1,0:T(8,128)(2,1)S(1)}, u32[]{:S(2)}, u32[]{:S(2)}) async-start(bf16[32,32,128]{2,1,0:T(8,128)(2,1)} %broadcast_in_dim.7), calls=%async_computation.5 | async-start | bytes 524288 | tf_op jit(solution)/shard_map/all_to_all | solution.py:291
  167.5 3.4 %copy-done.19 = bf16[2048,2048]{1,0:T(8,128)(2,1)S(1)} copy-done((bf16[2048,2048]{1,0:T(8,128)(2,1)S(1)}, bf16[2048,2048]{1,0:T(8,128)(2,1)}, u32[]{:S(2)}) %copy-start.19) | copy-done | bytes 8388632
  170.8 1.2 copy-done.25
  172.1 1.2 copy-done.27
  173.3 6.1 %own_grads.1.own_ref = f32[2048,256]{1,0:T(8,128)S(1)} custom-call(f32[2048,256]{1,0:T(8,128)S(1)} %copy-done.21, bf16[2048,256]{1,0:T(8,128)(2,1)S(1)} %copy-done.25, bf16[512,256]{1,0:T(8,128)(2,1)S(1)} %copy-done.8, bf16[256,2048]{1,0:T(8,128)(2,1)S(1)} %copy-done.27, bf16[2048,2048]{1,0:T(8,128)(2,1)S(1)} %copy-done.19), custom_call_target="tpu_custom_call" | custom-call | flops 4294967296 | bytes 12582912 | tf_op jit(solution)/shard_map/own_grads/pallas_call | solution.py:499
  182.0 2.2 %embeds_grads.1 = bf16[2048,256]{1,0:T(8,128)(2,1)} custom-call(f32[1]{0:T(128)} %bitcast.6.scale_ref, s32[8,128]{1,0:T(8,128)S(1)} %copy-done.16, f32[2048,256]{1,0:T(8,128)S(1)} %own_grads.1.own_ref, bf16[1024,256]{1,0:T(8,128)(2,1)S(1)} %bitcast.17), custom_call_target="tpu_custom_call" | custom-call | flops 2147483648 | bytes 6291456 | tf_op jit(solution)/shard_map/embeds_grads/pallas_call | solution.py:517
  184.3 0.9 reshape.148
  185.1 0.9 reshape.147
  (88 shorter events, 6.1 us)
Async XLA Ops:
  1.9 8.2 %all-to-all-start = ((s32[4,1,512]{2,1,0:T(1,128)}), s32[4,1,512]{2,1,0:T(1,128)S(1)}, u32[]{:S(2)}, u32[]{:S(2)}) async-start(s32[4,1,512]{2,1,0:T(1,128)} %reshape.136), calls=%async_computation | async-start | bytes 16384 | tf_op jit(solution)/shard_map/all_to_all | solution.py:291
  6.1 1.2 copy-start.4
  7.4 0.7 copy-start.15
  8.1 8.4 %copy-start.8 = (bf16[512,256]{1,0:T(8,128)(2,1)S(1)}, bf16[512,256]{1,0:T(8,128)(2,1)}, u32[]{:S(2)}) copy-start(bf16[512,256]{1,0:T(8,128)(2,1)} %gnn_ref.7) | copy-start | bytes 786436
  8.1 8.4 %copy-start.12 = (s32[2048,8]{0,1:T(8,128)S(1)}, s32[2048,8]{0,1:T(8,128)}, u32[]{:S(2)}) copy-start(s32[2048,8]{0,1:T(8,128)} %param.15) | copy-start | bytes 196612
  10.1 31.0 %all-to-all-start.1 = ((bf16[8,128,256]{2,1,0:T(8,128)(2,1)}), bf16[8,128,256]{2,1,0:T(8,128)(2,1)S(1)}, u32[]{:S(2)}, u32[]{:S(2)}) async-start(bf16[8,128,256]{2,1,0:T(8,128)(2,1)} %bitcast.2), calls=%async_computation.1 | async-start | bytes 1048576 | tf_op jit(solution)/shard_map/all_to_all | solution.py:291
  16.5 1.2 copy-start.5
  17.7 19.2 %copy-start.34 = (bf16[256]{0:T(256)(128)(2,1)S(1)}, bf16[256]{0:T(256)(128)(2,1)}, u32[]{:S(2)}) copy-start(bf16[256]{0:T(256)(128)(2,1)} %param.23) | copy-start | bytes 1540
  30.3 2.0 %copy-start.1 = (bf16[2048,1024]{1,0:T(8,128)(2,1)}, bf16[2048,1024]{1,0:T(8,128)(2,1)S(1)}, u32[]{:S(2)}) copy-start(bf16[2048,1024]{1,0:T(8,128)(2,1)S(1)} %get-tuple-element.63.halo_ref) | copy-start | bytes 12582916
  32.3 1.4 copy-start.2
  33.7 3.3 %copy-start.18 = (bf16[2048,2048]{1,0:T(8,128)(2,1)}, bf16[2048,2048]{1,0:T(8,128)(2,1)S(1)}, u32[]{:S(2)}) copy-start(bf16[2048,2048]{1,0:T(8,128)(2,1)S(1)} %get-tuple-element.94.own_ref) | copy-start | bytes 25165828
  37.9 3.3 %copy-start = (bf16[4,512,2048]{2,1,0:T(8,128)(2,1)}, bf16[4,512,2048]{2,1,0:T(8,128)(2,1)S(1)}, u32[]{:S(2)}) copy-start(bf16[4,512,2048]{2,1,0:T(8,128)(2,1)S(1)} %asked_onehot.1.hot_ref) | copy-start | bytes 25165828
  41.2 1.6 copy-start.3
  42.8 1.2 copy-start.6
  44.0 14.2 %copy-start.11 = (bf16[512,256]{1,0:T(8,128)(2,1)S(1)}, bf16[512,256]{1,0:T(8,128)(2,1)}, u32[]{:S(2)}) copy-start(bf16[512,256]{1,0:T(8,128)(2,1)} %w1_ref.9) | copy-start | bytes 786436
  44.0 14.2 %copy-start.14 = (s32[4,512]{1,0:T(4,128)S(1)}, s32[4,512]{1,0:T(4,128)}, u32[]{:S(2)}) copy-start(s32[4,512]{1,0:T(4,128)} %local_ref.3) | copy-start | bytes 24580
  55.1 1.0 copy-start.9
  56.1 9.9 %collective-permute-start = (bf16[512,256]{1,0:T(8,128)(2,1)S(1)}, bf16[512,256]{1,0:T(8,128)(2,1)S(1)}, u32[]{:S(2)}, u32[]{:S(2)}) collective-permute-start(bf16[512,256]{1,0:T(8,128)(2,1)S(1)} %get-tuple-element.70), channel_id=1, source_target_pairs={{0,8},{8,0},{16,24},{24,16},{1,9},{9,1},{17,25},{25,17},{2,10},{10... | collective-permute-start | bytes 786440 | tf_op jit(solution)/shard_map/ppermute | solution.py:322
  56.3 13.2 %collective-permute-start.2 = (bf16[512,256]{1,0:T(8,128)(2,1)}, bf16[512,256]{1,0:T(8,128)(2,1)S(1)}, u32[]{:S(2)}, u32[]{:S(2)}) collective-permute-start(bf16[512,256]{1,0:T(8,128)(2,1)} %get-tuple-element.72), channel_id=1, source_target_pairs={{0,24},{8,16},{16,8},{24,0},{1,25},{9,17},{17,9},{25,1},{2,26},{10... | collective-permute-start | bytes 786440 | tf_op jit(solution)/shard_map/ppermute | solution.py:322
  58.2 16.5 %collective-permute-start.1 = (bf16[512,256]{1,0:T(8,128)(2,1)}, bf16[512,256]{1,0:T(8,128)(2,1)S(1)}, u32[]{:S(2)}, u32[]{:S(2)}) collective-permute-start(bf16[512,256]{1,0:T(8,128)(2,1)} %get-tuple-element.71), channel_id=1, source_target_pairs={{0,16},{8,24},{16,0},{24,8},{1,17},{9,25},{17,1},{25,9},{2,18},{10... | collective-permute-start | bytes 786440 | tf_op jit(solution)/shard_map/ppermute | solution.py:322
  58.2 7.8 %copy-start.13 = (f32[4,512]{1,0:T(4,128)S(1)}, f32[4,512]{1,0:T(4,128)}, u32[]{:S(2)}) copy-start(f32[4,512]{1,0:T(4,128)} %target_ref.5) | copy-start | bytes 24580
  58.3 7.8 %copy-start.17 = (s32[1,4]{1,0:T(1,128)S(1)}, s32[1,4]{1,0:T(1,128)}, u32[]{:S(2)}) copy-start(s32[1,4]{1,0:T(1,128)} %count_ref.5) | copy-start | bytes 52
  65.0 1.0 copy-start.32
  66.0 2.0 %copy-start.22 = (f32[4,512,256]{2,1,0:T(8,128)}, f32[4,512,256]{2,1,0:T(8,128)S(1)}, u32[]{:S(2)}) copy-start(f32[4,512,256]{2,1,0:T(8,128)S(1)} %get-tuple-element.73.linear_ref) | copy-start | bytes 6291460
  66.0 2.1 %copy-start.28 = (f32[2048,256]{1,0:T(8,128)}, f32[2048,256]{1,0:T(8,128)S(1)}, u32[]{:S(2)}) copy-start(f32[2048,256]{1,0:T(8,128)S(1)} %get-tuple-element.88.slope_ref) | copy-start | bytes 6291460
  68.1 4.6 %copy-start.30 = (bf16[2,512,256]{2,1,0:T(8,128)(2,1)}, bf16[2,512,256]{2,1,0:T(8,128)(2,1)S(1)}, u32[]{:S(2)}) copy-start(bf16[2,512,256]{2,1,0:T(8,128)(2,1)S(1)} %get-tuple-element.74.refs_4_) | copy-start | bytes 1572868
  68.1 8.2 %collective-permute-start.3 = (bf16[512,256]{1,0:T(8,128)(2,1)S(1)}, bf16[512,256]{1,0:T(8,128)(2,1)S(1)}, u32[]{:S(2)}, u32[]{:S(2)}) collective-permute-start(bf16[512,256]{1,0:T(8,128)(2,1)S(1)} %get-tuple-element.78), channel_id=1, source_target_pairs={{0,8},{8,0},{16,24},{24,16},{1,9},{9,1},{17,25},{25,17},{2,10},{10... | collective-permute-start | bytes 786440 | tf_op jit(solution)/shard_map/ppermute | solution.py:322
  69.5 1.6 copy-start.23
  72.7 3.6 %copy-start.33 = (bf16[4,512,256]{2,1,0:T(8,128)(2,1)S(1)}, bf16[4,512,256]{2,1,0:T(8,128)(2,1)}, u32[]{:S(2)}) copy-start(bf16[4,512,256]{2,1,0:T(8,128)(2,1)} %copy-done.32) | copy-start | bytes 3145732
  72.7 3.6 %copy-start.31 = (bf16[2,512,256]{2,1,0:T(8,128)(2,1)S(1)}, bf16[2,512,256]{2,1,0:T(8,128)(2,1)}, u32[]{:S(2)}) copy-start(bf16[2,512,256]{2,1,0:T(8,128)(2,1)} %copy-done.30) | copy-start | bytes 1572868
  72.7 8.7 %collective-permute-start.5 = (bf16[512,256]{1,0:T(8,128)(2,1)S(1)}, bf16[512,256]{1,0:T(8,128)(2,1)S(1)}, u32[]{:S(2)}, u32[]{:S(2)}) collective-permute-start(bf16[512,256]{1,0:T(8,128)(2,1)S(1)} %get-tuple-element.90), channel_id=1, source_target_pairs={{0,24},{8,16},{16,8},{24,0},{1,25},{9,17},{17,9},{25,1},{2,26},{10... | collective-permute-start | bytes 786440 | tf_op jit(solution)/shard_map/ppermute | solution.py:322
  76.1 11.1 %collective-permute-start.4 = (bf16[512,256]{1,0:T(8,128)(2,1)S(1)}, bf16[512,256]{1,0:T(8,128)(2,1)S(1)}, u32[]{:S(2)}, u32[]{:S(2)}) collective-permute-start(bf16[512,256]{1,0:T(8,128)(2,1)S(1)} %get-tuple-element.89), channel_id=1, source_target_pairs={{0,16},{8,24},{16,0},{24,8},{1,17},{9,25},{17,1},{25,9},{2,18},{10... | collective-permute-start | bytes 786440 | tf_op jit(solution)/shard_map/ppermute | solution.py:322
  76.3 10.9 %copy-start.29 = (f32[2048,256]{1,0:T(8,128)S(1)}, f32[2048,256]{1,0:T(8,128)}, u32[]{:S(2)}) copy-start(f32[2048,256]{1,0:T(8,128)} %copy-done.28) | copy-start | bytes 6291460
  87.2 10.5 %copy-start.7 = (bf16[2048,256]{1,0:T(8,128)(2,1)S(1)}, bf16[2048,256]{1,0:T(8,128)(2,1)}, u32[]{:S(2)}) copy-start(bf16[2048,256]{1,0:T(8,128)(2,1)} %embeds_ref.7) | copy-start | bytes 3145732
  87.2 10.5 %copy-start.10 = (bf16[2048,256]{1,0:T(8,128)(2,1)S(1)}, bf16[2048,256]{1,0:T(8,128)(2,1)}, u32[]{:S(2)}) copy-start(bf16[2048,256]{1,0:T(8,128)(2,1)} %copy-done.9) | copy-start | bytes 3145732
  95.4 1.3 copy-start.20
  96.7 1.0 copy-start.26
  98.5 1.0 copy-start.24
  100.2 16.8 %all-to-all-start.4 = ((bf16[32,32,128]{2,1,0:T(8,128)(2,1)}), bf16[32,32,128]{2,1,0:T(8,128)(2,1)S(1)}, u32[]{:S(2)}, u32[]{:S(2)}) async-start(bf16[32,32,128]{2,1,0:T(8,128)(2,1)} %reshape.146), calls=%async_computation.4 | async-start | bytes 524288 | tf_op jit(solution)/shard_map/all_to_all | solution.py:291
  110.2 57.3 %copy-start.21 = (f32[2048,256]{1,0:T(8,128)S(1)}, f32[2048,256]{1,0:T(8,128)}, u32[]{:S(2)}) copy-start(f32[2048,256]{1,0:T(8,128)} %copy-done.20) | copy-start | bytes 6291460
  131.4 18.0 %all-to-all-start.3 = ((bf16[8,128,256]{2,1,0:T(8,128)(2,1)}), bf16[8,128,256]{2,1,0:T(8,128)(2,1)S(1)}, u32[]{:S(2)}, u32[]{:S(2)}) async-start(bf16[8,128,256]{2,1,0:T(8,128)(2,1)} %bitcast.7), calls=%async_computation.3 | async-start | bytes 1048576 | tf_op jit(solution)/shard_map/all_to_all | solution.py:291
  150.1 14.0 %all-to-all-start.6 = ((bf16[32,32,128]{2,1,0:T(8,128)(2,1)}), bf16[32,32,128]{2,1,0:T(8,128)(2,1)S(1)}, u32[]{:S(2)}, u32[]{:S(2)}) async-start(bf16[32,32,128]{2,1,0:T(8,128)(2,1)} %broadcast_in_dim.8), calls=%async_computation.6 | async-start | bytes 524288 | tf_op jit(solution)/shard_map/all_to_all | solution.py:291
  164.9 20.3 %all-to-all-start.5 = ((bf16[32,32,128]{2,1,0:T(8,128)(2,1)}), bf16[32,32,128]{2,1,0:T(8,128)(2,1)S(1)}, u32[]{:S(2)}, u32[]{:S(2)}) async-start(bf16[32,32,128]{2,1,0:T(8,128)(2,1)} %broadcast_in_dim.7), calls=%async_computation.5 | async-start | bytes 524288 | tf_op jit(solution)/shard_map/all_to_all | solution.py:291
  167.5 3.4 %copy-start.19 = (bf16[2048,2048]{1,0:T(8,128)(2,1)S(1)}, bf16[2048,2048]{1,0:T(8,128)(2,1)}, u32[]{:S(2)}) copy-start(bf16[2048,2048]{1,0:T(8,128)(2,1)} %copy-done.18) | copy-start | bytes 25165828
  170.8 1.2 copy-start.25
  172.1 1.2 copy-start.27
  173.3 8.7 %copy-start.16 = (s32[8,128]{1,0:T(8,128)S(1)}, s32[8,128]{1,0:T(8,128)}, u32[]{:S(2)}) copy-start(s32[8,128]{1,0:T(8,128)} %send_ref.3) | copy-start | bytes 12292

commit v2 on v0

v2 whole, which is shorter than its diff:
```python
import functools

import jax
import jax.numpy as jnp
from jax import lax
from jax.experimental import pallas as pl
from jax.experimental.pallas import tpu as pltpu
from jax.sharding import PartitionSpec as P

bf16 = jnp.bfloat16
f32 = jnp.float32
i32 = jnp.int32
i16 = jnp.int16
gelu_coef = 0.7978845608
BOTH = ("region", "dom")
BLOCK = 256
STEP = 512
TT = (((0,), (0,)), ((), ()))
NT = (((1,), (1,)), ((), ()))


def mm(a, b):
    return jnp.dot(a, b, preferred_element_type=f32)


def mm_dims(a, b, dims):
    return lax.dot_general(a, b, dims, preferred_element_type=f32)


def gelu_inner(value, square):
    return jnp.tanh(value * (gelu_coef + (gelu_coef * 0.044715) * square))


def gelu_of(value):
    half = 0.5 * value
    return half + half * gelu_inner(value, value * value)


def slope_of(value, square, inner):
    rise = value * (0.5 * gelu_coef + (1.5 * 0.044715 * gelu_coef) * square)
    return 0.5 + 0.5 * inner + (1.0 - inner * inner) * rise


def column_of(row):
    return jnp.broadcast_to(row, (128, row.shape[1])).T


def onehot_rows(row, width):
    column = column_of(row).astype(i16)
    lane = lax.broadcasted_iota(i32, column.shape, 1).astype(i16)
    one = jnp.ones(column.shape, bf16)
    zero = jnp.zeros(column.shape, bf16)
    return jnp.concatenate(
        [jnp.where(column == lane + jnp.int16(128 * j), one, zero) for j in range(width // 128)], 1
    )


def onehot_cols(row, first, height):
    shape = (height, row.shape[1])
    wide = jnp.broadcast_to(row - first, shape).astype(i16)
    sub = lax.broadcasted_iota(i32, shape, 0).astype(i16)
    return jnp.where(wide == sub, jnp.ones(shape, bf16), jnp.zeros(shape, bf16))


def halo_gather_kernel(send_ref, embeds_ref, out_ref):
    peers, halo = send_ref.shape
    nets = embeds_ref.shape[0]
    for p in range(peers):
        hot = onehot_rows(send_ref[p : p + 1, :], nets)
        out_ref[p * halo : (p + 1) * halo, :] = mm(hot, embeds_ref[...]).astype(bf16)


def adjacency_kernel(neigh_ref, embeds_ref, own_ref, halo_ref, sum_ref):
    degree = neigh_ref.shape[0]
    rows, nets = own_ref.shape
    listed = [neigh_ref[c : c + 1, :] for c in range(degree)]
    columns, counts = [], []
    for c in range(degree):
        count = jnp.ones_like(listed[c])
        seen = None
        for e in range(degree):
            if e != c:
                same = listed[e] == listed[c]
                if e > c:
                    count = count + same.astype(i32)
                else:
                    seen = same if seen is None else (seen | same)
        index = listed[c] if seen is None else jnp.where(seen, -1, listed[c])
        columns.append(column_of(index).astype(i16))
        counts.append(column_of(count).astype(f32).astype(bf16))
    lane = lax.broadcasted_iota(i32, (rows, 128), 1).astype(i16)
    zero = jnp.zeros((rows, 128), bf16)

    def tile(at):
        acc = zero
        here = lane + jnp.int16(at)
        for c in range(degree):
            acc = jnp.where(columns[c] == here, counts[c], acc)
        return acc

    for at in range(0, nets, 128):
        own_ref[:, at : at + 128] = tile(at)
    for at in range(0, halo_ref.shape[1], 128):
        halo_ref[:, at : at + 128] = tile(nets + at)
    sum_ref[...] = mm(own_ref[...], embeds_ref[...])


def layer_kernel(halo_ref, sum_ref, embeds_ref, gnn_ref, received_ref, *refs, degree, far):
    asked_refs, (pre_ref, agg_ref, nets_ref), send_refs = (
        refs[:far],
        refs[far : far + 3],
        refs[far + 3 :],
    )
    nets, feat = nets_ref.shape
    for at in range(0, nets, STEP):
        rows = pl.ds(at, STEP)
        total = sum_ref[rows, :] + mm(halo_ref[rows, :], received_ref[...])
        agg = (total * (1.0 / degree)).astype(bf16)
        agg_ref[rows, :] = agg
        agg_ref.flush(at + STEP)
        pre = mm(embeds_ref[rows, :], gnn_ref[:feat, :]) + mm(agg, gnn_ref[feat:, :])
        pre_ref[rows, :] = pre
        nets_ref[rows, :] = (embeds_ref[rows, :].astype(f32) + gelu_of(pre)).astype(bf16)
    for asked_ref, send_ref in zip(asked_refs, send_refs, strict=True):
        hot = onehot_rows(asked_ref[...], nets)
        send_ref[...] = mm(hot, nets_ref[...]).astype(bf16)


def gather_kernel(nets_ref, *refs):
    some = len(refs) // 2
    for asked_ref, out_ref in zip(refs[:some], refs[some:], strict=True):
        hot = onehot_rows(asked_ref[...], nets_ref.shape[0])
        out_ref[...] = mm(hot, nets_ref[...]).astype(bf16)


def victim_kernel(rid_ref, local_ref, nets_ref, w1_ref, pre_ref, victim_ref, linear_ref, slope_ref):
    regions, slots = local_ref.shape
    nets, feat = nets_ref.shape
    me = rid_ref[0]
    for k in range(regions):
        hot = onehot_rows(local_ref[pl.ds(me ^ k, 1), :], nets)
        victim = mm(hot, nets_ref[...]).astype(bf16)
        victim_ref[k] = victim
        victim_ref.flush(k + 1)
        linear_ref[k] = mm(victim, w1_ref[:feat, :])
    for at in range(0, nets, STEP):
        rows = pl.ds(at, STEP)
        pre = pre_ref[rows, :]
        square = pre * pre
        slope_ref[rows, :] = slope_of(pre, square, gelu_inner(pre, square))
        slope_ref.flush(at + STEP)


def pair_kernel(rid_ref, count_ref, target_ref, linear_ref, w1_ref, w2_ref, *refs, ks, first, last):
    some = len(ks)
    partner_refs, refs = refs[:some], refs[some:]
    if not first:
        before_ref, refs = refs[0], refs[1:]
    lin_grad_ref, sums_ref, *back_refs = refs
    me = rid_ref[0]
    slots, hid = linear_ref.shape[1:]
    feat = partner_refs[0].shape[1]
    w2_row = w2_ref[...].astype(f32)
    w2_column = column_of(w2_row).astype(bf16)
    w2_sum = jnp.zeros((1, hid), f32) if first else before_ref[0:1, :]
    sq_sum = jnp.zeros((1, hid), f32) if first else before_ref[1:2, :]
    slot = lax.broadcasted_iota(i32, (slots, 128), 0)
    for at, k in enumerate(ks):
        linear = linear_ref[k] + mm(partner_refs[at][...], w1_ref[feat:, :])
        square = linear * linear
        inner = gelu_inner(linear, square)
        half = 0.5 * linear
        activated = (half + half * inner).astype(bf16)
        scores = mm(activated, w2_column)
        live = slot < count_ref[0, me ^ k]
        errors = jnp.where(live, scores - column_of(target_ref[pl.ds(me ^ k, 1), :]), 0.0)
        errors = jnp.concatenate([errors] * (hid // 128), 1)
        sq_sum = sq_sum + jnp.sum(errors * errors, 0, keepdims=True)
        residual = 2.0 * errors
        w2_sum = w2_sum + jnp.sum(residual * activated.astype(f32), 0, keepdims=True)
        lin_grad = (residual * w2_row * slope_of(linear, square, inner)).astype(bf16)
        lin_grad_ref[at] = lin_grad
        lin_grad_ref.flush(at + 1)
        back_refs[at][...] = mm_dims(lin_grad, w1_ref[feat:, :], NT).astype(bf16)
    if not last:
        sums_ref[...] = jnp.concatenate([w2_sum, sq_sum, jnp.zeros((6, hid), f32)], 0)
    else:
        count = count_ref[0, 0]
        for q in range(1, count_ref.shape[1]):
            count = count + count_ref[0, q]
        count_row = jnp.zeros((1, hid), f32) + count.astype(f32)
        parts = []
        for row in (w2_sum, sq_sum, count_row):
            high = row.astype(bf16).astype(f32)
            parts += [high, row - high]
        sums_ref[...] = jnp.concatenate(parts + [jnp.zeros((2, hid), f32)], 0)


def w1_grad_kernel(after_ref, victim_ref, sums_ref, *refs, groups):
    regions, _, feat = victim_ref.shape
    partner_refs, lin_refs, out_ref = refs[:regions], refs[regions:-1], refs[-1]
    devices, rows, hid = out_ref.shape
    share = 2 * feat // devices
    top = jnp.zeros((feat, hid), f32)
    low = jnp.zeros((feat, hid), f32)
    for ref, ks in zip(lin_refs, groups, strict=True):
        for at, k in enumerate(ks):
            low = low + mm_dims(partner_refs[k][...], ref[at], TT)
            top = top + mm_dims(victim_ref[k], ref[at], TT)
    both = jnp.concatenate([top, low], 0)
    short = sums_ref[...]
    for d in range(devices):
        out_ref[d] = jnp.concatenate([both[d * share : (d + 1) * share], short], 0).astype(bf16)


def local_grad_kernel(rid_ref, local_ref, w1_ref, *refs, groups, near):
    asked_refs, refs = refs[:near], refs[near:]
    near_refs, refs = refs[:near], refs[near:]
    lin_refs, (grad_ref, vg_ref) = refs[:-2], refs[-2:]
    me = rid_ref[0]
    regions, slots = local_ref.shape
    nets, feat = grad_ref.shape
    for ref, ks in zip(lin_refs, groups, strict=True):
        for at, k in enumerate(ks):
            vg_ref[k * slots : (k + 1) * slots, :] = mm_dims(ref[at], w1_ref[:feat, :], NT).astype(
                bf16
            )
    local = [local_ref[pl.ds(me ^ k, 1), :] for k in range(regions)]
    for at in range(0, nets, BLOCK):
        hot = jnp.concatenate([onehot_cols(row, at, BLOCK) for row in local], 1)
        total = mm(hot, vg_ref[...])
        for k in range(near):
            total = total + mm(onehot_cols(asked_refs[k][...], at, BLOCK), near_refs[k][...])
        grad_ref[at : at + BLOCK, :] = total


def layer_grad_kernel(
    cid_ref, slope_ref, embeds_ref, agg_ref, gnn_ref, halo_ref, grad_ref, *refs, far, peers, degree
):
    asked_refs, refs = refs[:far], refs[far:]
    far_refs, refs = refs[:far], refs[far:]
    (total_ref, pre_grad_ref, agg_grad_ref, gnn_out_ref), refs = refs[:4], refs[4:]
    back_refs, back_ref = refs[:-1], refs[-1]
    nets, feat = grad_ref.shape
    halo = back_refs[0].shape[0]
    top = jnp.zeros((feat, feat), f32)
    low = jnp.zeros((feat, feat), f32)
    for at in range(0, nets, STEP):
        rows = pl.ds(at, STEP)
        total = grad_ref[rows, :]
        for k in range(far):
            total = total + mm(onehot_cols(asked_refs[k][...], at, STEP), far_refs[k][...])
        total_ref[rows, :] = total
        total_ref.flush(at + STEP)
        pre_grad = (total * slope_ref[rows, :]).astype(bf16)
        pre_grad_ref[rows, :] = pre_grad
        pre_grad_ref.flush(at + STEP)
        agg_grad = mm_dims(gnn_ref[feat:, :], pre_grad, NT)
        agg_grad_ref[:, rows] = (agg_grad * (1.0 / degree)).astype(bf16)
        top = top + mm_dims(embeds_ref[rows, :], pre_grad, TT)
        low = low + mm_dims(agg_ref[rows, :], pre_grad, TT)
    agg_grad_ref.flush()
    gnn_out_ref[:feat, :] = top.astype(bf16)
    gnn_out_ref[feat:, :] = low.astype(bf16)
    for at in range(0, halo_ref.shape[1], BLOCK):
        back = mm(agg_grad_ref[...], halo_ref[:, at : at + BLOCK])
        back_ref[at : at + BLOCK, :] = back.T.astype(bf16)
    me = cid_ref[0]
    for k, out_ref in enumerate(back_refs):
        out_ref[...] = back_ref[pl.ds(pl.multiple_of((me ^ k) * halo, halo), halo), :]


def own_grad_kernel(total_ref, pre_grad_ref, gnn_ref, agg_grad_ref, own_ref, out_ref):
    nets, feat = total_ref.shape
    for at in range(0, nets, STEP):
        rows = pl.ds(at, STEP)
        out_ref[rows, :] = (
            total_ref[rows, :]
            + mm_dims(pre_grad_ref[rows, :], gnn_ref[:feat, :], NT)
            + mm(agg_grad_ref[...], own_ref[:, rows]).T
        )


def share_kernel(w1_ref, gnn_ref, *refs, nets_total):
    wide_ref, short_ref = refs[-2:]
    share, hid = gnn_ref.shape[1:]
    w1_sum = jnp.sum(w1_ref[...].astype(f32), 0)
    gnn_sum = jnp.sum(gnn_ref[...].astype(f32), 0)
    short = w1_sum[share:]
    w2_sum = short[0:1] + short[1:2]
    sq_sum = short[2:3] + short[3:4]
    count = short[4:5] + short[5:6]
    factor = 8.0 / jnp.sqrt(count)
    both = (jnp.concatenate([w1_sum[:share], gnn_sum], 0) * factor).astype(bf16)
    wide_ref[...] = jnp.broadcast_to(both[None], wide_ref.shape)
    short_ref[...] = jnp.concatenate(
        [w2_sum * factor, sq_sum / count, 8.0 * nets_total / count, jnp.zeros((5, hid), f32)], 0
    )


def unpack_kernel(spread_ref, w1_ref, gnn_ref):
    devices, rows, _ = spread_ref.shape
    share = rows // 2
    for d in range(devices):
        got = spread_ref[d].astype(f32)
        w1_ref[d * share : (d + 1) * share, :] = got[:share]
        gnn_ref[d * share : (d + 1) * share, :] = got[share:]
        if (d + 1) % (devices // PARTS) == 0:
            w1_ref.flush((d + 1) * share)
            gnn_ref.flush((d + 1) * share)


def final_kernel(cid_ref, short_ref, send_ref, own_ref, *refs):
    got_refs, out_ref = refs[:-1], refs[-1]
    nets = out_ref.shape[0]
    me = cid_ref[0]
    scale = short_ref[2:3, :]
    got = jnp.concatenate([ref[...] for ref in got_refs], 0)
    sent = [send_ref[pl.ds(me ^ k, 1), :] for k in range(len(got_refs))]
    for at in range(0, nets, BLOCK):
        hot = jnp.concatenate([onehot_cols(row, at, BLOCK) for row in sent], 1)
        total = own_ref[at : at + BLOCK, :] + mm(hot, got)
        out_ref[at : at + BLOCK, :] = (total * scale).astype(bf16)


SM = pl.BlockSpec(memory_space=pltpu.SMEM)
VM = pl.BlockSpec(memory_space=pltpu.VMEM)
ANY = pl.BlockSpec(memory_space=pl.ANY)
SMALL = pl.CostEstimate(flops=1, bytes_accessed=1, transcendentals=0)
PARTS = 4


def shape(dims, dtype):
    return jax.ShapeDtypeStruct(dims, dtype)


def in_hbm(dims, dtype):
    return pltpu.MemorySpace.HBM(dims, dtype)


class Load:
    def __init__(self, source, target, sems):
        self.target, self.waited = target, 0
        self.shape = source.shape
        self.rows = max(source.shape[0] // PARTS, 1)
        self.copies = []
        for at in range(source.shape[0] // self.rows):
            part = pl.ds(at * self.rows, self.rows)
            self.copies.append(
                pltpu.make_async_copy(source.at[part], target.at[part], sems.at[at])
            )

    def __getitem__(self, index):
        first = index[0] if isinstance(index, tuple) else index
        last = self.shape[0]
        if isinstance(first, int):
            last = first + 1
        elif isinstance(first, pl.Slice):
            last = first.start + first.size
        while self.waited < -(-last // self.rows):
            self.copies[self.waited].wait()
            self.waited += 1
        return self.target[index]


class Store:
    def __init__(self, source, target, sems):
        self.source, self.target, self.sems = source, target, sems
        self.shape, self.dtype = source.shape, source.dtype
        self.copies, self.sent = [], 0

    def __setitem__(self, index, value):
        self.source[index] = value

    def __getitem__(self, index):
        return self.source[index]

    def flush(self, upto=None):
        upto = self.shape[0] if upto is None else upto
        part = pl.ds(self.sent, upto - self.sent)
        self.copies.append(
            pltpu.make_async_copy(
                self.source.at[part], self.target.at[part], self.sems.at[len(self.copies)]
            )
        )
        self.copies[-1].start()
        self.sent = upto

    def finish(self):
        if self.sent < self.shape[0]:
            self.flush()
        for copy in self.copies:
            copy.wait()


def call(kernel, name, outs, args, scratch=(), mib=24, flops=1):
    ins = [kind for _, kind in args]
    kinds = [kind for _, _, kind in outs]
    staged = [pltpu.VMEM(value.shape, value.dtype) for value, kind in args if kind == "H"]
    staged += [pltpu.VMEM(dims, dtype) for dims, dtype, kind in outs if kind == "H"]
    moved = len(staged)

    def body(*refs):
        operands, refs = list(refs[: len(ins)]), refs[len(ins) :]
        results, refs = list(refs[: len(kinds)]), refs[len(kinds) :]
        buffers, refs = list(refs[:moved]), refs[moved:]
        if moved:
            sems, refs = refs[0], refs[1:]
        at = 0
        for i, kind in enumerate(ins):
            if kind == "H":
                operands[i] = Load(operands[i], buffers[at], sems.at[at])
                at += 1
        loads = [operand for operand in operands if isinstance(operand, Load)]
        for part in range(PARTS):
            for load in loads:
                if part < len(load.copies):
                    load.copies[part].start()
        for i, kind in enumerate(kinds):
            if kind == "H":
                results[i] = Store(buffers[at], results[i], sems.at[at])
                at += 1
        kernel(*operands, *results, *refs)
        for result in results:
            if isinstance(result, Store):
                result.finish()

    spec_of = {"V": VM, "H": ANY, "S": SM, "A": ANY}
    return pl.pallas_call(
        body,
        out_shape=[(in_hbm if kind == "H" else shape)(dims, dtype) for dims, dtype, kind in outs],
        in_specs=[spec_of[kind] for kind in ins],
        out_specs=[spec_of[kind] for kind in kinds],
        scratch_shapes=staged
        + ([pltpu.SemaphoreType.DMA((moved, 2 * PARTS))] if moved else [])
        + list(scratch),
        compiler_params=pltpu.CompilerParams(vmem_limit_bytes=mib << 20),
        cost_estimate=pl.CostEstimate(flops=flops, bytes_accessed=1, transcendentals=0),
        name=name,
    )(
        *[
            pltpu.with_memory_space_constraint(value, pltpu.HBM) if kind == "H" else value
            for value, kind in args
        ]
    )


def exchange(value, axis):
    return lax.all_to_all(value, axis, split_axis=0, concat_axis=0, tiled=True)


def local(
    embeds,
    neighbours,
    halo_send,
    gnn_weight,
    pair_local,
    pair_remote,
    pair_count,
    targets,
    pair_w1,
    pair_w2,
):
    nets, feat = embeds.shape
    hid = pair_w1.shape[1]
    degree = neighbours.shape[1]
    regions, slots = pair_local.shape
    peers, halo = halo_send.shape
    halo_rows = peers * halo
    devices = lax.axis_size("region") * lax.axis_size("dom")
    my_region = lax.axis_index("region").astype(i32)
    rid = my_region.reshape(1)
    cid = lax.axis_index("dom").astype(i32).reshape(1)
    near = 2
    far = regions - near
    share = 2 * feat // devices

    def permute(value, k, axis="region"):
        size = lax.axis_size(axis)
        return lax.ppermute(value, axis, [(i, i ^ k) for i in range(size)])

    def v(*values):
        return [(value, "V") for value in values]

    def h(*values):
        return [(value, "H") for value in values]

    def out(kind, dtype, *dims):
        return [(dims, dtype, kind)]

    (outgoing,) = call(
        halo_gather_kernel,
        "halo_gather",
        out("V", bf16, halo_rows, feat),
        v(halo_send) + h(embeds),
    )
    received = exchange(outgoing.reshape(peers, halo, feat), "dom").reshape(halo_rows, feat)

    wanted = [lax.dynamic_slice_in_dim(pair_remote, my_region ^ k, 1, 0) for k in range(regions)]
    asked = [wanted[0]] + [permute(wanted[k], k) for k in range(1, regions)]

    own, from_halo, agg_sum = pl.pallas_call(
        adjacency_kernel,
        grid=(nets // BLOCK,),
        in_specs=[
            pl.BlockSpec((degree, BLOCK), lambda i: (0, i)),
            pl.BlockSpec((nets, feat), lambda i: (0, 0)),
        ],
        out_specs=[
            pl.BlockSpec((BLOCK, nets), lambda i: (i, 0)),
            pl.BlockSpec((BLOCK, halo_rows), lambda i: (i, 0)),
            pl.BlockSpec((BLOCK, feat), lambda i: (i, 0)),
        ],
        out_shape=[
            in_hbm((nets, nets), bf16),
            in_hbm((nets, halo_rows), bf16),
            in_hbm((nets, feat), f32),
        ],
        compiler_params=pltpu.CompilerParams(vmem_limit_bytes=16 << 20),
        cost_estimate=SMALL,
        name="adjacency",
    )(neighbours.T, embeds)

    pre, aggregate, net_values, *far_sends = call(
        functools.partial(layer_kernel, degree=degree, far=far),
        "layer",
        out("V", f32, nets, feat)
        + out("H", bf16, nets, feat)
        + out("V", bf16, nets, feat)
        + out("V", bf16, slots, feat) * far,
        h(from_halo, agg_sum, embeds, gnn_weight) + v(received, *asked[near:]),
    )
    near_sends = call(
        gather_kernel,
        "gather_near",
        out("V", bf16, slots, feat) * near,
        v(net_values, *asked[:near]),
    )
    partners = [near_sends[0]]
    partners += [permute(near_sends[k], k) for k in range(1, near)]
    partners += [permute(far_sends[k - near], k) for k in range(near, regions)]

    victim, linear_own, slope = call(
        victim_kernel,
        "victims",
        out("H", bf16, regions, slots, feat)
        + out("V", f32, regions, slots, hid)
        + out("H", f32, nets, feat),
        [(rid, "S")] + v(pair_local, net_values) + h(pair_w1) + v(pre),
    )

    groups = [tuple(range(near))] + [(k,) for k in range(near, regions)]
    w2_row = pair_w2.reshape(1, hid)
    lin_grads, backs, sums = [], [], []
    for ks in groups:
        lin_grad, sums_now, *back = call(
            functools.partial(pair_kernel, ks=ks, first=ks is groups[0], last=ks is groups[-1]),
            "pairs",
            out("H", bf16, len(ks), slots, hid)
            + out("V", f32, 8, hid)
            + out("V", bf16, slots, feat) * len(ks),
            [(rid, "S"), (pair_count, "S")]
            + v(targets, linear_own, pair_w1, w2_row)
            + v(*[partners[k] for k in ks])
            + v(*sums),
        )
        lin_grads.append(lin_grad)
        backs += back
        sums = [sums_now]
    returned = [backs[0]] + [permute(backs[k], k) for k in range(1, regions)]

    (local_grad,) = call(
        functools.partial(local_grad_kernel, groups=groups, near=near),
        "local_grads",
        out("V", f32, nets, feat),
        [(rid, "S")]
        + v(pair_local)
        + h(pair_w1)
        + v(*asked[:near], *returned[:near])
        + h(*lin_grads),
        [pltpu.VMEM((regions * slots, feat), bf16)],
    )
    (w1_parts,) = call(
        functools.partial(w1_grad_kernel, groups=groups),
        "w1_grads",
        out("V", bf16, devices, share + 8, hid),
        [(local_grad, "A")] + h(victim) + v(sums[0]) + h(*partners, *lin_grads),
    )
    w1_got = exchange(w1_parts, BOTH)

    total_grad, pre_grad, agg_grad, gnn_part, *backs = call(
        functools.partial(layer_grad_kernel, far=far, peers=peers, degree=degree),
        "layer_grad",
        out("H", f32, nets, feat)
        + out("H", bf16, nets, feat)
        + out("H", bf16, feat, nets)
        + out("V", bf16, 2 * feat, feat)
        + out("V", bf16, halo, feat) * peers,
        [(cid, "S")]
        + h(slope, embeds, aggregate, gnn_weight, from_halo)
        + v(local_grad, *asked[near:], *returned[near:]),
        [pltpu.VMEM((halo_rows, feat), bf16)],
        mib=24,
        flops=10000000000,
    )
    gnn_part, w1_got = lax.optimization_barrier((gnn_part, w1_got))
    gnn_got = exchange(gnn_part.reshape(devices, share, feat), BOTH)
    returned_halo = [backs[0]] + [permute(backs[k], k, "dom") for k in range(1, peers)]

    wide, short = call(
        functools.partial(share_kernel, nets_total=nets * devices),
        "shares",
        out("V", bf16, devices, 2 * share, feat) + out("V", f32, 8, hid),
        v(w1_got, gnn_got) + [(value, "A") for value in returned_halo],
    )
    spread = exchange(wide, BOTH)

    (own_grad,) = call(
        own_grad_kernel,
        "own_grads",
        out("V", f32, nets, feat),
        h(total_grad, pre_grad, gnn_weight, agg_grad, own),
        mib=24,
    )
    (embeds_grad,) = call(
        final_kernel,
        "embeds_grads",
        out("V", bf16, nets, feat),
        [(cid, "S")] + v(short, halo_send, own_grad, *returned_halo),
    )
    w1_grad, gnn_grad = call(
        unpack_kernel,
        "unpack",
        out("H", f32, 2 * feat, hid) + out("H", f32, 2 * feat, feat),
        v(spread),
    )
    return embeds_grad, gnn_grad, w1_grad, short[0], short[1, 0]


def solution(mesh):
    split = P(BOTH, None)
    in_specs = (split, split, split, P(), split, split, split, split, P(), P())
    out_specs = (split, P(), P(), P(), P())
    return jax.shard_map(local, mesh=mesh, in_specs=in_specs, out_specs=out_specs, check_vma=False)
```

time: 341 us -> 138 us (0.40)
  waiting for transfers between devices: 110 us -> 11.8 us
  Pallas kernels: 0 us -> 79.1 us
  matrix products: 76.5 us -> 0 us
  blocking collectives: 41.8 us -> 0 us
  other arithmetic: 39.1 us -> 0 us
  local copies, waits for them, and re-layouts: 29.8 us -> 4.29 us
  starting transfers between devices: 22.1 us -> 40.9 us
  between operations: 19.3 us -> 1.2 us
    psum x1 -> x0, waiting for transfers between devices: 89.9 us -> none  [local(): lax.psum((grad_gnn, grad_w1, grad_w2, sq_local), ('region', 'dom'))]
    pallas_call x0 -> x15, Pallas kernels: none -> 79.1 us  [the longest x14 65.5 us: call(): pl.pallas_call(body, out_shape=[(in_hbm if kind == 'H' else shape)(dims,...]
    dot_general x11 -> x0, matrix products: 76.5 us -> none  [the longest x1 30.3 us: local(): lax.dot_general(adjacency, agg_grad, contract_rows, preferred_element_typ...]
    psum x1 -> x0, blocking collectives: 41.8 us -> none  [local(): total_count = lax.psum(local_count, ('region', 'dom'))]
    scatter-add x2 -> x0, other arithmetic: 28.9 us -> none  [the longest x1 15.3 us: local(): nets_grad.at[asked.reshape(-1)]]
    ppermute x0 -> x16, starting transfers between devices: none -> 19.1 us  [permute(): return lax.ppermute(value, axis, [(i, i ^ k) for i in range(size)])]
    gather x2 -> x0, local copies, waits for them, and re-layouts: 18 us -> none  [the longest x1 9.05 us: local(): nets[asked]]
    all_to_all x5 -> x4, waiting for transfers between devices: 19.8 us -> 5.58 us  [exchange(): return lax.all_to_all(value, axis, split_axis=0, concat_axis=0, tiled=True)]
  transfers between devices with their start and end apart: 6 -> 20, of which waited for: 4 -> 4; matrix products, arithmetic and copies ran while one was open for 10% -> 1% of each run, Pallas kernels for 0% -> 53%
where the time goes in v2:
time: 138 us; the launch traced here: 137 us
  Pallas kernels  79.1 us (57%)
  starting transfers between devices  40.9 us (30%)
  waiting for transfers between devices  11.8 us (9%)
  local copies, waits for them, and re-layouts  4.29 us (3%)
    pallas_call x14, Pallas kernels, call(): pl.pallas_call(body, out_shape=[(in_hbm if kind == 'H' else shape)(dims,...  65.5 us
    all_to_all x4, starting transfers between devices, exchange(): return lax.all_to_all(value, axis, split_axis=0, concat_axis=0, tiled=True)  21.9 us
    ppermute x16, starting transfers between devices, permute(): return lax.ppermute(value, axis, [(i, i ^ k) for i in range(size)])  19.1 us
    pallas_call x1, Pallas kernels, local(): pl.pallas_call(adjacency_kernel, grid=(nets // BLOCK,), in_specs=[pl.Bloc...  13.6 us
    ppermute x16, waiting for transfers between devices, permute(): return lax.ppermute(value, axis, [(i, i ^ k) for i in range(size)])  6.19 us
    all_to_all x4, waiting for transfers between devices, exchange(): return lax.all_to_all(value, axis, split_axis=0, concat_axis=0, tiled=True)  5.58 us
    unnamed x36, local copies, waits for them, and re-layouts  3.2 us
  transfers between devices with their start and end apart: 20, of which 4 were waited for; matrix products, arithmetic and copies ran while one was open for 1% of the time, Pallas kernels for 53%

profile of v2, /device:TPU:0, one launch (start us, length us, event | category | flops | bytes accessed | tf_op | source)
XLA Modules:
  0.0 137.3 jit_solution(17767449822542444300)
XLA Ops:
  0.6 0.0 copy-start
  0.7 0.8 copy-done.13
  1.4 3.4 %halo_gather.1 = bf16[1024,256]{1,0:T(8,128)(2,1)} custom-call(s32[8,128]{1,0:T(8,128)S(1)} %copy-done.13, bf16[2048,256]{1,0:T(8,128)(2,1)} %refs_2_.13), custom_call_target="tpu_custom_call" | custom-call | flops 1 | bytes 1 | tf_op jit(solution)/shard_map/halo_gather/pallas_call | solution.py:429
  4.8 7.3 %all-to-all-start = ((bf16[8,128,256]{2,1,0:T(8,128)(2,1)}), bf16[8,128,256]{2,1,0:T(8,128)(2,1)S(1)}, u32[]{:S(2)}, u32[]{:S(2)}) async-start(bf16[8,128,256]{2,1,0:T(8,128)(2,1)} %bitcast.3), calls=%async_computation | async-start | bytes 1048576 | tf_op jit(solution)/shard_map/all_to_all | solution.py:449
  12.1 0.7 collective-permute-start.1
  12.8 0.9 collective-permute-start
  13.7 0.3 collective-permute-start.2
  14.0 13.6 %adjacency.1 = (bf16[2048,2048]{1,0:T(8,128)(2,1)}, bf16[2048,1024]{1,0:T(8,128)(2,1)}, f32[2048,256]{1,0:T(8,128)}) custom-call(s32[8,2048]{1,0:T(8,128)S(1)} %bitcast.9, bf16[2048,256]{1,0:T(8,128)(2,1)S(1)} %copy-done), custom_call_target="tpu_custom_call" | custom-call | flops 1 | bytes 1 | tf_op jit(solution)/shard_map/adjacency/pallas_call | solution.py:502
  27.7 0.0 copy-start.17
  27.7 0.0 copy-start.12
  27.7 8.7 %layer.1 = (f32[2048,256]{1,0:T(8,128)S(1)}, bf16[2048,256]{1,0:T(8,128)(2,1)}, bf16[2048,256]{1,0:T(8,128)(2,1)S(1)}, bf16[512,256]{1,0:T(8,128)(2,1)S(1)}, bf16[512,256]{1,0:T(8,128)(2,1)S(1)}) custom-call(bf16[2048,1024]{1,0:T(8,128)(2,1)} %get-tuple-element.46.refs_0_.refs_5_, f32[2048,256]{1,0:T(8,128)} %get-tuple-element.47.refs_1_, ...), custom_call_target="tpu_custom_call" | custom-call | flops 1 | bytes 1 | tf_op jit(solution)/shard_map/layer/pallas_call | solution.py:429
  36.4 1.3 gather_near.1
  37.8 0.3 collective-permute-start.3
  38.0 1.4 collective-permute-start.5
  39.4 0.3 collective-permute-start.6
  39.7 8.2 %victims.1 = (bf16[4,512,256]{2,1,0:T(8,128)(2,1)}, f32[4,512,256]{2,1,0:T(8,128)S(1)}, f32[2048,256]{1,0:T(8,128)}) custom-call(s32[1]{0:T(128)} %bitcast.1.refs_0_, s32[4,512]{1,0:T(4,128)S(1)} %copy-done.12, bf16[2048,256]{1,0:T(8,128)(2,1)S(1)} %get-tuple-element.48.refs_2_.refs_0_, bf16[512,256]{1,0:T(8,128)(2,1)} %refs_2_.12, ...), custom_call_target="tpu_custom_call" | custom-call | flops 1 | bytes 1 | tf_op jit(solution)/shard_map/victims/pallas_call | solution.py:429
  47.9 2.5 %pairs.3 = (bf16[2,512,256]{2,1,0:T(8,128)(2,1)}, f32[8,256]{1,0:T(8,128)S(1)}, bf16[512,256]{1,0:T(8,128)(2,1)S(1)}, bf16[512,256]{1,0:T(8,128)(2,1)S(1)}) custom-call(s32[1]{0:T(128)} %bitcast.1.refs_0_, s32[1,4]{1,0:T(1,128)S(1)} %copy-done.15, f32[4,512]{1,0:T(4,128)S(1)} %copy-done.10, f32[4,512,256]{2,1,0:T(8,128)S(1)} %get-tuple-element.52.refs_3_, ...), custom_call_target="tpu_custom_call" | custom-call | flops 1 | bytes 1 | tf_op jit(solution)/shard_map/pairs/pallas_call | solution.py:429
  50.4 0.7 copy-done.6
  51.1 0.5 collective-permute-start.4
  51.6 2.7 %pairs.4 = (bf16[1,512,256]{2,1,0:T(8,128)(2,1)}, f32[8,256]{1,0:T(8,128)S(1)}, bf16[512,256]{1,0:T(8,128)(2,1)}) custom-call(s32[1]{0:T(128)} %bitcast.1.refs_0_, s32[1,4]{1,0:T(1,128)S(1)} %copy-done.15, f32[4,512]{1,0:T(4,128)S(1)} %copy-done.10, f32[4,512,256]{2,1,0:T(8,128)S(1)} %get-tuple-element.52.refs_3_, bf16[512,256]{1,0:T(8,128)(2,1)S(1)} %copy-done.1, ...), custom_call_target="tpu_custom_call" | custom-call | flops 1 | bytes 1 | tf_op jit(solution)/shard_map/pairs/pallas_call | solution.py:429
  54.4 2.9 %pairs.5 = (bf16[1,512,256]{2,1,0:T(8,128)(2,1)}, f32[8,256]{1,0:T(8,128)S(1)}, bf16[512,256]{1,0:T(8,128)(2,1)}) custom-call(s32[1]{0:T(128)} %bitcast.1.refs_0_, s32[1,4]{1,0:T(1,128)S(1)} %copy-done.15, f32[4,512]{1,0:T(4,128)S(1)} %copy-done.10, f32[4,512,256]{2,1,0:T(8,128)S(1)} %get-tuple-element.52.refs_3_, bf16[512,256]{1,0:T(8,128)(2,1)S(1)} %copy-done.1, ...), custom_call_target="tpu_custom_call" | custom-call | flops 1 | bytes 1 | tf_op jit(solution)/shard_map/pairs/pallas_call | solution.py:429
  57.3 1.2 collective-permute-start.8
  58.5 0.5 collective-permute-start.7
  59.0 0.7 copy-done.8
  59.7 0.9 copy-done.9
  60.7 6.0 %local_grads.1.refs_6_.refs_0_ = f32[2048,256]{1,0:T(8,128)S(1)} custom-call(s32[1]{0:T(128)} %bitcast.1.refs_0_, s32[4,512]{1,0:T(4,128)S(1)} %copy-done.12, bf16[512,256]{1,0:T(8,128)(2,1)} %refs_2_.12, s32[1,512]{1,0:T(1,128)S(1)} %get-tuple-element.90.refs_1_.refs_3_, s32[1,512]{1,0:T(1,128)S(1)} %collective-permute-done.2.refs_2_.refs_4_, ...), custom_call_target="tpu_custom_call" | custom-call | flops 1 | bytes 1 | tf_op jit(solution)/shard_map/local_grads/pallas_call | solution.py:429
  66.7 4.8 %w1_grads.1 = bf16[32,24,256]{2,1,0:T(8,128)(2,1)} custom-call(f32[2048,256]{1,0:T(8,128)S(1)} %local_grads.1.refs_6_.refs_0_, bf16[4,512,256]{2,1,0:T(8,128)(2,1)} %get-tuple-element.67.refs_1_, f32[8,256]{1,0:T(8,128)S(1)} %get-tuple-element.68.refs_2_, bf16[512,256]{1,0:T(8,128)(2,1)} %copy-done.2, bf16[512,256]{1,0:T(8,128)(2,1)} %copy-done.3, ...), custom_call_target="tpu_custom_call" | custom-call | flops 1 | bytes 1 | tf_op jit(solution)/shard_map/w1_grads/pallas_call | solution.py:429
  71.6 6.0 %all-to-all-start.1 = ((bf16[32,24,256]{2,1,0:T(8,128)(2,1)}), bf16[32,24,256]{2,1,0:T(8,128)(2,1)S(1)}, u32[]{:S(2)}, u32[]{:S(2)}) async-start(bf16[32,24,256]{2,1,0:T(8,128)(2,1)} %w1_grads.1), calls=%async_computation.1 | async-start | bytes 786432 | tf_op jit(solution)/shard_map/all_to_all | solution.py:449
  77.6 11.8 %layer_grad.1 = (f32[2048,256]{1,0:T(8,128)}, bf16[2048,256]{1,0:T(8,128)(2,1)}, bf16[256,2048]{1,0:T(8,128)(2,1)}, bf16[512,256]{1,0:T(8,128)(2,1)}, bf16[128,2...) custom-call(s32[1]{0:T(128)} %bitcast.refs_0_, ...), custom_call_target="tpu_custom_call" | custom-call | flops 10000000000 | bytes 1 | tf_op jit(solution)/shard_map/layer_grad/pallas_call | solution.py:429
  89.4 1.7 %all-to-all-done.1.refs_0_ = bf16[32,24,256]{2,1,0:T(8,128)(2,1)S(1)} async-done(((bf16[32,24,256]{2,1,0:T(8,128)(2,1)}), bf16[32,24,256]{2,1,0:T(8,128)(2,1)S(1)}, u32[]{:S(2)}, u32[]{:S(2)}) %all-to-all-start.1) | async-done | bytes 393248 | tf_op jit(solution)/shard_map/all_to_all | solution.py:449
  91.2 4.1 %all-to-all-start.2 = ((bf16[32,16,256]{2,1,0:T(8,128)(2,1)}), bf16[32,16,256]{2,1,0:T(8,128)(2,1)S(1)}, u32[]{:S(2)}, u32[]{:S(2)}) async-start(bf16[32,16,256]{2,1,0:T(8,128)(2,1)} %bitcast.5), calls=%async_computation.2 | async-start | bytes 524288 | tf_op jit(solution)/shard_map/all_to_all | solution.py:449
  95.3 1.8 %collective-permute-start.9 = (bf16[128,256]{1,0:T(8,128)(2,1)S(1)}, bf16[128,256]{1,0:T(8,128)(2,1)S(1)}, u32[]{:S(2)}, u32[]{:S(2)}) collective-permute-start(bf16[128,256]{1,0:T(8,128)(2,1)S(1)} %get-tuple-element.72), channel_id=1, source_target_pairs={{0,1},{1,0},{2,3},{3,2},{4,5},{5,4},{6,7},{7,6},{8,9},{9,8},{10,11... | collective-permute-start | bytes 196616 | tf_op jit(solution)/shard_map/ppermute | solution.py:480
  97.1 1.5 %collective-permute-start.10 = (bf16[128,256]{1,0:T(8,128)(2,1)S(1)}, bf16[128,256]{1,0:T(8,128)(2,1)S(1)}, u32[]{:S(2)}, u32[]{:S(2)}) collective-permute-start(bf16[128,256]{1,0:T(8,128)(2,1)S(1)} %get-tuple-element.73), channel_id=1, source_target_pairs={{0,2},{1,3},{2,0},{3,1},{4,6},{5,7},{6,4},{7,5},{8,10},{9,11},{10,... | collective-permute-start | bytes 196616 | tf_op jit(solution)/shard_map/ppermute | solution.py:480
  98.6 0.3 collective-permute-start.11
  98.8 2.7 %collective-permute-start.12 = (bf16[128,256]{1,0:T(8,128)(2,1)S(1)}, bf16[128,256]{1,0:T(8,128)(2,1)S(1)}, u32[]{:S(2)}, u32[]{:S(2)}) collective-permute-start(bf16[128,256]{1,0:T(8,128)(2,1)S(1)} %get-tuple-element.75), channel_id=1, source_target_pairs={{0,4},{1,5},{2,6},{3,7},{4,0},{5,1},{6,2},{7,3},{8,12},{9,13},{10,... | collective-permute-start | bytes 196616 | tf_op jit(solution)/shard_map/ppermute | solution.py:480
  101.5 1.5 %collective-permute-start.13 = (bf16[128,256]{1,0:T(8,128)(2,1)S(1)}, bf16[128,256]{1,0:T(8,128)(2,1)S(1)}, u32[]{:S(2)}, u32[]{:S(2)}) collective-permute-start(bf16[128,256]{1,0:T(8,128)(2,1)S(1)} %get-tuple-element.76), channel_id=1, source_target_pairs={{0,5},{1,4},{2,7},{3,6},{4,1},{5,0},{6,3},{7,2},{8,13},{9,12},{10,... | collective-permute-start | bytes 196616 | tf_op jit(solution)/shard_map/ppermute | solution.py:480
  103.0 3.3 %collective-permute-start.14 = (bf16[128,256]{1,0:T(8,128)(2,1)S(1)}, bf16[128,256]{1,0:T(8,128)(2,1)S(1)}, u32[]{:S(2)}, u32[]{:S(2)}) collective-permute-start(bf16[128,256]{1,0:T(8,128)(2,1)S(1)} %get-tuple-element.77), channel_id=1, source_target_pairs={{0,6},{1,7},{2,4},{3,5},{4,2},{5,3},{6,0},{7,1},{8,14},{9,15},{10,... | collective-permute-start | bytes 196616 | tf_op jit(solution)/shard_map/ppermute | solution.py:480
  106.3 2.0 %collective-permute-start.15 = (bf16[128,256]{1,0:T(8,128)(2,1)S(1)}, bf16[128,256]{1,0:T(8,128)(2,1)S(1)}, u32[]{:S(2)}, u32[]{:S(2)}) collective-permute-start(bf16[128,256]{1,0:T(8,128)(2,1)S(1)} %get-tuple-element.78), channel_id=1, source_target_pairs={{0,7},{1,6},{2,5},{3,4},{4,3},{5,2},{6,1},{7,0},{8,15},{9,14},{10,... | collective-permute-start | bytes 196616 | tf_op jit(solution)/shard_map/ppermute | solution.py:480
  108.3 0.1 collective-permute-done.11.refs_5_.refs_7_
  108.4 6.1 %collective-permute-done.13.refs_7_.refs_9_ = bf16[128,256]{1,0:T(8,128)(2,1)S(1)} collective-permute-done((bf16[128,256]{1,0:T(8,128)(2,1)S(1)}, bf16[128,256]{1,0:T(8,128)(2,1)S(1)}, u32[]{:S(2)}, u32[]{:S(2)}) %collective-permute-start.13) | collective-permute-done | bytes 65568 | tf_op jit(solution)/shard_map/ppermute | solution.py:480
  114.5 0.9 shares.1
  115.4 4.4 %all-to-all-start.3 = ((bf16[32,32,256]{2,1,0:T(8,128)(2,1)}), bf16[32,32,256]{2,1,0:T(8,128)(2,1)S(1)}, u32[]{:S(2)}, u32[]{:S(2)}) async-start(bf16[32,32,256]{2,1,0:T(8,128)(2,1)} %get-tuple-element.84), calls=%async_computation.3 | async-start | bytes 1048576 | tf_op jit(solution)/shard_map/all_to_all | solution.py:449
  119.9 8.9 %own_grads.1.refs_3_ = f32[2048,256]{1,0:T(8,128)S(1)} custom-call(f32[2048,256]{1,0:T(8,128)} %get-tuple-element.80.refs_0_, bf16[2048,256]{1,0:T(8,128)(2,1)} %get-tuple-element.81.refs_1_, bf16[512,256]{1,0:T(8,128)(2,1)} %refs_2_.14, bf16[256,2048]{1,0:T(8,128)(2,1)} %get-tuple-element.82.refs_3_, bf16[2048,2048]{1,0:T(8,128)(2,1)} %get-tuple-element.83.refs_4_), custom_call_target="tpu_custom_call" | custom-call | flops 1 | bytes 1 | tf_op jit(solution)/shard_map/own_grads/pallas_call | solution.py:429
  128.8 2.2 %embeds_grads.1 = bf16[2048,256]{1,0:T(8,128)(2,1)} custom-call(s32[1]{0:T(128)} %bitcast.refs_0_, f32[8,256]{1,0:T(8,128)S(1)} %get-tuple-element.79.refs_1_, s32[8,128]{1,0:T(8,128)S(1)} %copy-done.14, f32[2048,256]{1,0:T(8,128)S(1)} %own_grads.1.refs_3_, bf16[128,256]{1,0:T(8,128)(2,1)S(1)} %get-tuple-element.71.refs_2_.refs_4_, ...), custom_call_target="tpu_custom_call" | custom-call | flops 1 | bytes 1 | tf_op jit(solution)/shard_map/embeds_grads/pallas_call | solution.py:429
  131.1 0.5 slice.7
  131.6 0.6 slice.6
  132.1 3.8 %all-to-all-done.3.refs_0_ = bf16[32,32,256]{2,1,0:T(8,128)(2,1)S(1)} async-done(((bf16[32,32,256]{2,1,0:T(8,128)(2,1)}), bf16[32,32,256]{2,1,0:T(8,128)(2,1)S(1)}, u32[]{:S(2)}, u32[]{:S(2)}) %all-to-all-start.3) | async-done | bytes 524320 | tf_op jit(solution)/shard_map/all_to_all | solution.py:449
  136.0 1.1 unpack.1
  (47 shorter events, 0.1 us)
Async XLA Ops:
  0.6 13.4 %copy-start = (bf16[2048,256]{1,0:T(8,128)(2,1)S(1)}, bf16[2048,256]{1,0:T(8,128)(2,1)}, u32[]{:S(2)}) copy-start(bf16[2048,256]{1,0:T(8,128)(2,1)} %refs_2_.13) | copy-start | bytes 3145732
  0.6 13.4 %copy-start.11 = (s32[2048,8]{0,1:T(8,128)S(1)}, s32[2048,8]{0,1:T(8,128)}, u32[]{:S(2)}) copy-start(s32[2048,8]{0,1:T(8,128)} %param.11) | copy-start | bytes 196612
  0.7 0.8 copy-start.13
  1.4 10.7 %copy-start.16 = (s32[4,512]{1,0:T(4,128)S(1)}, s32[4,512]{1,0:T(4,128)}, u32[]{:S(2)}) copy-start(s32[4,512]{1,0:T(4,128)} %param.15) | copy-start | bytes 24580
  4.8 22.9 %all-to-all-start = ((bf16[8,128,256]{2,1,0:T(8,128)(2,1)}), bf16[8,128,256]{2,1,0:T(8,128)(2,1)S(1)}, u32[]{:S(2)}, u32[]{:S(2)}) async-start(bf16[8,128,256]{2,1,0:T(8,128)(2,1)} %bitcast.3), calls=%async_computation | async-start | bytes 1048576 | tf_op jit(solution)/shard_map/all_to_all | solution.py:449
  12.1 15.5 %collective-permute-start.1 = (s32[1,512]{1,0:T(1,128)S(1)}, s32[1,512]{1,0:T(1,128)S(1)}, u32[]{:S(2)}, u32[]{:S(2)}) collective-permute-start(s32[1,512]{1,0:T(1,128)S(1)} %get-tuple-element.88), channel_id=1, source_target_pairs={{0,24},{8,16},{16,8},{24,0},{1,25},{9,17},{17,9},{25,1},{2,26},{10... | collective-permute-start | bytes 6152 | tf_op jit(solution)/shard_map/ppermute | solution.py:480
  12.8 14.8 %collective-permute-start = (s32[1,512]{1,0:T(1,128)S(1)}, s32[1,512]{1,0:T(1,128)S(1)}, u32[]{:S(2)}, u32[]{:S(2)}) collective-permute-start(s32[1,512]{1,0:T(1,128)S(1)} %get-tuple-element.89), channel_id=1, source_target_pairs={{0,16},{8,24},{16,0},{24,8},{1,17},{9,25},{17,1},{25,9},{2,18},{10... | collective-permute-start | bytes 6152 | tf_op jit(solution)/shard_map/ppermute | solution.py:480
  13.7 22.7 %collective-permute-start.2 = (s32[1,512]{1,0:T(1,128)S(1)}, s32[1,512]{1,0:T(1,128)S(1)}, u32[]{:S(2)}, u32[]{:S(2)}) collective-permute-start(s32[1,512]{1,0:T(1,128)S(1)} %get-tuple-element.87), channel_id=1, source_target_pairs={{0,8},{8,0},{16,24},{24,16},{1,9},{9,1},{17,25},{25,17},{2,10},{10... | collective-permute-start | bytes 6152 | tf_op jit(solution)/shard_map/ppermute | solution.py:480
  27.7 12.0 %copy-start.17 = (bf16[256]{0:T(256)(128)(2,1)S(1)}, bf16[256]{0:T(256)(128)(2,1)}, u32[]{:S(2)}) copy-start(bf16[256]{0:T(256)(128)(2,1)} %param.19) | copy-start | bytes 1540
  27.7 12.0 %copy-start.12 = (s32[4,512]{1,0:T(4,128)S(1)}, s32[4,512]{1,0:T(4,128)}, u32[]{:S(2)}) copy-start(s32[4,512]{1,0:T(4,128)} %refs_1_.11) | copy-start | bytes 24580
  36.4 11.5 %copy-start.1 = (bf16[512,256]{1,0:T(8,128)(2,1)S(1)}, bf16[512,256]{1,0:T(8,128)(2,1)}, u32[]{:S(2)}) copy-start(bf16[512,256]{1,0:T(8,128)(2,1)} %refs_2_.12) | copy-start | bytes 786436
  36.4 11.5 %copy-start.10 = (f32[4,512]{1,0:T(4,128)S(1)}, f32[4,512]{1,0:T(4,128)}, u32[]{:S(2)}) copy-start(f32[4,512]{1,0:T(4,128)} %refs_2_.11) | copy-start | bytes 24580
  36.4 11.5 %copy-start.15 = (s32[1,4]{1,0:T(1,128)S(1)}, s32[1,4]{1,0:T(1,128)}, u32[]{:S(2)}) copy-start(s32[1,4]{1,0:T(1,128)} %refs_1_.10) | copy-start | bytes 52
  37.8 12.7 %copy-start.2 = (bf16[512,256]{1,0:T(8,128)(2,1)}, bf16[512,256]{1,0:T(8,128)(2,1)S(1)}, u32[]{:S(2)}) copy-start(bf16[512,256]{1,0:T(8,128)(2,1)S(1)} %get-tuple-element.53.refs_6_.refs_3_) | copy-start | bytes 786436
  37.8 10.1 %collective-permute-start.3 = (bf16[512,256]{1,0:T(8,128)(2,1)S(1)}, bf16[512,256]{1,0:T(8,128)(2,1)S(1)}, u32[]{:S(2)}, u32[]{:S(2)}) collective-permute-start(bf16[512,256]{1,0:T(8,128)(2,1)S(1)} %get-tuple-element.54), channel_id=1, source_target_pairs={{0,8},{8,0},{16,24},{24,16},{1,9},{9,1},{17,25},{25,17},{2,10},{10... | collective-permute-start | bytes 786440 | tf_op jit(solution)/shard_map/ppermute | solution.py:480
  38.0 13.6 %collective-permute-start.5 = (bf16[512,256]{1,0:T(8,128)(2,1)S(1)}, bf16[512,256]{1,0:T(8,128)(2,1)S(1)}, u32[]{:S(2)}, u32[]{:S(2)}) collective-permute-start(bf16[512,256]{1,0:T(8,128)(2,1)S(1)} %get-tuple-element.58), channel_id=1, source_target_pairs={{0,16},{8,24},{16,0},{24,8},{1,17},{9,25},{17,1},{25,9},{2,18},{10... | collective-permute-start | bytes 786440 | tf_op jit(solution)/shard_map/ppermute | solution.py:480
  39.4 15.0 %collective-permute-start.6 = (bf16[512,256]{1,0:T(8,128)(2,1)S(1)}, bf16[512,256]{1,0:T(8,128)(2,1)S(1)}, u32[]{:S(2)}, u32[]{:S(2)}) collective-permute-start(bf16[512,256]{1,0:T(8,128)(2,1)S(1)} %get-tuple-element.61), channel_id=1, source_target_pairs={{0,24},{8,16},{16,8},{24,0},{1,25},{9,17},{17,9},{25,1},{2,26},{10... | collective-permute-start | bytes 786440 | tf_op jit(solution)/shard_map/ppermute | solution.py:480
  47.9 6.5 %copy-start.3 = (bf16[512,256]{1,0:T(8,128)(2,1)}, bf16[512,256]{1,0:T(8,128)(2,1)S(1)}, u32[]{:S(2)}) copy-start(bf16[512,256]{1,0:T(8,128)(2,1)S(1)} %collective-permute-done.3.refs_7_.refs_4_) | copy-start | bytes 786436
  50.4 0.7 copy-start.6
  51.1 7.9 %collective-permute-start.4 = (bf16[512,256]{1,0:T(8,128)(2,1)S(1)}, bf16[512,256]{1,0:T(8,128)(2,1)S(1)}, u32[]{:S(2)}, u32[]{:S(2)}) collective-permute-start(bf16[512,256]{1,0:T(8,128)(2,1)S(1)} %get-tuple-element.56), channel_id=1, source_target_pairs={{0,8},{8,0},{16,24},{24,16},{1,9},{9,1},{17,25},{25,17},{2,10},{10... | collective-permute-start | bytes 786440 | tf_op jit(solution)/shard_map/ppermute | solution.py:480
  51.6 5.7 %copy-start.4 = (bf16[512,256]{1,0:T(8,128)(2,1)}, bf16[512,256]{1,0:T(8,128)(2,1)S(1)}, u32[]{:S(2)}) copy-start(bf16[512,256]{1,0:T(8,128)(2,1)S(1)} %collective-permute-done.5.refs_6_.refs_5_) | copy-start | bytes 786436
  51.6 8.1 %copy-start.7 = (bf16[512,256]{1,0:T(8,128)(2,1)S(1)}, bf16[512,256]{1,0:T(8,128)(2,1)}, u32[]{:S(2)}) copy-start(bf16[512,256]{1,0:T(8,128)(2,1)} %copy-done.6) | copy-start | bytes 786436
  54.4 12.4 %copy-start.5 = (bf16[512,256]{1,0:T(8,128)(2,1)}, bf16[512,256]{1,0:T(8,128)(2,1)S(1)}, u32[]{:S(2)}) copy-start(bf16[512,256]{1,0:T(8,128)(2,1)S(1)} %collective-permute-done.6.refs_6_) | copy-start | bytes 786436
  57.3 20.3 %collective-permute-start.8 = (bf16[512,256]{1,0:T(8,128)(2,1)}, bf16[512,256]{1,0:T(8,128)(2,1)S(1)}, u32[]{:S(2)}, u32[]{:S(2)}) collective-permute-start(bf16[512,256]{1,0:T(8,128)(2,1)} %get-tuple-element.65), channel_id=1, source_target_pairs={{0,24},{8,16},{16,8},{24,0},{1,25},{9,17},{17,9},{25,1},{2,26},{10... | collective-permute-start | bytes 786440 | tf_op jit(solution)/shard_map/ppermute | solution.py:480
  58.5 19.1 %collective-permute-start.7 = (bf16[512,256]{1,0:T(8,128)(2,1)}, bf16[512,256]{1,0:T(8,128)(2,1)}, u32[]{:S(2)}, u32[]{:S(2)}) collective-permute-start(bf16[512,256]{1,0:T(8,128)(2,1)} %get-tuple-element.64), channel_id=1, source_target_pairs={{0,16},{8,24},{16,0},{24,8},{1,17},{9,25},{17,1},{25,9},{2,18},{10... | collective-permute-start | bytes 786440 | tf_op jit(solution)/shard_map/ppermute | solution.py:480
  59.0 0.7 copy-start.8
  59.7 1.0 copy-start.9
  71.6 19.6 %all-to-all-start.1 = ((bf16[32,24,256]{2,1,0:T(8,128)(2,1)}), bf16[32,24,256]{2,1,0:T(8,128)(2,1)S(1)}, u32[]{:S(2)}, u32[]{:S(2)}) async-start(bf16[32,24,256]{2,1,0:T(8,128)(2,1)} %w1_grads.1), calls=%async_computation.1 | async-start | bytes 786432 | tf_op jit(solution)/shard_map/all_to_all | solution.py:449
  91.2 23.3 %all-to-all-start.2 = ((bf16[32,16,256]{2,1,0:T(8,128)(2,1)}), bf16[32,16,256]{2,1,0:T(8,128)(2,1)S(1)}, u32[]{:S(2)}, u32[]{:S(2)}) async-start(bf16[32,16,256]{2,1,0:T(8,128)(2,1)} %bitcast.5), calls=%async_computation.2 | async-start | bytes 524288 | tf_op jit(solution)/shard_map/all_to_all | solution.py:449
  95.3 7.7 %collective-permute-start.9 = (bf16[128,256]{1,0:T(8,128)(2,1)S(1)}, bf16[128,256]{1,0:T(8,128)(2,1)S(1)}, u32[]{:S(2)}, u32[]{:S(2)}) collective-permute-start(bf16[128,256]{1,0:T(8,128)(2,1)S(1)} %get-tuple-element.72), channel_id=1, source_target_pairs={{0,1},{1,0},{2,3},{3,2},{4,5},{5,4},{6,7},{7,6},{8,9},{9,8},{10,11... | collective-permute-start | bytes 196616 | tf_op jit(solution)/shard_map/ppermute | solution.py:480
  97.1 9.2 %collective-permute-start.10 = (bf16[128,256]{1,0:T(8,128)(2,1)S(1)}, bf16[128,256]{1,0:T(8,128)(2,1)S(1)}, u32[]{:S(2)}, u32[]{:S(2)}) collective-permute-start(bf16[128,256]{1,0:T(8,128)(2,1)S(1)} %get-tuple-element.73), channel_id=1, source_target_pairs={{0,2},{1,3},{2,0},{3,1},{4,6},{5,7},{6,4},{7,5},{8,10},{9,11},{10,... | collective-permute-start | bytes 196616 | tf_op jit(solution)/shard_map/ppermute | solution.py:480
  98.6 9.8 %collective-permute-start.11 = (bf16[128,256]{1,0:T(8,128)(2,1)S(1)}, bf16[128,256]{1,0:T(8,128)(2,1)S(1)}, u32[]{:S(2)}, u32[]{:S(2)}) collective-permute-start(bf16[128,256]{1,0:T(8,128)(2,1)S(1)} %get-tuple-element.74), channel_id=1, source_target_pairs={{0,3},{1,2},{2,1},{3,0},{4,7},{5,6},{6,5},{7,4},{8,11},{9,10},{10,... | collective-permute-start | bytes 196616 | tf_op jit(solution)/shard_map/ppermute | solution.py:480
  98.8 9.6 %collective-permute-start.12 = (bf16[128,256]{1,0:T(8,128)(2,1)S(1)}, bf16[128,256]{1,0:T(8,128)(2,1)S(1)}, u32[]{:S(2)}, u32[]{:S(2)}) collective-permute-start(bf16[128,256]{1,0:T(8,128)(2,1)S(1)} %get-tuple-element.75), channel_id=1, source_target_pairs={{0,4},{1,5},{2,6},{3,7},{4,0},{5,1},{6,2},{7,3},{8,12},{9,13},{10,... | collective-permute-start | bytes 196616 | tf_op jit(solution)/shard_map/ppermute | solution.py:480
  101.5 13.0 %collective-permute-start.13 = (bf16[128,256]{1,0:T(8,128)(2,1)S(1)}, bf16[128,256]{1,0:T(8,128)(2,1)S(1)}, u32[]{:S(2)}, u32[]{:S(2)}) collective-permute-start(bf16[128,256]{1,0:T(8,128)(2,1)S(1)} %get-tuple-element.76), channel_id=1, source_target_pairs={{0,5},{1,4},{2,7},{3,6},{4,1},{5,0},{6,3},{7,2},{8,13},{9,12},{10,... | collective-permute-start | bytes 196616 | tf_op jit(solution)/shard_map/ppermute | solution.py:480
  103.0 11.5 %collective-permute-start.14 = (bf16[128,256]{1,0:T(8,128)(2,1)S(1)}, bf16[128,256]{1,0:T(8,128)(2,1)S(1)}, u32[]{:S(2)}, u32[]{:S(2)}) collective-permute-start(bf16[128,256]{1,0:T(8,128)(2,1)S(1)} %get-tuple-element.77), channel_id=1, source_target_pairs={{0,6},{1,7},{2,4},{3,5},{4,2},{5,3},{6,0},{7,1},{8,14},{9,15},{10,... | collective-permute-start | bytes 196616 | tf_op jit(solution)/shard_map/ppermute | solution.py:480
  106.3 8.2 %collective-permute-start.15 = (bf16[128,256]{1,0:T(8,128)(2,1)S(1)}, bf16[128,256]{1,0:T(8,128)(2,1)S(1)}, u32[]{:S(2)}, u32[]{:S(2)}) collective-permute-start(bf16[128,256]{1,0:T(8,128)(2,1)S(1)} %get-tuple-element.78), channel_id=1, source_target_pairs={{0,7},{1,6},{2,5},{3,4},{4,3},{5,2},{6,1},{7,0},{8,15},{9,14},{10,... | collective-permute-start | bytes 196616 | tf_op jit(solution)/shard_map/ppermute | solution.py:480
  115.4 20.5 %all-to-all-start.3 = ((bf16[32,32,256]{2,1,0:T(8,128)(2,1)}), bf16[32,32,256]{2,1,0:T(8,128)(2,1)S(1)}, u32[]{:S(2)}, u32[]{:S(2)}) async-start(bf16[32,32,256]{2,1,0:T(8,128)(2,1)} %get-tuple-element.84), calls=%async_computation.3 | async-start | bytes 1048576 | tf_op jit(solution)/shard_map/all_to_all | solution.py:449
  119.9 8.9 %copy-start.14 = (s32[8,128]{1,0:T(8,128)S(1)}, s32[8,128]{1,0:T(8,128)}, u32[]{:S(2)}) copy-start(s32[8,128]{1,0:T(8,128)} %refs_2_.15) | copy-start | bytes 12292

commit v3 on v2

--- a/solution.py
+++ b/solution.py
@@ -1,4 +1,5 @@
 import functools
+import math
 
 import jax
 import jax.numpy as jnp
@@ -14,6 +15,9 @@
 gelu_coef = 0.7978845608
 BOTH = ("region", "dom")
 BLOCK = 256
+VICTIMS = 10**10
+PAIRS = 2 * 10**9
+FINAL = 2 * 10**10
 STEP = 512
 TT = (((0,), (0,)), ((), ()))
 NT = (((1,), (1,)), ((), ()))
@@ -70,39 +74,35 @@
         out_ref[p * halo : (p + 1) * halo, :] = mm(hot, embeds_ref[...]).astype(bf16)
 
 
-def adjacency_kernel(neigh_ref, embeds_ref, own_ref, halo_ref, sum_ref):
-    degree = neigh_ref.shape[0]
-    rows, nets = own_ref.shape
-    listed = [neigh_ref[c : c + 1, :] for c in range(degree)]
-    columns, counts = [], []
-    for c in range(degree):
-        count = jnp.ones_like(listed[c])
-        seen = None
-        for e in range(degree):
-            if e != c:
-                same = listed[e] == listed[c]
-                if e > c:
-                    count = count + same.astype(i32)
-                else:
-                    seen = same if seen is None else (seen | same)
-        index = listed[c] if seen is None else jnp.where(seen, -1, listed[c])
-        columns.append(column_of(index).astype(i16))
-        counts.append(column_of(count).astype(f32).astype(bf16))
-    lane = lax.broadcasted_iota(i32, (rows, 128), 1).astype(i16)
-    zero = jnp.zeros((rows, 128), bf16)
-
-    def tile(at):
-        acc = zero
-        here = lane + jnp.int16(at)
+def adjacency_kernel(neigh_ref, embeds_ref, own_ref, halo_ref, sum_ref, across_ref):
+    degree, rows = neigh_ref.shape
+    nets, halo_rows = own_ref.shape[1], halo_ref.shape[1]
+
+    @pl.when(pl.program_id(0) == 0)
+    def turn():
+        across_ref[...] = embeds_ref[...].T
+
+    listed = neigh_ref[...]
+    low = listed & 127
+    high = listed >> 7
+    bit = jnp.left_shift(jnp.ones_like(listed), (high & 7) * 4)
+    words = -(-(nets + halo_rows) // 1024)
+    parts = [jnp.where((high >> 3) == k, bit, 0) for k in range(words)]
+    for first in range(0, 128, 32):
+        sub = lax.broadcasted_iota(i32, (32, rows), 0) + first
+        packed = [jnp.zeros((32, rows), i32) for _ in range(words)]
         for c in range(degree):
-            acc = jnp.where(columns[c] == here, counts[c], acc)
-        return acc
-
-    for at in range(0, nets, 128):
-        own_ref[:, at : at + 128] = tile(at)
-    for at in range(0, halo_ref.shape[1], 128):
-        halo_ref[:, at : at + 128] = tile(nets + at)
-    sum_ref[...] = mm(own_ref[...], embeds_ref[...])
+            same = sub == low[c : c + 1, :]
+            for k in range(words):
+                packed[k] = packed[k] + jnp.where(same, parts[k][c : c + 1, :], 0)
+        for at in range(0, nets + halo_rows, 128):
+            j = at // 128
+            counts = ((packed[j // 8] >> (4 * (j % 8))) & 15).astype(f32).astype(bf16)
+            if at < nets:
+                own_ref[0, at + first : at + first + 32, :] = counts
+            else:
+                halo_ref[0, at - nets + first : at - nets + first + 32, :] = counts
+    sum_ref[...] = mm(across_ref[...], own_ref[0]).T
 
 
 def layer_kernel(halo_ref, sum_ref, embeds_ref, gnn_ref, received_ref, *refs, degree, far):
@@ -112,9 +112,10 @@
         refs[far + 3 :],
     )
     nets, feat = nets_ref.shape
+    across = received_ref[...].T
     for at in range(0, nets, STEP):
         rows = pl.ds(at, STEP)
-        total = sum_ref[rows, :] + mm(halo_ref[rows, :], received_ref[...])
+        total = sum_ref[rows, :] + mm(across, halo_ref[at // STEP]).T
         agg = (total * (1.0 / degree)).astype(bf16)
         agg_ref[rows, :] = agg
         agg_ref.flush(at + STEP)
@@ -126,29 +127,33 @@
         send_ref[...] = mm(hot, nets_ref[...]).astype(bf16)
 
 
-def gather_kernel(nets_ref, *refs):
-    some = len(refs) // 2
-    for asked_ref, out_ref in zip(refs[:some], refs[some:], strict=True):
-        hot = onehot_rows(asked_ref[...], nets_ref.shape[0])
-        out_ref[...] = mm(hot, nets_ref[...]).astype(bf16)
-
-
-def victim_kernel(rid_ref, local_ref, nets_ref, w1_ref, pre_ref, victim_ref, linear_ref, slope_ref):
+def victim_kernel(
+    rid_ref, local_ref, nets_ref, w1_ref, pre_ref, *refs, near
+):
+    asked_refs, (victim_ref, linear_ref, slope_ref), near_refs = (
+        refs[:near],
+        refs[near : near + 3],
+        refs[near + 3 :],
+    )
     regions, slots = local_ref.shape
     nets, feat = nets_ref.shape
     me = rid_ref[0]
+    for asked_ref, near_ref in zip(asked_refs, near_refs, strict=True):
+        hot = onehot_rows(asked_ref[...], nets)
+        near_ref[...] = mm(hot, nets_ref[...]).astype(bf16)
     for k in range(regions):
         hot = onehot_rows(local_ref[pl.ds(me ^ k, 1), :], nets)
         victim = mm(hot, nets_ref[...]).astype(bf16)
         victim_ref[k] = victim
-        victim_ref.flush(k + 1)
         linear_ref[k] = mm(victim, w1_ref[:feat, :])
+    victim_ref.flush()
     for at in range(0, nets, STEP):
         rows = pl.ds(at, STEP)
         pre = pre_ref[rows, :]
         square = pre * pre
-        slope_ref[rows, :] = slope_of(pre, square, gelu_inner(pre, square))
-        slope_ref.flush(at + STEP)
+        slope_ref[rows, :] = slope_of(pre, square, gelu_inner(pre, square)).astype(bf16)
+        if at + STEP == nets // 2:
+            slope_ref.flush(nets // 2)
 
 
 def pair_kernel(rid_ref, count_ref, target_ref, linear_ref, w1_ref, w2_ref, *refs, ks, first, last):
@@ -181,7 +186,11 @@
         lin_grad = (residual * w2_row * slope_of(linear, square, inner)).astype(bf16)
         lin_grad_ref[at] = lin_grad
         lin_grad_ref.flush(at + 1)
-        back_refs[at][...] = mm_dims(lin_grad, w1_ref[feat:, :], NT).astype(bf16)
+        back = mm_dims(lin_grad, w1_ref[feat:, :], NT).astype(bf16)
+        pieces = len(back_refs) // some
+        rows = slots // pieces
+        for piece in range(pieces):
+            back_refs[at * pieces + piece][...] = back[piece * rows : (piece + 1) * rows]
     if not last:
         sums_ref[...] = jnp.concatenate([w2_sum, sq_sum, jnp.zeros((6, hid), f32)], 0)
     else:
@@ -196,42 +205,44 @@
         sums_ref[...] = jnp.concatenate(parts + [jnp.zeros((2, hid), f32)], 0)
 
 
-def w1_grad_kernel(after_ref, victim_ref, sums_ref, *refs, groups):
-    regions, _, feat = victim_ref.shape
-    partner_refs, lin_refs, out_ref = refs[:regions], refs[regions:-1], refs[-1]
-    devices, rows, hid = out_ref.shape
+def local_grad_kernel(rid_ref, local_ref, w1_ref, sums_ref, *refs, groups, near):
+    regions, slots = local_ref.shape
+    asked_refs, refs = refs[:near], refs[near:]
+    near_refs, refs = refs[: 2 * near], refs[2 * near :]
+    near_rows = [
+        jnp.concatenate([near_refs[2 * k][...], near_refs[2 * k + 1][...]], 0) for k in range(near)
+    ]
+    lin_refs, refs = refs[: len(groups)], refs[len(groups) :]
+    partner_refs, (victim_ref, grad_ref, out_ref, vg_ref) = refs[:regions], refs[regions:]
+    nets, feat = grad_ref.shape
+    devices, _, hid = out_ref.shape
     share = 2 * feat // devices
-    top = jnp.zeros((feat, hid), f32)
-    low = jnp.zeros((feat, hid), f32)
+    me = rid_ref[0]
+    lin_grads = {}
     for ref, ks in zip(lin_refs, groups, strict=True):
         for at, k in enumerate(ks):
-            low = low + mm_dims(partner_refs[k][...], ref[at], TT)
-            top = top + mm_dims(victim_ref[k], ref[at], TT)
-    both = jnp.concatenate([top, low], 0)
-    short = sums_ref[...]
-    for d in range(devices):
-        out_ref[d] = jnp.concatenate([both[d * share : (d + 1) * share], short], 0).astype(bf16)
-
-
-def local_grad_kernel(rid_ref, local_ref, w1_ref, *refs, groups, near):
-    asked_refs, refs = refs[:near], refs[near:]
-    near_refs, refs = refs[:near], refs[near:]
-    lin_refs, (grad_ref, vg_ref) = refs[:-2], refs[-2:]
-    me = rid_ref[0]
-    regions, slots = local_ref.shape
-    nets, feat = grad_ref.shape
-    for ref, ks in zip(lin_refs, groups, strict=True):
-        for at, k in enumerate(ks):
-            vg_ref[k * slots : (k + 1) * slots, :] = mm_dims(ref[at], w1_ref[:feat, :], NT).astype(
-                bf16
-            )
+            lin_grads[k] = ref[at]
+            vg_ref[k * slots : (k + 1) * slots, :] = mm_dims(
+                lin_grads[k], w1_ref[:feat, :], NT
+            ).astype(bf16)
     local = [local_ref[pl.ds(me ^ k, 1), :] for k in range(regions)]
     for at in range(0, nets, BLOCK):
         hot = jnp.concatenate([onehot_cols(row, at, BLOCK) for row in local], 1)
         total = mm(hot, vg_ref[...])
         for k in range(near):
-            total = total + mm(onehot_cols(asked_refs[k][...], at, BLOCK), near_refs[k][...])
+            total = total + mm(onehot_cols(asked_refs[k][...], at, BLOCK), near_rows[k])
         grad_ref[at : at + BLOCK, :] = total
+        if (at + BLOCK) * 2 % nets == 0:
+            grad_ref.flush(at + BLOCK)
+    top = jnp.zeros((feat, hid), f32)
+    low = jnp.zeros((feat, hid), f32)
+    for k in range(regions):
+        top = top + mm_dims(victim_ref[k], lin_grads[k], TT)
+        low = low + mm_dims(partner_refs[k][...], lin_grads[k], TT)
+    both = jnp.concatenate([top, low], 0)
+    short = sums_ref[...]
+    for d in range(devices):
+        out_ref[d] = jnp.concatenate([both[d * share : (d + 1) * share], short], 0).astype(bf16)
 
 
 def layer_grad_kernel(
@@ -239,50 +250,52 @@
 ):
     asked_refs, refs = refs[:far], refs[far:]
     far_refs, refs = refs[:far], refs[far:]
-    (total_ref, pre_grad_ref, agg_grad_ref, gnn_out_ref), refs = refs[:4], refs[4:]
+    (rest_ref, agg_grad_ref, gnn_out_ref), refs = refs[:3], refs[3:]
     back_refs, back_ref = refs[:-1], refs[-1]
     nets, feat = grad_ref.shape
     halo = back_refs[0].shape[0]
     top = jnp.zeros((feat, feat), f32)
     low = jnp.zeros((feat, feat), f32)
+    back = jnp.zeros(back_ref.shape, f32)
     for at in range(0, nets, STEP):
         rows = pl.ds(at, STEP)
         total = grad_ref[rows, :]
         for k in range(far):
             total = total + mm(onehot_cols(asked_refs[k][...], at, STEP), far_refs[k][...])
-        total_ref[rows, :] = total
-        total_ref.flush(at + STEP)
-        pre_grad = (total * slope_ref[rows, :]).astype(bf16)
-        pre_grad_ref[rows, :] = pre_grad
-        pre_grad_ref.flush(at + STEP)
-        agg_grad = mm_dims(gnn_ref[feat:, :], pre_grad, NT)
-        agg_grad_ref[:, rows] = (agg_grad * (1.0 / degree)).astype(bf16)
+        pre_grad = (total * slope_ref[rows, :].astype(f32)).astype(bf16)
+        agg_grad = mm_dims(pre_grad, gnn_ref[feat:, :], NT)
+        agg_grad = (agg_grad * (1.0 / degree)).astype(bf16)
+        agg_grad_ref[rows, :] = agg_grad
+        rest_ref[rows, :] = total + mm_dims(pre_grad, gnn_ref[:feat, :], NT)
+        if (at + STEP) * 2 % nets == 0:
+            rest_ref.flush(at + STEP)
+            agg_grad_ref.flush(at + STEP)
         top = top + mm_dims(embeds_ref[rows, :], pre_grad, TT)
         low = low + mm_dims(agg_ref[rows, :], pre_grad, TT)
-    agg_grad_ref.flush()
+        back = back + mm(halo_ref[at // STEP], agg_grad)
     gnn_out_ref[:feat, :] = top.astype(bf16)
     gnn_out_ref[feat:, :] = low.astype(bf16)
-    for at in range(0, halo_ref.shape[1], BLOCK):
-        back = mm(agg_grad_ref[...], halo_ref[:, at : at + BLOCK])
-        back_ref[at : at + BLOCK, :] = back.T.astype(bf16)
+    gnn_out_ref.flush()
+    back_ref[...] = back.astype(bf16)
     me = cid_ref[0]
     for k, out_ref in enumerate(back_refs):
         out_ref[...] = back_ref[pl.ds(pl.multiple_of((me ^ k) * halo, halo), halo), :]
 
 
-def own_grad_kernel(total_ref, pre_grad_ref, gnn_ref, agg_grad_ref, own_ref, out_ref):
-    nets, feat = total_ref.shape
+def own_grad_kernel(after_ref, rest_ref, agg_grad_ref, own_ref, out_ref):
+    nets, feat = out_ref.shape
+    for at in range(0, nets, STEP):
+        part = mm(own_ref[at // STEP], agg_grad_ref[pl.ds(at, STEP), :])
+        if at == 0:
+            out_ref[...] = part
+        else:
+            out_ref[...] += part
     for at in range(0, nets, STEP):
         rows = pl.ds(at, STEP)
-        out_ref[rows, :] = (
-            total_ref[rows, :]
-            + mm_dims(pre_grad_ref[rows, :], gnn_ref[:feat, :], NT)
-            + mm(agg_grad_ref[...], own_ref[:, rows]).T
-        )
-
-
-def share_kernel(w1_ref, gnn_ref, *refs, nets_total):
-    wide_ref, short_ref = refs[-2:]
+        out_ref[rows, :] += rest_ref[rows, :]
+
+
+def share_kernel(w1_ref, gnn_ref, wide_ref, short_ref, *, nets_total, doms):
     share, hid = gnn_ref.shape[1:]
     w1_sum = jnp.sum(w1_ref[...].astype(f32), 0)
     gnn_sum = jnp.sum(gnn_ref[...].astype(f32), 0)
@@ -291,27 +304,31 @@
     sq_sum = short[2:3] + short[3:4]
     count = short[4:5] + short[5:6]
     factor = 8.0 / jnp.sqrt(count)
-    both = (jnp.concatenate([w1_sum[:share], gnn_sum], 0) * factor).astype(bf16)
-    wide_ref[...] = jnp.broadcast_to(both[None], wide_ref.shape)
+    halves = [(w1_sum[:share] * factor).astype(bf16), (gnn_sum * factor).astype(bf16)]
+    for d in range(wide_ref.shape[0]):
+        wide_ref[d] = halves[d // doms % 2]
     short_ref[...] = jnp.concatenate(
         [w2_sum * factor, sq_sum / count, 8.0 * nets_total / count, jnp.zeros((5, hid), f32)], 0
     )
 
 
-def unpack_kernel(spread_ref, w1_ref, gnn_ref):
-    devices, rows, _ = spread_ref.shape
-    share = rows // 2
+def unpack_kernel(rid_ref, mine_ref, other_ref, w1_ref, gnn_ref):
+    devices, share, _ = mine_ref.shape
+    even = rid_ref[0] % 2 == 0
     for d in range(devices):
-        got = spread_ref[d].astype(f32)
-        w1_ref[d * share : (d + 1) * share, :] = got[:share]
-        gnn_ref[d * share : (d + 1) * share, :] = got[share:]
+        rows = slice(d * share, (d + 1) * share)
+        mine, other = mine_ref[d].astype(f32), other_ref[d].astype(f32)
+        w1_ref[rows, :] = jnp.where(even, mine, other)
+        gnn_ref[rows, :] = jnp.where(even, other, mine)
         if (d + 1) % (devices // PARTS) == 0:
             w1_ref.flush((d + 1) * share)
             gnn_ref.flush((d + 1) * share)
 
 
 def final_kernel(cid_ref, short_ref, send_ref, own_ref, *refs):
-    got_refs, out_ref = refs[:-1], refs[-1]
+    got_refs, (out_ref, w2_ref, loss_ref) = refs[:-3], refs[-3:]
+    w2_ref[...] = short_ref[0:1, :]
+    loss_ref[...] = short_ref[1:2, :]
     nets = out_ref.shape[0]
     me = cid_ref[0]
     scale = short_ref[2:3, :]
@@ -342,7 +359,9 @@
     def __init__(self, source, target, sems):
         self.target, self.waited = target, 0
         self.shape = source.shape
-        self.rows = max(source.shape[0] // PARTS, 1)
+        size = math.prod(source.shape) * jnp.dtype(source.dtype).itemsize
+        parts = PARTS if size > 1 << 20 else 2 if size > 1 << 19 else 1
+        self.rows = max(source.shape[0] // parts, 1)
         self.copies = []
         for at in range(source.shape[0] // self.rows):
             part = pl.ds(at * self.rows, self.rows)
@@ -393,7 +412,7 @@
             copy.wait()
 
 
-def call(kernel, name, outs, args, scratch=(), mib=24, flops=1):
+def call(kernel, name, outs, args, scratch=(), mib=32, flops=1):
     ins = [kind for _, kind in args]
     kinds = [kind for _, _, kind in outs]
     staged = [pltpu.VMEM(value.shape, value.dtype) for value, kind in args if kind == "H"]
@@ -499,24 +518,26 @@
     wanted = [lax.dynamic_slice_in_dim(pair_remote, my_region ^ k, 1, 0) for k in range(regions)]
     asked = [wanted[0]] + [permute(wanted[k], k) for k in range(1, regions)]
 
+    steps = nets // STEP
     own, from_halo, agg_sum = pl.pallas_call(
         adjacency_kernel,
-        grid=(nets // BLOCK,),
+        grid=(steps,),
         in_specs=[
-            pl.BlockSpec((degree, BLOCK), lambda i: (0, i)),
+            pl.BlockSpec((degree, STEP), lambda i: (0, i)),
             pl.BlockSpec((nets, feat), lambda i: (0, 0)),
         ],
         out_specs=[
-            pl.BlockSpec((BLOCK, nets), lambda i: (i, 0)),
-            pl.BlockSpec((BLOCK, halo_rows), lambda i: (i, 0)),
-            pl.BlockSpec((BLOCK, feat), lambda i: (i, 0)),
+            pl.BlockSpec((1, nets, STEP), lambda i: (i, 0, 0)),
+            pl.BlockSpec((1, halo_rows, STEP), lambda i: (i, 0, 0)),
+            pl.BlockSpec((STEP, feat), lambda i: (i, 0)),
         ],
         out_shape=[
-            in_hbm((nets, nets), bf16),
-            in_hbm((nets, halo_rows), bf16),
+            in_hbm((steps, nets, STEP), bf16),
+            in_hbm((steps, halo_rows, STEP), bf16),
             in_hbm((nets, feat), f32),
         ],
-        compiler_params=pltpu.CompilerParams(vmem_limit_bytes=16 << 20),
+        scratch_shapes=[pltpu.VMEM((feat, nets), bf16)],
+        compiler_params=pltpu.CompilerParams(vmem_limit_bytes=24 << 20),
         cost_estimate=SMALL,
         name="adjacency",
     )(neighbours.T, embeds)
@@ -530,88 +551,78 @@
         + out("V", bf16, slots, feat) * far,
         h(from_halo, agg_sum, embeds, gnn_weight) + v(received, *asked[near:]),
     )
-    near_sends = call(
-        gather_kernel,
-        "gather_near",
-        out("V", bf16, slots, feat) * near,
-        v(net_values, *asked[:near]),
+    victim, linear_own, slope, *near_sends = call(
+        functools.partial(victim_kernel, near=near),
+        "victims",
+        out("H", bf16, regions, slots, feat)
+        + out("V", f32, regions, slots, hid)
+        + out("H", bf16, nets, feat)
+        + out("V", bf16, slots, feat) * near,
+        [(rid, "S")] + v(pair_local, net_values) + h(pair_w1) + v(pre, *asked[:near]),
+        flops=VICTIMS,
     )
     partners = [near_sends[0]]
     partners += [permute(near_sends[k], k) for k in range(1, near)]
     partners += [permute(far_sends[k - near], k) for k in range(near, regions)]
 
-    victim, linear_own, slope = call(
-        victim_kernel,
-        "victims",
-        out("H", bf16, regions, slots, feat)
-        + out("V", f32, regions, slots, hid)
-        + out("H", f32, nets, feat),
-        [(rid, "S")] + v(pair_local, net_values) + h(pair_w1) + v(pre),
-    )
-
-    groups = [tuple(range(near))] + [(k,) for k in range(near, regions)]
+    groups = [(k,) for k in range(near, regions)] + [tuple(range(near))]
     w2_row = pair_w2.reshape(1, hid)
-    lin_grads, backs, sums = [], [], []
+    lin_grads, backs, sums = [], {}, []
     for ks in groups:
+        pieces = 2 if ks[0] < near else 1
         lin_grad, sums_now, *back = call(
             functools.partial(pair_kernel, ks=ks, first=ks is groups[0], last=ks is groups[-1]),
             "pairs",
             out("H", bf16, len(ks), slots, hid)
             + out("V", f32, 8, hid)
-            + out("V", bf16, slots, feat) * len(ks),
+            + out("V", bf16, slots // pieces, feat) * (pieces * len(ks)),
             [(rid, "S"), (pair_count, "S")]
             + v(targets, linear_own, pair_w1, w2_row)
             + v(*[partners[k] for k in ks])
             + v(*sums),
+            flops=PAIRS,
         )
         lin_grads.append(lin_grad)
-        backs += back
+        for at, k in enumerate(ks):
+            backs[k] = back[at * pieces : (at + 1) * pieces]
         sums = [sums_now]
-    returned = [backs[0]] + [permute(backs[k], k) for k in range(1, regions)]
-
-    (local_grad,) = call(
+    returned = [backs[0]] + [[permute(x, k) for x in backs[k]] for k in range(1, regions)]
+
+    local_grad, w1_parts = call(
         functools.partial(local_grad_kernel, groups=groups, near=near),
         "local_grads",
-        out("V", f32, nets, feat),
+        out("H", f32, nets, feat) + out("V", bf16, devices, share + 8, hid),
         [(rid, "S")]
         + v(pair_local)
         + h(pair_w1)
-        + v(*asked[:near], *returned[:near])
-        + h(*lin_grads),
+        + v(sums[0], *asked[:near], *sum(returned[:near], []))
+        + h(*lin_grads, *partners, victim),
         [pltpu.VMEM((regions * slots, feat), bf16)],
     )
-    (w1_parts,) = call(
-        functools.partial(w1_grad_kernel, groups=groups),
-        "w1_grads",
-        out("V", bf16, devices, share + 8, hid),
-        [(local_grad, "A")] + h(victim) + v(sums[0]) + h(*partners, *lin_grads),
-    )
     w1_got = exchange(w1_parts, BOTH)
 
-    total_grad, pre_grad, agg_grad, gnn_part, *backs = call(
+    rest, agg_grad, gnn_part, *backs = call(
         functools.partial(layer_grad_kernel, far=far, peers=peers, degree=degree),
         "layer_grad",
         out("H", f32, nets, feat)
         + out("H", bf16, nets, feat)
-        + out("H", bf16, feat, nets)
-        + out("V", bf16, 2 * feat, feat)
+        + out("H", bf16, 2 * feat, feat)
         + out("V", bf16, halo, feat) * peers,
         [(cid, "S")]
-        + h(slope, embeds, aggregate, gnn_weight, from_halo)
-        + v(local_grad, *asked[near:], *returned[near:]),
+        + h(slope, embeds, aggregate, gnn_weight, from_halo, local_grad)
+        + v(*asked[near:], *sum(returned[near:], [])),
         [pltpu.VMEM((halo_rows, feat), bf16)],
-        mib=24,
-        flops=10000000000,
+        flops=10**10,
     )
     gnn_part, w1_got = lax.optimization_barrier((gnn_part, w1_got))
     gnn_got = exchange(gnn_part.reshape(devices, share, feat), BOTH)
     returned_halo = [backs[0]] + [permute(backs[k], k, "dom") for k in range(1, peers)]
 
     wide, short = call(
-        functools.partial(share_kernel, nets_total=nets * devices),
+        functools.partial(share_kernel, nets_total=nets * devices, doms=peers),
         "shares",
-        out("V", bf16, devices, 2 * share, feat) + out("V", f32, 8, hid),
-        v(w1_got, gnn_got) + [(value, "A") for value in returned_halo],
+        out("V", bf16, devices, share, feat) + out("V", f32, 8, hid),
+        v(w1_got, gnn_got),
     )
     spread = exchange(wide, BOTH)
 
@@ -619,22 +630,23 @@
         own_grad_kernel,
         "own_grads",
         out("V", f32, nets, feat),
-        h(total_grad, pre_grad, gnn_weight, agg_grad, own),
-        mib=24,
-    )
-    (embeds_grad,) = call(
+        [(short, "A")] + h(rest, agg_grad, own),
+    )
+    embeds_grad, w2_grad, loss = call(
         final_kernel,
         "embeds_grads",
-        out("V", bf16, nets, feat),
+        out("V", bf16, nets, feat) + out("V", f32, 1, hid) * 2,
         [(cid, "S")] + v(short, halo_send, own_grad, *returned_halo),
-    )
+        flops=FINAL,
+    )
+    spread, w2_grad = lax.optimization_barrier((spread, w2_grad))
     w1_grad, gnn_grad = call(
         unpack_kernel,
         "unpack",
         out("H", f32, 2 * feat, hid) + out("H", f32, 2 * feat, feat),
-        v(spread),
-    )
-    return embeds_grad, gnn_grad, w1_grad, short[0], short[1, 0]
+        [(rid, "S")] + v(spread, permute(spread, 1)),
+    )
+    return embeds_grad, gnn_grad, w1_grad, w2_grad[0], loss[0, 0]
 
 
 def solution(mesh):

time: 138 us -> 116 us (0.84)
  Pallas kernels: 79.1 us -> 65.9 us
  waiting for transfers between devices: 11.8 us -> 8.73 us
  local copies, waits for them, and re-layouts: 4.29 us -> 1.36 us
  starting transfers between devices: 40.9 us -> 38.2 us
    pallas_call x14 -> x12, Pallas kernels: 65.5 us -> 57.3 us  [call(): pl.pallas_call(body, out_shape=[(in_hbm if kind == 'H' else shape)(dims,...]
    pallas_call x1, Pallas kernels: 13.6 us -> 8.55 us  [local(): pl.pallas_call(adjacency_kernel, grid=(steps,), in_specs=[pl.BlockSpec((d...]
    ppermute x16 -> x18, waiting for transfers between devices: 6.19 us -> 2.1 us  [permute(): return lax.ppermute(value, axis, [(i, i ^ k) for i in range(size)])]
    all_to_all x4, starting transfers between devices: 21.9 us -> 18.4 us  [exchange(): return lax.all_to_all(value, axis, split_axis=0, concat_axis=0, tiled=True)]
    unnamed x36 -> x28, local copies, waits for them, and re-layouts: 3.2 us -> 0.83 us
    ppermute x16 -> x18, starting transfers between devices: 19.1 us -> 19.8 us  [permute(): return lax.ppermute(value, axis, [(i, i ^ k) for i in range(size)])]
  transfers between devices with their start and end apart: 20 -> 22, of which waited for: 4 -> 6; matrix products, arithmetic and copies ran while one was open for 1% -> 0% of each run, Pallas kernels for 53% -> 53%
where the time goes in v3:
time: 116 us; the launch traced here: 115 us
  Pallas kernels  65.9 us (57%)
  starting transfers between devices  38.2 us (33%)
  waiting for transfers between devices  8.73 us (8%)
  local copies, waits for them, and re-layouts  1.36 us (1%)
  between operations  1.16 us (1%)
    pallas_call x12, Pallas kernels, call(): pl.pallas_call(body, out_shape=[(in_hbm if kind == 'H' else shape)(dims,...  57.3 us
    ppermute x18, starting transfers between devices, permute(): return lax.ppermute(value, axis, [(i, i ^ k) for i in range(size)])  19.8 us
    all_to_all x4, starting transfers between devices, exchange(): return lax.all_to_all(value, axis, split_axis=0, concat_axis=0, tiled=True)  18.4 us
    pallas_call x1, Pallas kernels, local(): pl.pallas_call(adjacency_kernel, grid=(steps,), in_specs=[pl.BlockSpec((d...  8.55 us
    all_to_all x4, waiting for transfers between devices, exchange(): return lax.all_to_all(value, axis, split_axis=0, concat_axis=0, tiled=True)  6.63 us
  transfers between devices with their start and end apart: 22, of which 6 were waited for; matrix products, arithmetic and copies ran while one was open for 0% of the time, Pallas kernels for 53%

profile of v3, /device:TPU:0, one launch (start us, length us, event | category | flops | bytes accessed | tf_op | source)
XLA Modules:
  0.0 115.3 jit_solution(449507243936126669)
XLA Ops:
  0.6 0.0 copy-start
  0.7 0.0 copy-start.8
  0.7 0.8 copy-done.8
  1.4 3.4 %halo_gather.1 = bf16[1024,256]{1,0:T(8,128)(2,1)} custom-call(s32[8,128]{1,0:T(8,128)S(1)} %copy-done.8, bf16[2048,256]{1,0:T(8,128)(2,1)} %refs_2_.12), custom_call_target="tpu_custom_call" | custom-call | flops 1 | bytes 1 | tf_op jit(solution)/shard_map/halo_gather/pallas_call | solution.py:448
  4.8 7.3 %all-to-all-start = ((bf16[8,128,256]{2,1,0:T(8,128)(2,1)}), bf16[8,128,256]{2,1,0:T(8,128)(2,1)S(1)}, u32[]{:S(2)}, u32[]{:S(2)}) async-start(bf16[8,128,256]{2,1,0:T(8,128)(2,1)} %bitcast.3), calls=%async_computation | async-start | bytes 1048576 | tf_op jit(solution)/shard_map/all_to_all | solution.py:468
  12.1 1.6 %collective-permute-start = (s32[1,512]{1,0:T(1,128)S(1)}, s32[1,512]{1,0:T(1,128)S(1)}, u32[]{:S(2)}, u32[]{:S(2)}) collective-permute-start(s32[1,512]{1,0:T(1,128)S(1)} %get-tuple-element.105), channel_id=1, source_target_pairs={{0,16},{8,24},{16,0},{24,8},{1,17},{9,25},{17,1},{25,9},{2,18},{10... | collective-permute-start | bytes 6152 | tf_op jit(solution)/shard_map/ppermute | solution.py:499
  13.7 0.7 collective-permute-start.2
  14.3 8.6 %adjacency.1 = (bf16[4,2048,512]{2,1,0:T(8,128)(2,1)}, bf16[4,1024,512]{2,1,0:T(8,128)(2,1)}, f32[2048,256]{1,0:T(8,128)}) custom-call(s32[8,2048]{1,0:T(8,128)S(1)} %bitcast.9, bf16[2048,256]{1,0:T(8,128)(2,1)S(1)} %copy-done), custom_call_target="tpu_custom_call" | custom-call | flops 1 | bytes 1 | tf_op jit(solution)/shard_map/adjacency/pallas_call | solution.py:522
  22.9 3.7 %all-to-all-done = bf16[8,128,256]{2,1,0:T(8,128)(2,1)S(1)} async-done(((bf16[8,128,256]{2,1,0:T(8,128)(2,1)}), bf16[8,128,256]{2,1,0:T(8,128)(2,1)S(1)}, u32[]{:S(2)}, u32[]{:S(2)}) %all-to-all-start) | async-done | bytes 524320 | tf_op jit(solution)/shard_map/all_to_all | solution.py:468
  26.6 6.9 %layer.1 = (f32[2048,256]{1,0:T(8,128)S(1)}, bf16[2048,256]{1,0:T(8,128)(2,1)}, bf16[2048,256]{1,0:T(8,128)(2,1)S(1)}, bf16[512,256]{1,0:T(8,128)(2,1)S(1)}, bf16[512,256]{1,0:T(8,128)(2,1)S(1)}) custom-call(bf16[4,1024,512]{2,1,0:T(8,128)(2,1)} %get-tuple-element.54.refs_0_.refs_5_, f32[2048,256]{1,0:T(8,128)} %get-tuple-element.55.refs_1_, ...), custom_call_target="tpu_custom_call" | custom-call | flops 1 | bytes 1 | tf_op jit(solution)/shard_map/layer/pallas_call | solution.py:448
  33.5 1.6 %collective-permute-start.5 = (bf16[512,256]{1,0:T(8,128)(2,1)S(1)}, bf16[512,256]{1,0:T(8,128)(2,1)S(1)}, u32[]{:S(2)}, u32[]{:S(2)}) collective-permute-start(bf16[512,256]{1,0:T(8,128)(2,1)S(1)} %get-tuple-element.64), channel_id=1, source_target_pairs={{0,16},{8,24},{16,0},{24,8},{1,17},{9,25},{17,1},{25,9},{2,18},{10... | collective-permute-start | bytes 786440 | tf_op jit(solution)/shard_map/ppermute | solution.py:499
  35.1 0.0 collective-permute-start.4
  35.1 0.0 collective-permute-done.2.refs_6_.refs_5_
  35.1 0.0 copy-start.1
  35.1 0.0 copy-start.10
  35.1 0.0 copy-start.11
  35.1 9.3 %victims.1 = (bf16[4,512,256]{2,1,0:T(8,128)(2,1)}, f32[4,512,256]{2,1,0:T(8,128)S(1)}, bf16[2048,256]{1,0:T(8,128)(2,1)}, bf16[512,256]{1,0:T(8,128)(2,1)S(1)}, bf16[512,256]{1,0:T(8,128)(2,1)S(1)}) custom-call(s32[1]{0:T(128)} %bitcast.1.refs_0_, s32[4,512]{1,0:T(4,128)S(1)} %copy-done.7, bf16[2048,256]{1,0:T(8,128)(2,1)S(1)} %get-tuple-element.56.refs_2_, ...), custom_call_target="tpu_custom_call" | custom-call | flops 10000000000 | bytes 1 | tf_op jit(solution)/shard_map/victims/pallas_call | solution.py:448
  44.5 0.7 collective-permute-start.3
  45.2 2.0 %pairs.3 = (bf16[1,512,256]{2,1,0:T(8,128)(2,1)}, f32[8,256]{1,0:T(8,128)S(1)}, bf16[512,256]{1,0:T(8,128)(2,1)S(1)}) custom-call(s32[1]{0:T(128)} %bitcast.1.refs_0_, s32[1,4]{1,0:T(1,128)S(1)} %copy-done.11, f32[4,512]{1,0:T(4,128)S(1)} %copy-done.10, f32[4,512,256]{2,1,0:T(8,128)S(1)} %get-tuple-element.60.refs_3_, bf16[512,256]{1,0:T(8,128)(2,1)S(1)} %copy-done.1, ...), custom_call_target="tpu_custom_call" | custom-call | flops 2000000000 | bytes 1 | tf_op jit(solution)/shard_map/pairs/pallas_call | solution.py:448
  47.3 2.0 %pairs.4 = (bf16[1,512,256]{2,1,0:T(8,128)(2,1)}, f32[8,256]{1,0:T(8,128)S(1)}, bf16[512,256]{1,0:T(8,128)(2,1)S(1)}) custom-call(s32[1]{0:T(128)} %bitcast.1.refs_0_, s32[1,4]{1,0:T(1,128)S(1)} %copy-done.11, f32[4,512]{1,0:T(4,128)S(1)} %copy-done.10, f32[4,512,256]{2,1,0:T(8,128)S(1)} %get-tuple-element.60.refs_3_, bf16[512,256]{1,0:T(8,128)(2,1)S(1)} %copy-done.1, ...), custom_call_target="tpu_custom_call" | custom-call | flops 2000000000 | bytes 1 | tf_op jit(solution)/shard_map/pairs/pallas_call | solution.py:448
  49.2 1.2 %collective-permute-start.9 = (bf16[512,256]{1,0:T(8,128)(2,1)S(1)}, bf16[512,256]{1,0:T(8,128)(2,1)S(1)}, u32[]{:S(2)}, u32[]{:S(2)}) collective-permute-start(bf16[512,256]{1,0:T(8,128)(2,1)S(1)} %get-tuple-element.78), channel_id=1, source_target_pairs={{0,24},{8,16},{16,8},{24,0},{1,25},{9,17},{17,9},{25,1},{2,26},{10... | collective-permute-start | bytes 786440 | tf_op jit(solution)/shard_map/ppermute | solution.py:499
  50.5 0.5 collective-permute-start.8
  51.0 2.7 %pairs.5 = (bf16[2,512,256]{2,1,0:T(8,128)(2,1)}, f32[8,256]{1,0:T(8,128)S(1)}, bf16[256,256]{1,0:T(8,128)(2,1)S(1)}, bf16[256,256]{1,0:T(8,128)(2,1)S(1)}, bf16...) custom-call(s32[1]{0:T(128)} %bitcast.1.refs_0_, s32[1,4]{1,0:T(1,128)S(1)} %copy-done.11, ...), custom_call_target="tpu_custom_call" | custom-call | flops 2000000000 | bytes 1 | tf_op jit(solution)/shard_map/pairs/pallas_call | solution.py:448
  53.7 0.3 collective-permute-start.6
  54.0 0.3 collective-permute-start.7
  54.3 0.8 collective-permute-done.6.refs_8_
  55.1 0.2 collective-permute-done.7.refs_9_
  55.3 8.2 %local_grads.1 = (f32[2048,256]{1,0:T(8,128)}, bf16[32,24,256]{2,1,0:T(8,128)(2,1)}) custom-call(s32[1]{0:T(128)} %bitcast.1.refs_0_, s32[4,512]{1,0:T(4,128)S(1)} %copy-done.7, bf16[512,256]{1,0:T(8,128)(2,1)} %refs_2_.11, f32[8,256]{1,0:T(8,128)S(1)} %get-tuple-element.67.refs_3_, s32[1,512]{1,0:T(1,128)S(1)} %get-tuple-element.106.refs_5_.refs_4_, ...), custom_call_target="tpu_custom_call" | custom-call | flops 1 | bytes 1 | tf_op jit(solution)/shard_map/local_grads/pallas_call | solution.py:448
  63.5 3.7 %all-to-all-start.1 = ((bf16[32,24,256]{2,1,0:T(8,128)(2,1)}), bf16[32,24,256]{2,1,0:T(8,128)(2,1)S(1)}, u32[]{:S(2)}, u32[]{:S(2)}) async-start(bf16[32,24,256]{2,1,0:T(8,128)(2,1)} %get-tuple-element.80), calls=%async_computation.1 | async-start | bytes 786432 | tf_op jit(solution)/shard_map/all_to_all | solution.py:468
  67.2 10.8 %layer_grad.1 = (f32[2048,256]{1,0:T(8,128)}, bf16[2048,256]{1,0:T(8,128)(2,1)}, bf16[512,256]{1,0:T(8,128)(2,1)}, bf16[128,256]{1,0:T(8,128)(2,1)S(1)}, bf16[12...) custom-call(s32[1]{0:T(128)} %bitcast.refs_0_, ...), custom_call_target="tpu_custom_call" | custom-call | flops 10000000000 | bytes 1 | tf_op jit(solution)/shard_map/layer_grad/pallas_call | solution.py:448
  78.1 2.7 %all-to-all-done.1.refs_0_ = bf16[32,24,256]{2,1,0:T(8,128)(2,1)S(1)} async-done(((bf16[32,24,256]{2,1,0:T(8,128)(2,1)}), bf16[32,24,256]{2,1,0:T(8,128)(2,1)S(1)}, u32[]{:S(2)}, u32[]{:S(2)}) %all-to-all-start.1) | async-done | bytes 393248 | tf_op jit(solution)/shard_map/all_to_all | solution.py:468
  80.7 3.2 %all-to-all-start.2 = ((bf16[32,16,256]{2,1,0:T(8,128)(2,1)}), bf16[32,16,256]{2,1,0:T(8,128)(2,1)S(1)}, u32[]{:S(2)}, u32[]{:S(2)}) async-start(bf16[32,16,256]{2,1,0:T(8,128)(2,1)} %bitcast.10), calls=%async_computation.2 | async-start | bytes 524288 | tf_op jit(solution)/shard_map/all_to_all | solution.py:468
  83.9 1.8 %collective-permute-start.10 = (bf16[128,256]{1,0:T(8,128)(2,1)S(1)}, bf16[128,256]{1,0:T(8,128)(2,1)S(1)}, u32[]{:S(2)}, u32[]{:S(2)}) collective-permute-start(bf16[128,256]{1,0:T(8,128)(2,1)S(1)} %get-tuple-element.88), channel_id=1, source_target_pairs={{0,1},{1,0},{2,3},{3,2},{4,5},{5,4},{6,7},{7,6},{8,9},{9,8},{10,11... | collective-permute-start | bytes 196616 | tf_op jit(solution)/shard_map/ppermute | solution.py:499
  85.8 1.5 %collective-permute-start.11 = (bf16[128,256]{1,0:T(8,128)(2,1)S(1)}, bf16[128,256]{1,0:T(8,128)(2,1)S(1)}, u32[]{:S(2)}, u32[]{:S(2)}) collective-permute-start(bf16[128,256]{1,0:T(8,128)(2,1)S(1)} %get-tuple-element.89), channel_id=1, source_target_pairs={{0,2},{1,3},{2,0},{3,1},{4,6},{5,7},{6,4},{7,5},{8,10},{9,11},{10,... | collective-permute-start | bytes 196616 | tf_op jit(solution)/shard_map/ppermute | solution.py:499
  87.2 0.3 collective-permute-start.12
  87.5 2.7 %collective-permute-start.13 = (bf16[128,256]{1,0:T(8,128)(2,1)S(1)}, bf16[128,256]{1,0:T(8,128)(2,1)S(1)}, u32[]{:S(2)}, u32[]{:S(2)}) collective-permute-start(bf16[128,256]{1,0:T(8,128)(2,1)S(1)} %get-tuple-element.91), channel_id=1, source_target_pairs={{0,4},{1,5},{2,6},{3,7},{4,0},{5,1},{6,2},{7,3},{8,12},{9,13},{10,... | collective-permute-start | bytes 196616 | tf_op jit(solution)/shard_map/ppermute | solution.py:499
  90.2 1.5 %collective-permute-start.14 = (bf16[128,256]{1,0:T(8,128)(2,1)S(1)}, bf16[128,256]{1,0:T(8,128)(2,1)S(1)}, u32[]{:S(2)}, u32[]{:S(2)}) collective-permute-start(bf16[128,256]{1,0:T(8,128)(2,1)S(1)} %get-tuple-element.92), channel_id=1, source_target_pairs={{0,5},{1,4},{2,7},{3,6},{4,1},{5,0},{6,3},{7,2},{8,13},{9,12},{10,... | collective-permute-start | bytes 196616 | tf_op jit(solution)/shard_map/ppermute | solution.py:499
  91.6 3.3 %collective-permute-start.15 = (bf16[128,256]{1,0:T(8,128)(2,1)S(1)}, bf16[128,256]{1,0:T(8,128)(2,1)S(1)}, u32[]{:S(2)}, u32[]{:S(2)}) collective-permute-start(bf16[128,256]{1,0:T(8,128)(2,1)S(1)} %get-tuple-element.93), channel_id=1, source_target_pairs={{0,6},{1,7},{2,4},{3,5},{4,2},{5,3},{6,0},{7,1},{8,14},{9,15},{10,... | collective-permute-start | bytes 196616 | tf_op jit(solution)/shard_map/ppermute | solution.py:499
  95.0 2.0 %collective-permute-start.16 = (bf16[128,256]{1,0:T(8,128)(2,1)S(1)}, bf16[128,256]{1,0:T(8,128)(2,1)S(1)}, u32[]{:S(2)}, u32[]{:S(2)}) collective-permute-start(bf16[128,256]{1,0:T(8,128)(2,1)S(1)} %get-tuple-element.94), channel_id=1, source_target_pairs={{0,7},{1,6},{2,5},{3,4},{4,3},{5,2},{6,1},{7,0},{8,15},{9,14},{10,... | collective-permute-start | bytes 196616 | tf_op jit(solution)/shard_map/ppermute | solution.py:499
  97.0 0.8 shares.1
  97.8 4.3 %all-to-all-start.3 = ((bf16[32,16,256]{2,1,0:T(8,128)(2,1)}), bf16[32,16,256]{2,1,0:T(8,128)(2,1)S(1)}, u32[]{:S(2)}, u32[]{:S(2)}) async-start(bf16[32,16,256]{2,1,0:T(8,128)(2,1)} %get-tuple-element.96), calls=%async_computation.3 | async-start | bytes 524288 | tf_op jit(solution)/shard_map/all_to_all | solution.py:468
  102.1 0.0 copy-start.9
  102.1 7.8 %own_grads.1.refs_3_ = f32[2048,256]{1,0:T(8,128)S(1)} custom-call(f32[8,256]{1,0:T(8,128)S(1)} %get-tuple-element.83.refs_0_.refs_1_, f32[2048,256]{1,0:T(8,128)} %get-tuple-element.84.refs_1_, bf16[2048,256]{1,0:T(8,128)(2,1)} %get-tuple-element.85.refs_2_, bf16[4,2048,512]{2,1,0:T(8,128)(2,1)} %get-tuple-element.86.refs_3_), custom_call_target="tpu_custom_call" | custom-call | flops 1 | bytes 1 | tf_op jit(solution)/shard_map/own_grads/pallas_call | solution.py:448
  109.9 2.3 %embeds_grads.1 = (bf16[2048,256]{1,0:T(8,128)(2,1)}, f32[1,256]{1,0:T(1,128)}, f32[1,256]{1,0:T(1,128)S(1)}) custom-call(s32[1]{0:T(128)} %bitcast.refs_0_, f32[8,256]{1,0:T(8,128)S(1)} %get-tuple-element.83.refs_0_.refs_1_, s32[8,128]{1,0:T(8,128)S(1)} %copy-done.9, f32[2048,256]{1,0:T(8,128)S(1)} %own_grads.1.refs_3_, ...), custom_call_target="tpu_custom_call" | custom-call | flops 20000000000 | bytes 1 | tf_op jit(solution)/shard_map/embeds_grads/pallas_call | solution.py:448
  112.2 0.3 all-to-all-done.3.refs_1_
  112.5 0.5 slice.3
  113.0 1.0 collective-permute-done.17.refs_2_
  114.0 1.1 unpack.1
  (40 shorter events, 0.1 us)
Async XLA Ops:
  0.6 13.7 %copy-start = (bf16[2048,256]{1,0:T(8,128)(2,1)S(1)}, bf16[2048,256]{1,0:T(8,128)(2,1)}, u32[]{:S(2)}) copy-start(bf16[2048,256]{1,0:T(8,128)(2,1)} %refs_2_.12) | copy-start | bytes 3145732
  0.6 13.7 %copy-start.6 = (s32[2048,8]{0,1:T(8,128)S(1)}, s32[2048,8]{0,1:T(8,128)}, u32[]{:S(2)}) copy-start(s32[2048,8]{0,1:T(8,128)} %param.11) | copy-start | bytes 196612
  0.7 0.8 copy-start.8
  1.4 10.7 %copy-start.12 = (s32[4,512]{1,0:T(4,128)S(1)}, s32[4,512]{1,0:T(4,128)}, u32[]{:S(2)}) copy-start(s32[4,512]{1,0:T(4,128)} %param.15) | copy-start | bytes 24580
  1.4 21.5 %copy-start.13 = (bf16[256]{0:T(256)(128)(2,1)S(1)}, bf16[256]{0:T(256)(128)(2,1)}, u32[]{:S(2)}) copy-start(bf16[256]{0:T(256)(128)(2,1)} %param.19) | copy-start | bytes 1540
  4.8 21.8 %all-to-all-start = ((bf16[8,128,256]{2,1,0:T(8,128)(2,1)}), bf16[8,128,256]{2,1,0:T(8,128)(2,1)S(1)}, u32[]{:S(2)}, u32[]{:S(2)}) async-start(bf16[8,128,256]{2,1,0:T(8,128)(2,1)} %bitcast.3), calls=%async_computation | async-start | bytes 1048576 | tf_op jit(solution)/shard_map/all_to_all | solution.py:468
  12.1 10.8 %collective-permute-start = (s32[1,512]{1,0:T(1,128)S(1)}, s32[1,512]{1,0:T(1,128)S(1)}, u32[]{:S(2)}, u32[]{:S(2)}) collective-permute-start(s32[1,512]{1,0:T(1,128)S(1)} %get-tuple-element.105), channel_id=1, source_target_pairs={{0,16},{8,24},{16,0},{24,8},{1,17},{9,25},{17,1},{25,9},{2,18},{10... | collective-permute-start | bytes 6152 | tf_op jit(solution)/shard_map/ppermute | solution.py:499
  13.7 9.2 %collective-permute-start.1 = (s32[1,512]{1,0:T(1,128)S(1)}, s32[1,512]{1,0:T(1,128)S(1)}, u32[]{:S(2)}, u32[]{:S(2)}) collective-permute-start(s32[1,512]{1,0:T(1,128)S(1)} %get-tuple-element.104), channel_id=1, source_target_pairs={{0,24},{8,16},{16,8},{24,0},{1,25},{9,17},{17,9},{25,1},{2,26},{10... | collective-permute-start | bytes 6152 | tf_op jit(solution)/shard_map/ppermute | solution.py:499
  13.7 21.4 %collective-permute-start.2 = (s32[1,512]{1,0:T(1,128)S(1)}, s32[1,512]{1,0:T(1,128)S(1)}, u32[]{:S(2)}, u32[]{:S(2)}) collective-permute-start(s32[1,512]{1,0:T(1,128)S(1)} %get-tuple-element.103), channel_id=1, source_target_pairs={{0,8},{8,0},{16,24},{24,16},{1,9},{9,1},{17,25},{25,17},{2,10},{10... | collective-permute-start | bytes 6152 | tf_op jit(solution)/shard_map/ppermute | solution.py:499
  26.6 8.5 %copy-start.7 = (s32[4,512]{1,0:T(4,128)S(1)}, s32[4,512]{1,0:T(4,128)}, u32[]{:S(2)}) copy-start(s32[4,512]{1,0:T(4,128)} %refs_1_.11) | copy-start | bytes 24580
  33.5 11.6 %collective-permute-start.5 = (bf16[512,256]{1,0:T(8,128)(2,1)S(1)}, bf16[512,256]{1,0:T(8,128)(2,1)S(1)}, u32[]{:S(2)}, u32[]{:S(2)}) collective-permute-start(bf16[512,256]{1,0:T(8,128)(2,1)S(1)} %get-tuple-element.64), channel_id=1, source_target_pairs={{0,16},{8,24},{16,0},{24,8},{1,17},{9,25},{17,1},{25,9},{2,18},{10... | collective-permute-start | bytes 786440 | tf_op jit(solution)/shard_map/ppermute | solution.py:499
  35.1 12.1 %collective-permute-start.4 = (bf16[512,256]{1,0:T(8,128)(2,1)S(1)}, bf16[512,256]{1,0:T(8,128)(2,1)S(1)}, u32[]{:S(2)}, u32[]{:S(2)}) collective-permute-start(bf16[512,256]{1,0:T(8,128)(2,1)S(1)} %get-tuple-element.63), channel_id=1, source_target_pairs={{0,24},{8,16},{16,8},{24,0},{1,25},{9,17},{17,9},{25,1},{2,26},{10... | collective-permute-start | bytes 786440 | tf_op jit(solution)/shard_map/ppermute | solution.py:499
  35.1 10.1 %copy-start.1 = (bf16[512,256]{1,0:T(8,128)(2,1)S(1)}, bf16[512,256]{1,0:T(8,128)(2,1)}, u32[]{:S(2)}) copy-start(bf16[512,256]{1,0:T(8,128)(2,1)} %refs_2_.11) | copy-start | bytes 786436
  35.1 10.1 %copy-start.10 = (f32[4,512]{1,0:T(4,128)S(1)}, f32[4,512]{1,0:T(4,128)}, u32[]{:S(2)}) copy-start(f32[4,512]{1,0:T(4,128)} %refs_2_.10) | copy-start | bytes 24580
  35.1 10.0 %copy-start.11 = (s32[1,4]{1,0:T(1,128)S(1)}, s32[1,4]{1,0:T(1,128)}, u32[]{:S(2)}) copy-start(s32[1,4]{1,0:T(1,128)} %refs_1_.10) | copy-start | bytes 52
  44.5 6.5 %copy-start.4 = (bf16[512,256]{1,0:T(8,128)(2,1)}, bf16[512,256]{1,0:T(8,128)(2,1)S(1)}, u32[]{:S(2)}) copy-start(bf16[512,256]{1,0:T(8,128)(2,1)S(1)} %get-tuple-element.61.refs_6_.refs_13_) | copy-start | bytes 786436
  44.5 6.5 %collective-permute-start.3 = (bf16[512,256]{1,0:T(8,128)(2,1)S(1)}, bf16[512,256]{1,0:T(8,128)(2,1)S(1)}, u32[]{:S(2)}, u32[]{:S(2)}) collective-permute-start(bf16[512,256]{1,0:T(8,128)(2,1)S(1)} %get-tuple-element.62), channel_id=1, source_target_pairs={{0,8},{8,0},{16,24},{24,16},{1,9},{9,1},{17,25},{25,17},{2,10},{10... | collective-permute-start | bytes 786440 | tf_op jit(solution)/shard_map/ppermute | solution.py:499
  45.2 2.0 %copy-start.2 = (bf16[512,256]{1,0:T(8,128)(2,1)}, bf16[512,256]{1,0:T(8,128)(2,1)S(1)}, u32[]{:S(2)}) copy-start(bf16[512,256]{1,0:T(8,128)(2,1)S(1)} %collective-permute-done.5.refs_6_.refs_15_) | copy-start | bytes 786436
  47.2 2.0 %copy-start.3 = (bf16[512,256]{1,0:T(8,128)(2,1)}, bf16[512,256]{1,0:T(8,128)(2,1)S(1)}, u32[]{:S(2)}) copy-start(bf16[512,256]{1,0:T(8,128)(2,1)S(1)} %collective-permute-done.4.refs_6_.refs_16_) | copy-start | bytes 786436
  49.2 18.0 %collective-permute-start.9 = (bf16[512,256]{1,0:T(8,128)(2,1)S(1)}, bf16[512,256]{1,0:T(8,128)(2,1)S(1)}, u32[]{:S(2)}, u32[]{:S(2)}) collective-permute-start(bf16[512,256]{1,0:T(8,128)(2,1)S(1)} %get-tuple-element.78), channel_id=1, source_target_pairs={{0,24},{8,16},{16,8},{24,0},{1,25},{9,17},{17,9},{25,1},{2,26},{10... | collective-permute-start | bytes 786440 | tf_op jit(solution)/shard_map/ppermute | solution.py:499
  50.5 16.8 %collective-permute-start.8 = (bf16[512,256]{1,0:T(8,128)(2,1)S(1)}, bf16[512,256]{1,0:T(8,128)(2,1)S(1)}, u32[]{:S(2)}, u32[]{:S(2)}) collective-permute-start(bf16[512,256]{1,0:T(8,128)(2,1)S(1)} %get-tuple-element.77), channel_id=1, source_target_pairs={{0,16},{8,24},{16,0},{24,8},{1,17},{9,25},{17,1},{25,9},{2,18},{10... | collective-permute-start | bytes 786440 | tf_op jit(solution)/shard_map/ppermute | solution.py:499
  51.0 2.7 %copy-start.5 = (bf16[512,256]{1,0:T(8,128)(2,1)}, bf16[512,256]{1,0:T(8,128)(2,1)S(1)}, u32[]{:S(2)}) copy-start(bf16[512,256]{1,0:T(8,128)(2,1)S(1)} %collective-permute-done.3.refs_7_.refs_14_) | copy-start | bytes 786436
  53.7 1.4 %collective-permute-start.6 = (bf16[256,256]{1,0:T(8,128)(2,1)S(1)}, bf16[256,256]{1,0:T(8,128)(2,1)S(1)}, u32[]{:S(2)}, u32[]{:S(2)}) collective-permute-start(bf16[256,256]{1,0:T(8,128)(2,1)S(1)} %get-tuple-element.70), channel_id=1, source_target_pairs={{0,8},{8,0},{16,24},{24,16},{1,9},{9,1},{17,25},{25,17},{2,10},{10... | collective-permute-start | bytes 393224 | tf_op jit(solution)/shard_map/ppermute | solution.py:499
  54.0 1.3 %collective-permute-start.7 = (bf16[256,256]{1,0:T(8,128)(2,1)S(1)}, bf16[256,256]{1,0:T(8,128)(2,1)S(1)}, u32[]{:S(2)}, u32[]{:S(2)}) collective-permute-start(bf16[256,256]{1,0:T(8,128)(2,1)S(1)} %get-tuple-element.71), channel_id=1, source_target_pairs={{0,8},{8,0},{16,24},{24,16},{1,9},{9,1},{17,25},{25,17},{2,10},{10... | collective-permute-start | bytes 393224 | tf_op jit(solution)/shard_map/ppermute | solution.py:499
  63.5 17.2 %all-to-all-start.1 = ((bf16[32,24,256]{2,1,0:T(8,128)(2,1)}), bf16[32,24,256]{2,1,0:T(8,128)(2,1)S(1)}, u32[]{:S(2)}, u32[]{:S(2)}) async-start(bf16[32,24,256]{2,1,0:T(8,128)(2,1)} %get-tuple-element.80), calls=%async_computation.1 | async-start | bytes 786432 | tf_op jit(solution)/shard_map/all_to_all | solution.py:468
  80.7 16.2 %all-to-all-start.2 = ((bf16[32,16,256]{2,1,0:T(8,128)(2,1)}), bf16[32,16,256]{2,1,0:T(8,128)(2,1)S(1)}, u32[]{:S(2)}, u32[]{:S(2)}) async-start(bf16[32,16,256]{2,1,0:T(8,128)(2,1)} %bitcast.10), calls=%async_computation.2 | async-start | bytes 524288 | tf_op jit(solution)/shard_map/all_to_all | solution.py:468
  83.9 7.7 %collective-permute-start.10 = (bf16[128,256]{1,0:T(8,128)(2,1)S(1)}, bf16[128,256]{1,0:T(8,128)(2,1)S(1)}, u32[]{:S(2)}, u32[]{:S(2)}) collective-permute-start(bf16[128,256]{1,0:T(8,128)(2,1)S(1)} %get-tuple-element.88), channel_id=1, source_target_pairs={{0,1},{1,0},{2,3},{3,2},{4,5},{5,4},{6,7},{7,6},{8,9},{9,8},{10,11... | collective-permute-start | bytes 196616 | tf_op jit(solution)/shard_map/ppermute | solution.py:499
  85.8 9.2 %collective-permute-start.11 = (bf16[128,256]{1,0:T(8,128)(2,1)S(1)}, bf16[128,256]{1,0:T(8,128)(2,1)S(1)}, u32[]{:S(2)}, u32[]{:S(2)}) collective-permute-start(bf16[128,256]{1,0:T(8,128)(2,1)S(1)} %get-tuple-element.89), channel_id=1, source_target_pairs={{0,2},{1,3},{2,0},{3,1},{4,6},{5,7},{6,4},{7,5},{8,10},{9,11},{10,... | collective-permute-start | bytes 196616 | tf_op jit(solution)/shard_map/ppermute | solution.py:499
  87.2 22.6 %collective-permute-start.12 = (bf16[128,256]{1,0:T(8,128)(2,1)S(1)}, bf16[128,256]{1,0:T(8,128)(2,1)S(1)}, u32[]{:S(2)}, u32[]{:S(2)}) collective-permute-start(bf16[128,256]{1,0:T(8,128)(2,1)S(1)} %get-tuple-element.90), channel_id=1, source_target_pairs={{0,3},{1,2},{2,1},{3,0},{4,7},{5,6},{6,5},{7,4},{8,11},{9,10},{10,... | collective-permute-start | bytes 196616 | tf_op jit(solution)/shard_map/ppermute | solution.py:499
  87.5 22.4 %collective-permute-start.13 = (bf16[128,256]{1,0:T(8,128)(2,1)S(1)}, bf16[128,256]{1,0:T(8,128)(2,1)S(1)}, u32[]{:S(2)}, u32[]{:S(2)}) collective-permute-start(bf16[128,256]{1,0:T(8,128)(2,1)S(1)} %get-tuple-element.91), channel_id=1, source_target_pairs={{0,4},{1,5},{2,6},{3,7},{4,0},{5,1},{6,2},{7,3},{8,12},{9,13},{10,... | collective-permute-start | bytes 196616 | tf_op jit(solution)/shard_map/ppermute | solution.py:499
  90.2 19.7 %collective-permute-start.14 = (bf16[128,256]{1,0:T(8,128)(2,1)S(1)}, bf16[128,256]{1,0:T(8,128)(2,1)S(1)}, u32[]{:S(2)}, u32[]{:S(2)}) collective-permute-start(bf16[128,256]{1,0:T(8,128)(2,1)S(1)} %get-tuple-element.92), channel_id=1, source_target_pairs={{0,5},{1,4},{2,7},{3,6},{4,1},{5,0},{6,3},{7,2},{8,13},{9,12},{10,... | collective-permute-start | bytes 196616 | tf_op jit(solution)/shard_map/ppermute | solution.py:499
  91.6 18.3 %collective-permute-start.15 = (bf16[128,256]{1,0:T(8,128)(2,1)S(1)}, bf16[128,256]{1,0:T(8,128)(2,1)S(1)}, u32[]{:S(2)}, u32[]{:S(2)}) collective-permute-start(bf16[128,256]{1,0:T(8,128)(2,1)S(1)} %get-tuple-element.93), channel_id=1, source_target_pairs={{0,6},{1,7},{2,4},{3,5},{4,2},{5,3},{6,0},{7,1},{8,14},{9,15},{10,... | collective-permute-start | bytes 196616 | tf_op jit(solution)/shard_map/ppermute | solution.py:499
  95.0 14.9 %collective-permute-start.16 = (bf16[128,256]{1,0:T(8,128)(2,1)S(1)}, bf16[128,256]{1,0:T(8,128)(2,1)S(1)}, u32[]{:S(2)}, u32[]{:S(2)}) collective-permute-start(bf16[128,256]{1,0:T(8,128)(2,1)S(1)} %get-tuple-element.94), channel_id=1, source_target_pairs={{0,7},{1,6},{2,5},{3,4},{4,3},{5,2},{6,1},{7,0},{8,15},{9,14},{10,... | collective-permute-start | bytes 196616 | tf_op jit(solution)/shard_map/ppermute | solution.py:499
  97.8 14.7 %all-to-all-start.3 = ((bf16[32,16,256]{2,1,0:T(8,128)(2,1)}), bf16[32,16,256]{2,1,0:T(8,128)(2,1)S(1)}, u32[]{:S(2)}, u32[]{:S(2)}) async-start(bf16[32,16,256]{2,1,0:T(8,128)(2,1)} %get-tuple-element.96), calls=%async_computation.3 | async-start | bytes 524288 | tf_op jit(solution)/shard_map/all_to_all | solution.py:468
  102.1 7.8 %copy-start.9 = (s32[8,128]{1,0:T(8,128)S(1)}, s32[8,128]{1,0:T(8,128)}, u32[]{:S(2)}) copy-start(s32[8,128]{1,0:T(8,128)} %refs_2_.13) | copy-start | bytes 12292
  112.5 1.5 %collective-permute-start.17 = (bf16[32,16,256]{2,1,0:T(8,128)(2,1)S(1)}, bf16[32,16,256]{2,1,0:T(8,128)(2,1)S(1)}, u32[]{:S(2)}, u32[]{:S(2)}) collective-permute-start(bf16[32,16,256]{2,1,0:T(8,128)(2,1)S(1)} %all-to-all-done.3.refs_1_), channel_id=1, source_target_pairs={{0,8},{8,0},{16,24},{24,16},{1,9},{9,1},{17,25},{25,17},{2,10},{10... | collective-permute-start | bytes 786440 | tf_op jit(solution)/shard_map/ppermute | solution.py:499

commit v4 on v3

--- a/solution.py
+++ b/solution.py
@@ -17,6 +17,8 @@
 BLOCK = 256
 VICTIMS = 10**10
 PAIRS = 2 * 10**9
+LOCAL = 1
+SHARES = 1
 FINAL = 2 * 10**10
 STEP = 512
 TT = (((0,), (0,)), ((), ()))
@@ -51,27 +53,37 @@
 
 def onehot_rows(row, width):
     column = column_of(row).astype(i16)
-    lane = lax.broadcasted_iota(i32, column.shape, 1).astype(i16)
+    lane = lax.broadcasted_iota(i32, (16, 128), 1)
     one = jnp.ones(column.shape, bf16)
     zero = jnp.zeros(column.shape, bf16)
-    return jnp.concatenate(
-        [jnp.where(column == lane + jnp.int16(128 * j), one, zero) for j in range(width // 128)], 1
-    )
+    tiles = []
+    for j in range(width // 128):
+        lanes = jnp.concatenate([(lane + 128 * j).astype(i16)] * (column.shape[0] // 16), 0)
+        tiles.append(jnp.where(column == lanes, one, zero))
+    return jnp.concatenate(tiles, 1)
 
 
 def onehot_cols(row, first, height):
-    shape = (height, row.shape[1])
-    wide = jnp.broadcast_to(row - first, shape).astype(i16)
-    sub = lax.broadcasted_iota(i32, shape, 0).astype(i16)
-    return jnp.where(wide == sub, jnp.ones(shape, bf16), jnp.zeros(shape, bf16))
+    width = row.shape[1]
+    wide = jnp.broadcast_to(row, (16, width)).astype(i16)
+    wide = jnp.concatenate([wide] * (height // 16), 0)
+    sub = (lax.broadcasted_iota(i32, (height, 128), 0) + first).astype(i16)
+    sub = jnp.concatenate([sub] * (width // 128), 1)
+    return jnp.where(wide == sub, jnp.ones(wide.shape, bf16), jnp.zeros(wide.shape, bf16))
 
 
 def halo_gather_kernel(send_ref, embeds_ref, out_ref):
     peers, halo = send_ref.shape
     nets = embeds_ref.shape[0]
-    for p in range(peers):
-        hot = onehot_rows(send_ref[p : p + 1, :], nets)
-        out_ref[p * halo : (p + 1) * halo, :] = mm(hot, embeds_ref[...]).astype(bf16)
+    group = max(peers // 2, 1)
+    sent = send_ref[...]
+    hots = [
+        jnp.concatenate([onehot_rows(sent[q : q + 1, :], nets) for q in range(p, p + group)], 0)
+        for p in range(0, peers, group)
+    ]
+    for at, hot in enumerate(hots):
+        rows = slice(at * group * halo, (at + 1) * group * halo)
+        out_ref[rows, :] = mm(hot, embeds_ref[...]).astype(bf16)
 
 
 def adjacency_kernel(neigh_ref, embeds_ref, own_ref, halo_ref, sum_ref, across_ref):
@@ -109,10 +121,13 @@
     asked_refs, (pre_ref, agg_ref, nets_ref), send_refs = (
         refs[:far],
         refs[far : far + 3],
-        refs[far + 3 :],
-    )
+        refs[far + 3 : -1],
+    )
+    hot_ref = refs[-1]
     nets, feat = nets_ref.shape
     across = received_ref[...].T
+    for k, asked_ref in enumerate(asked_refs):
+        hot_ref[k] = onehot_rows(asked_ref[...], nets)
     for at in range(0, nets, STEP):
         rows = pl.ds(at, STEP)
         total = sum_ref[rows, :] + mm(across, halo_ref[at // STEP]).T
@@ -122,9 +137,8 @@
         pre = mm(embeds_ref[rows, :], gnn_ref[:feat, :]) + mm(agg, gnn_ref[feat:, :])
         pre_ref[rows, :] = pre
         nets_ref[rows, :] = (embeds_ref[rows, :].astype(f32) + gelu_of(pre)).astype(bf16)
-    for asked_ref, send_ref in zip(asked_refs, send_refs, strict=True):
-        hot = onehot_rows(asked_ref[...], nets)
-        send_ref[...] = mm(hot, nets_ref[...]).astype(bf16)
+    for k, send_ref in enumerate(send_refs):
+        send_ref[...] = mm(hot_ref[k], nets_ref[...]).astype(bf16)
 
 
 def victim_kernel(
@@ -138,33 +152,37 @@
     regions, slots = local_ref.shape
     nets, feat = nets_ref.shape
     me = rid_ref[0]
-    for asked_ref, near_ref in zip(asked_refs, near_refs, strict=True):
-        hot = onehot_rows(asked_ref[...], nets)
-        near_ref[...] = mm(hot, nets_ref[...]).astype(bf16)
-    for k in range(regions):
-        hot = onehot_rows(local_ref[pl.ds(me ^ k, 1), :], nets)
-        victim = mm(hot, nets_ref[...]).astype(bf16)
-        victim_ref[k] = victim
-        linear_ref[k] = mm(victim, w1_ref[:feat, :])
-    victim_ref.flush()
     for at in range(0, nets, STEP):
         rows = pl.ds(at, STEP)
         pre = pre_ref[rows, :]
         square = pre * pre
         slope_ref[rows, :] = slope_of(pre, square, gelu_inner(pre, square)).astype(bf16)
-        if at + STEP == nets // 2:
-            slope_ref.flush(nets // 2)
+    slope_ref.flush()
+    for k in range(regions):
+        hot = onehot_rows(local_ref[pl.ds(me ^ k, 1), :], nets)
+        victim_ref[k] = mm(hot, nets_ref[...]).astype(bf16)
+    victim_ref.flush()
+    for asked_ref, near_ref in zip(asked_refs, near_refs, strict=True):
+        hot = onehot_rows(asked_ref[...], nets)
+        near_ref[...] = mm(hot, nets_ref[...]).astype(bf16)
+    for k in range(regions):
+        linear_ref[k] = mm(victim_ref[k], w1_ref[:feat, :])
 
 
 def pair_kernel(rid_ref, count_ref, target_ref, linear_ref, w1_ref, w2_ref, *refs, ks, first, last):
     some = len(ks)
+    slots, hid = linear_ref.shape[1:]
+    feat = refs[0].shape[1]
+    me = rid_ref[0]
     partner_refs, refs = refs[:some], refs[some:]
+    if last:
+        victim_ref, refs = refs[0], refs[1:]
+        others = victim_ref.shape[0] - some
+        old_partner_refs, old_lin_ref, refs = refs[:others], refs[others], refs[others + 1 :]
     if not first:
         before_ref, refs = refs[0], refs[1:]
     lin_grad_ref, sums_ref, *back_refs = refs
-    me = rid_ref[0]
-    slots, hid = linear_ref.shape[1:]
-    feat = partner_refs[0].shape[1]
+    across = []
     w2_row = w2_ref[...].astype(f32)
     w2_column = column_of(w2_row).astype(bf16)
     w2_sum = jnp.zeros((1, hid), f32) if first else before_ref[0:1, :]
@@ -191,62 +209,58 @@
         rows = slots // pieces
         for piece in range(pieces):
             back_refs[at * pieces + piece][...] = back[piece * rows : (piece + 1) * rows]
+        if last:
+            across.append(lin_grad.T)
     if not last:
         sums_ref[...] = jnp.concatenate([w2_sum, sq_sum, jnp.zeros((6, hid), f32)], 0)
-    else:
-        count = count_ref[0, 0]
-        for q in range(1, count_ref.shape[1]):
-            count = count + count_ref[0, q]
-        count_row = jnp.zeros((1, hid), f32) + count.astype(f32)
-        parts = []
-        for row in (w2_sum, sq_sum, count_row):
-            high = row.astype(bf16).astype(f32)
-            parts += [high, row - high]
-        sums_ref[...] = jnp.concatenate(parts + [jnp.zeros((2, hid), f32)], 0)
-
-
-def local_grad_kernel(rid_ref, local_ref, w1_ref, sums_ref, *refs, groups, near):
+        return
+    for at in range(others):
+        across.append(old_lin_ref[at].T)
+    across = jnp.concatenate(across, 1)
+    victims = jnp.concatenate([victim_ref[k] for k in range(some + others)], 0)
+    partners = jnp.concatenate([ref[...] for ref in [*partner_refs, *old_partner_refs]], 0)
+    both = jnp.concatenate([mm(across, victims).T, mm(across, partners).T], 0)
+    count = count_ref[0, 0]
+    for q in range(1, count_ref.shape[1]):
+        count = count + count_ref[0, q]
+    count_row = jnp.zeros((1, hid), f32) + count.astype(f32)
+    parts = []
+    for row in (w2_sum, sq_sum, count_row):
+        high = row.astype(bf16).astype(f32)
+        parts += [high, row - high]
+    short = jnp.concatenate(parts + [jnp.zeros((2, hid), f32)], 0)
+    devices = sums_ref.shape[0]
+    share = 2 * feat // devices
+    for d in range(devices):
+        sums_ref[d] = jnp.concatenate([both[d * share : (d + 1) * share], short], 0).astype(bf16)
+
+
+def local_grad_kernel(rid_ref, local_ref, w1_ref, after_ref, *refs, groups, near):
     regions, slots = local_ref.shape
     asked_refs, refs = refs[:near], refs[near:]
     near_refs, refs = refs[: 2 * near], refs[2 * near :]
-    near_rows = [
-        jnp.concatenate([near_refs[2 * k][...], near_refs[2 * k + 1][...]], 0) for k in range(near)
-    ]
-    lin_refs, refs = refs[: len(groups)], refs[len(groups) :]
-    partner_refs, (victim_ref, grad_ref, out_ref, vg_ref) = refs[:regions], refs[regions:]
+    lin_refs, (grad_ref, vg_ref) = refs[: len(groups)], refs[len(groups) :]
     nets, feat = grad_ref.shape
-    devices, _, hid = out_ref.shape
-    share = 2 * feat // devices
     me = rid_ref[0]
-    lin_grads = {}
+    returned = jnp.concatenate([near_ref[...] for near_ref in near_refs], 0)
+    for at in range(0, nets, BLOCK):
+        hot = jnp.concatenate([onehot_cols(ref[...], at, BLOCK) for ref in asked_refs], 1)
+        grad_ref[at : at + BLOCK, :] = mm(hot, returned)
     for ref, ks in zip(lin_refs, groups, strict=True):
         for at, k in enumerate(ks):
-            lin_grads[k] = ref[at]
-            vg_ref[k * slots : (k + 1) * slots, :] = mm_dims(
-                lin_grads[k], w1_ref[:feat, :], NT
-            ).astype(bf16)
-    local = [local_ref[pl.ds(me ^ k, 1), :] for k in range(regions)]
+            vg_ref[k * slots : (k + 1) * slots, :] = mm_dims(ref[at], w1_ref[:feat, :], NT).astype(
+                bf16
+            )
+    listed = [local_ref[pl.ds(me ^ k, 1), :] for k in range(regions)]
     for at in range(0, nets, BLOCK):
-        hot = jnp.concatenate([onehot_cols(row, at, BLOCK) for row in local], 1)
-        total = mm(hot, vg_ref[...])
-        for k in range(near):
-            total = total + mm(onehot_cols(asked_refs[k][...], at, BLOCK), near_rows[k])
-        grad_ref[at : at + BLOCK, :] = total
-        if (at + BLOCK) * 2 % nets == 0:
+        hot = jnp.concatenate([onehot_cols(row, at, BLOCK) for row in listed], 1)
+        grad_ref[at : at + BLOCK, :] += mm(hot, vg_ref[...])
+        if (at + BLOCK) * PARTS % nets == 0:
             grad_ref.flush(at + BLOCK)
-    top = jnp.zeros((feat, hid), f32)
-    low = jnp.zeros((feat, hid), f32)
-    for k in range(regions):
-        top = top + mm_dims(victim_ref[k], lin_grads[k], TT)
-        low = low + mm_dims(partner_refs[k][...], lin_grads[k], TT)
-    both = jnp.concatenate([top, low], 0)
-    short = sums_ref[...]
-    for d in range(devices):
-        out_ref[d] = jnp.concatenate([both[d * share : (d + 1) * share], short], 0).astype(bf16)
 
 
 def layer_grad_kernel(
-    cid_ref, slope_ref, embeds_ref, agg_ref, gnn_ref, halo_ref, grad_ref, *refs, far, peers, degree
+    cid_ref, grad_ref, slope_ref, gnn_ref, embeds_ref, agg_ref, halo_ref, *refs, far, peers, degree
 ):
     asked_refs, refs = refs[:far], refs[far:]
     far_refs, refs = refs[:far], refs[far:]
@@ -256,43 +270,32 @@
     halo = back_refs[0].shape[0]
     top = jnp.zeros((feat, feat), f32)
     low = jnp.zeros((feat, feat), f32)
-    back = jnp.zeros(back_ref.shape, f32)
+    returned = jnp.concatenate([ref[...] for ref in far_refs], 0)
     for at in range(0, nets, STEP):
         rows = pl.ds(at, STEP)
-        total = grad_ref[rows, :]
-        for k in range(far):
-            total = total + mm(onehot_cols(asked_refs[k][...], at, STEP), far_refs[k][...])
+        hot = jnp.concatenate([onehot_cols(ref[...], at, STEP) for ref in asked_refs], 1)
+        total = mm(hot, returned)
+        total = total + grad_ref[rows, :]
         pre_grad = (total * slope_ref[rows, :].astype(f32)).astype(bf16)
         agg_grad = mm_dims(pre_grad, gnn_ref[feat:, :], NT)
         agg_grad = (agg_grad * (1.0 / degree)).astype(bf16)
         agg_grad_ref[rows, :] = agg_grad
-        rest_ref[rows, :] = total + mm_dims(pre_grad, gnn_ref[:feat, :], NT)
+        rest_ref[rows, :] = (total + mm_dims(pre_grad, gnn_ref[:feat, :], NT)).astype(bf16)
         if (at + STEP) * 2 % nets == 0:
             rest_ref.flush(at + STEP)
             agg_grad_ref.flush(at + STEP)
         top = top + mm_dims(embeds_ref[rows, :], pre_grad, TT)
         low = low + mm_dims(agg_ref[rows, :], pre_grad, TT)
-        back = back + mm(halo_ref[at // STEP], agg_grad)
     gnn_out_ref[:feat, :] = top.astype(bf16)
     gnn_out_ref[feat:, :] = low.astype(bf16)
     gnn_out_ref.flush()
+    back = jnp.zeros(back_ref.shape, f32)
+    for at in range(0, nets, STEP):
+        back = back + mm(halo_ref[at // STEP], agg_grad_ref[pl.ds(at, STEP), :])
     back_ref[...] = back.astype(bf16)
     me = cid_ref[0]
     for k, out_ref in enumerate(back_refs):
         out_ref[...] = back_ref[pl.ds(pl.multiple_of((me ^ k) * halo, halo), halo), :]
-
-
-def own_grad_kernel(after_ref, rest_ref, agg_grad_ref, own_ref, out_ref):
-    nets, feat = out_ref.shape
-    for at in range(0, nets, STEP):
-        part = mm(own_ref[at // STEP], agg_grad_ref[pl.ds(at, STEP), :])
-        if at == 0:
-            out_ref[...] = part
-        else:
-            out_ref[...] += part
-    for at in range(0, nets, STEP):
-        rows = pl.ds(at, STEP)
-        out_ref[rows, :] += rest_ref[rows, :]
 
 
 def share_kernel(w1_ref, gnn_ref, wide_ref, short_ref, *, nets_total, doms):
@@ -325,8 +328,8 @@
             gnn_ref.flush((d + 1) * share)
 
 
-def final_kernel(cid_ref, short_ref, send_ref, own_ref, *refs):
-    got_refs, (out_ref, w2_ref, loss_ref) = refs[:-3], refs[-3:]
+def final_kernel(cid_ref, short_ref, send_ref, rest_ref, agg_grad_ref, own_ref, *refs):
+    got_refs, (out_ref, w2_ref, loss_ref, given_ref) = refs[:-4], refs[-4:]
     w2_ref[...] = short_ref[0:1, :]
     loss_ref[...] = short_ref[1:2, :]
     nets = out_ref.shape[0]
@@ -334,10 +337,19 @@
     scale = short_ref[2:3, :]
     got = jnp.concatenate([ref[...] for ref in got_refs], 0)
     sent = [send_ref[pl.ds(me ^ k, 1), :] for k in range(len(got_refs))]
+    given_ref[: got.shape[0], :] = got
+    hots = [
+        jnp.concatenate([onehot_cols(row, at, BLOCK) for row in sent], 1)
+        for at in range(0, nets, BLOCK)
+    ]
+    given_ref[got.shape[0] :, :] = agg_grad_ref[...]
     for at in range(0, nets, BLOCK):
-        hot = jnp.concatenate([onehot_cols(row, at, BLOCK) for row in sent], 1)
-        total = own_ref[at : at + BLOCK, :] + mm(hot, got)
-        out_ref[at : at + BLOCK, :] = (total * scale).astype(bf16)
+        rows = pl.ds(at, BLOCK)
+        parts = [own_ref[i, rows, :] for i in range(own_ref.shape[0])]
+        total = mm(jnp.concatenate([hots[at // BLOCK]] + parts, 1), given_ref[...])
+        out_ref[rows, :] = ((total + rest_ref[rows, :]) * scale).astype(bf16)
+        if (at + BLOCK) * PARTS % nets == 0:
+            out_ref.flush(at + BLOCK)
 
 
 SM = pl.BlockSpec(memory_space=pltpu.SMEM)
@@ -356,29 +368,18 @@
 
 
 class Load:
-    def __init__(self, source, target, sems):
-        self.target, self.waited = target, 0
-        self.shape = source.shape
-        size = math.prod(source.shape) * jnp.dtype(source.dtype).itemsize
-        parts = PARTS if size > 1 << 20 else 2 if size > 1 << 19 else 1
-        self.rows = max(source.shape[0] // parts, 1)
-        self.copies = []
-        for at in range(source.shape[0] // self.rows):
-            part = pl.ds(at * self.rows, self.rows)
-            self.copies.append(
-                pltpu.make_async_copy(source.at[part], target.at[part], sems.at[at])
-            )
+    def __init__(self, source, target, sem):
+        self.target, self.shape, self.waited = target, source.shape, False
+        self.copy = pltpu.make_async_copy(source, target, sem)
+        self.copy.start()
+
+    def wait(self):
+        if not self.waited:
+            self.copy.wait()
+        self.waited = True
 
     def __getitem__(self, index):
-        first = index[0] if isinstance(index, tuple) else index
-        last = self.shape[0]
-        if isinstance(first, int):
-            last = first + 1
-        elif isinstance(first, pl.Slice):
-            last = first.start + first.size
-        while self.waited < -(-last // self.rows):
-            self.copies[self.waited].wait()
-            self.waited += 1
+        self.wait()
         return self.target[index]
 
 
@@ -428,18 +429,16 @@
         at = 0
         for i, kind in enumerate(ins):
             if kind == "H":
-                operands[i] = Load(operands[i], buffers[at], sems.at[at])
+                operands[i] = Load(operands[i], buffers[at], sems.at[at, 0])
                 at += 1
-        loads = [operand for operand in operands if isinstance(operand, Load)]
-        for part in range(PARTS):
-            for load in loads:
-                if part < len(load.copies):
-                    load.copies[part].start()
         for i, kind in enumerate(kinds):
             if kind == "H":
                 results[i] = Store(buffers[at], results[i], sems.at[at])
                 at += 1
         kernel(*operands, *results, *refs)
+        for operand in operands:
+            if isinstance(operand, Load):
+                operand.wait()
         for result in results:
             if isinstance(result, Store):
                 result.finish()
@@ -511,7 +510,7 @@
         halo_gather_kernel,
         "halo_gather",
         out("V", bf16, halo_rows, feat),
-        v(halo_send) + h(embeds),
+        h(halo_send, embeds),
     )
     received = exchange(outgoing.reshape(peers, halo, feat), "dom").reshape(halo_rows, feat)
 
@@ -549,7 +548,8 @@
         + out("H", bf16, nets, feat)
         + out("V", bf16, nets, feat)
         + out("V", bf16, slots, feat) * far,
-        h(from_halo, agg_sum, embeds, gnn_weight) + v(received, *asked[near:]),
+        h(from_halo, agg_sum) + v(embeds, gnn_weight, received, *asked[near:]),
+        [pltpu.VMEM((far, slots, nets), bf16)],
     )
     victim, linear_own, slope, *near_sends = call(
         functools.partial(victim_kernel, near=near),
@@ -565,20 +565,22 @@
     partners += [permute(near_sends[k], k) for k in range(1, near)]
     partners += [permute(far_sends[k - near], k) for k in range(near, regions)]
 
-    groups = [(k,) for k in range(near, regions)] + [tuple(range(near))]
+    groups = [tuple(range(near, regions)), tuple(range(near))]
     w2_row = pair_w2.reshape(1, hid)
     lin_grads, backs, sums = [], {}, []
     for ks in groups:
-        pieces = 2 if ks[0] < near else 1
+        last = ks is groups[-1]
+        pieces = 2 if last else 1
         lin_grad, sums_now, *back = call(
-            functools.partial(pair_kernel, ks=ks, first=ks is groups[0], last=ks is groups[-1]),
+            functools.partial(pair_kernel, ks=ks, first=ks is groups[0], last=last),
             "pairs",
             out("H", bf16, len(ks), slots, hid)
-            + out("V", f32, 8, hid)
+            + (out("V", bf16, devices, share + 8, hid) if last else out("V", f32, 8, hid))
             + out("V", bf16, slots // pieces, feat) * (pieces * len(ks)),
             [(rid, "S"), (pair_count, "S")]
             + v(targets, linear_own, pair_w1, w2_row)
             + v(*[partners[k] for k in ks])
+            + (h(victim, *partners[near:], *lin_grads) if last else [])
             + v(*sums),
             flops=PAIRS,
         )
@@ -588,55 +590,55 @@
         sums = [sums_now]
     returned = [backs[0]] + [[permute(x, k) for x in backs[k]] for k in range(1, regions)]
 
-    local_grad, w1_parts = call(
+    (w1_parts,) = sums
+    w1_got = exchange(w1_parts, BOTH)
+    (local_grad,) = call(
         functools.partial(local_grad_kernel, groups=groups, near=near),
         "local_grads",
-        out("H", f32, nets, feat) + out("V", bf16, devices, share + 8, hid),
+        out("H", f32, nets, feat),
         [(rid, "S")]
         + v(pair_local)
         + h(pair_w1)
-        + v(sums[0], *asked[:near], *sum(returned[:near], []))
-        + h(*lin_grads, *partners, victim),
+        + [(w1_parts, "A")]
+        + v(*asked[:near], *sum(returned[:near], []))
+        + h(*lin_grads),
         [pltpu.VMEM((regions * slots, feat), bf16)],
-    )
-    w1_got = exchange(w1_parts, BOTH)
-
+        flops=LOCAL,
+    )
     rest, agg_grad, gnn_part, *backs = call(
         functools.partial(layer_grad_kernel, far=far, peers=peers, degree=degree),
         "layer_grad",
-        out("H", f32, nets, feat)
-        + out("H", bf16, nets, feat)
+        out("H", bf16, nets, feat) * 2
         + out("H", bf16, 2 * feat, feat)
         + out("V", bf16, halo, feat) * peers,
         [(cid, "S")]
-        + h(slope, embeds, aggregate, gnn_weight, from_halo, local_grad)
+        + h(local_grad, slope)
+        + v(gnn_weight, embeds)
+        + h(aggregate, from_halo)
         + v(*asked[near:], *sum(returned[near:], [])),
         [pltpu.VMEM((halo_rows, feat), bf16)],
         flops=10**10,
     )
     gnn_part, w1_got = lax.optimization_barrier((gnn_part, w1_got))
     gnn_got = exchange(gnn_part.reshape(devices, share, feat), BOTH)
-    returned_halo = [backs[0]] + [permute(backs[k], k, "dom") for k in range(1, peers)]
+    returned_halo = {k: permute(backs[k], k, "dom") for k in range(peers - 1, 0, -1)}
+    returned_halo = [backs[0]] + [returned_halo[k] for k in range(1, peers)]
 
     wide, short = call(
         functools.partial(share_kernel, nets_total=nets * devices, doms=peers),
         "shares",
         out("V", bf16, devices, share, feat) + out("V", f32, 8, hid),
         v(w1_got, gnn_got),
+        flops=SHARES,
     )
     spread = exchange(wide, BOTH)
 
-    (own_grad,) = call(
-        own_grad_kernel,
-        "own_grads",
-        out("V", f32, nets, feat),
-        [(short, "A")] + h(rest, agg_grad, own),
-    )
     embeds_grad, w2_grad, loss = call(
         final_kernel,
         "embeds_grads",
-        out("V", bf16, nets, feat) + out("V", f32, 1, hid) * 2,
-        [(cid, "S")] + v(short, halo_send, own_grad, *returned_halo),
+        out("H", bf16, nets, feat) + out("V", f32, 1, hid) * 2,
+        [(cid, "S")] + v(short, halo_send) + h(rest, agg_grad, own) + v(*returned_halo),
+        [pltpu.VMEM((halo_rows + nets, feat), bf16)],
         flops=FINAL,
     )
     spread, w2_grad = lax.optimization_barrier((spread, w2_grad))

time: 116 us -> 111 us (0.957)
  Pallas kernels: 65.9 us -> 58.4 us
  starting transfers between devices: 38.2 us -> 42.6 us
    pallas_call x12 -> x10, Pallas kernels: 57.3 us -> 49.8 us  [call(): pl.pallas_call(body, out_shape=[(in_hbm if kind == 'H' else shape)(dims,...]
    all_to_all x4, starting transfers between devices: 18.4 us -> 22.3 us  [exchange(): return lax.all_to_all(value, axis, split_axis=0, concat_axis=0, tiled=True)]
    all_to_all x4, waiting for transfers between devices: 6.63 us -> 3.91 us  [exchange(): return lax.all_to_all(value, axis, split_axis=0, concat_axis=0, tiled=True)]
    ppermute x18, waiting for transfers between devices: 2.1 us -> 4.36 us  [permute(): return lax.ppermute(value, axis, [(i, i ^ k) for i in range(size)])]
  transfers between devices with their start and end apart: 22 -> 22, of which waited for: 6 -> 5; matrix products, arithmetic and copies ran while one was open for 0% -> 0% of each run, Pallas kernels for 53% -> 48%
where the time goes in v4:
time: 111 us
  Pallas kernels  58.4 us (53%)
  starting transfers between devices  42.6 us (38%)
  waiting for transfers between devices  8.27 us (7%)
  between operations  1.11 us (1%)
    pallas_call x10, Pallas kernels, call(): pl.pallas_call(body, out_shape=[(in_hbm if kind == 'H' else shape)(dims,...  49.8 us
    all_to_all x4, starting transfers between devices, exchange(): return lax.all_to_all(value, axis, split_axis=0, concat_axis=0, tiled=True)  22.3 us
    ppermute x18, starting transfers between devices, permute(): return lax.ppermute(value, axis, [(i, i ^ k) for i in range(size)])  20.3 us
    pallas_call x1, Pallas kernels, local(): pl.pallas_call(adjacency_kernel, grid=(steps,), in_specs=[pl.BlockSpec((d...  8.57 us
    ppermute x18, waiting for transfers between devices, permute(): return lax.ppermute(value, axis, [(i, i ^ k) for i in range(size)])  4.36 us
    all_to_all x4, waiting for transfers between devices, exchange(): return lax.all_to_all(value, axis, split_axis=0, concat_axis=0, tiled=True)  3.91 us
  transfers between devices with their start and end apart: 22, of which 5 were waited for; matrix products, arithmetic and copies ran while one was open for 0% of the time, Pallas kernels for 48%

profile of v4, /device:TPU:0, one launch (start us, length us, event | category | flops | bytes accessed | tf_op | source)
XLA Modules:
  0.0 110.9 jit_solution(17693930932752722777)
XLA Ops:
  0.7 3.5 %halo_gather.1 = bf16[1024,256]{1,0:T(8,128)(2,1)} custom-call(s32[8,128]{1,0:T(8,128)} %refs_2_.9, bf16[2048,256]{1,0:T(8,128)(2,1)} %refs_4_.5), custom_call_target="tpu_custom_call" | custom-call | flops 1 | bytes 1 | tf_op jit(solution)/shard_map/halo_gather/pallas_call | solution.py:447
  4.2 7.3 %all-to-all-start = ((bf16[8,128,256]{2,1,0:T(8,128)(2,1)}), bf16[8,128,256]{2,1,0:T(8,128)(2,1)S(1)}, u32[]{:S(2)}, u32[]{:S(2)}) async-start(bf16[8,128,256]{2,1,0:T(8,128)(2,1)} %bitcast.3), calls=%async_computation | async-start | bytes 1048576 | tf_op jit(solution)/shard_map/all_to_all | solution.py:467
  11.5 1.6 %collective-permute-start = (s32[1,512]{1,0:T(1,128)S(1)}, s32[1,512]{1,0:T(1,128)S(1)}, u32[]{:S(2)}, u32[]{:S(2)}) collective-permute-start(s32[1,512]{1,0:T(1,128)S(1)} %get-tuple-element.97), channel_id=1, source_target_pairs={{0,16},{8,24},{16,0},{24,8},{1,17},{9,25},{17,1},{25,9},{2,18},{10... | collective-permute-start | bytes 6152 | tf_op jit(solution)/shard_map/ppermute | solution.py:498
  13.1 0.6 collective-permute-start.2
  13.7 8.6 %adjacency.1 = (bf16[4,2048,512]{2,1,0:T(8,128)(2,1)}, bf16[4,1024,512]{2,1,0:T(8,128)(2,1)}, f32[2048,256]{1,0:T(8,128)}) custom-call(s32[8,2048]{1,0:T(8,128)S(1)} %bitcast.9, bf16[2048,256]{1,0:T(8,128)(2,1)S(1)} %copy-done), custom_call_target="tpu_custom_call" | custom-call | flops 1 | bytes 1 | tf_op jit(solution)/shard_map/adjacency/pallas_call | solution.py:521
  22.3 0.0 collective-permute-done.refs_5_.refs_7_
  22.3 0.0 collective-permute-done.1.refs_6_.refs_8_
  22.3 3.7 %all-to-all-done = bf16[8,128,256]{2,1,0:T(8,128)(2,1)S(1)} async-done(((bf16[8,128,256]{2,1,0:T(8,128)(2,1)}), bf16[8,128,256]{2,1,0:T(8,128)(2,1)S(1)}, u32[]{:S(2)}, u32[]{:S(2)}) %all-to-all-start) | async-done | bytes 524320 | tf_op jit(solution)/shard_map/all_to_all | solution.py:467
  26.0 7.3 %layer.1 = (f32[2048,256]{1,0:T(8,128)S(1)}, bf16[2048,256]{1,0:T(8,128)(2,1)}, bf16[2048,256]{1,0:T(8,128)(2,1)S(1)}, bf16[512,256]{1,0:T(8,128)(2,1)S(1)}, bf16[512,256]{1,0:T(8,128)(2,1)S(1)}) custom-call(bf16[4,1024,512]{2,1,0:T(8,128)(2,1)} %get-tuple-element.50.refs_0_.refs_6_, f32[2048,256]{1,0:T(8,128)} %get-tuple-element.51.refs_1_, ...), custom_call_target="tpu_custom_call" | custom-call | flops 1 | bytes 1 | tf_op jit(solution)/shard_map/layer/pallas_call | solution.py:447
  33.3 1.6 %collective-permute-start.4 = (bf16[512,256]{1,0:T(8,128)(2,1)S(1)}, bf16[512,256]{1,0:T(8,128)(2,1)S(1)}, u32[]{:S(2)}, u32[]{:S(2)}) collective-permute-start(bf16[512,256]{1,0:T(8,128)(2,1)S(1)} %get-tuple-element.58), channel_id=1, source_target_pairs={{0,16},{8,24},{16,0},{24,8},{1,17},{9,25},{17,1},{25,9},{2,18},{10... | collective-permute-start | bytes 786440 | tf_op jit(solution)/shard_map/ppermute | solution.py:498
  34.8 0.0 copy-start.11
  34.9 0.0 copy-start.2
  34.9 0.0 copy-start.8
  34.9 0.0 copy-start.9
  34.9 7.0 %victims.1 = (bf16[4,512,256]{2,1,0:T(8,128)(2,1)}, f32[4,512,256]{2,1,0:T(8,128)S(1)}, bf16[2048,256]{1,0:T(8,128)(2,1)}, bf16[512,256]{1,0:T(8,128)(2,1)S(1)}, bf16[512,256]{1,0:T(8,128)(2,1)S(1)}) custom-call(s32[1]{0:T(128)} %bitcast.1.refs_0_, s32[4,512]{1,0:T(4,128)S(1)} %copy-done.4, bf16[2048,256]{1,0:T(8,128)(2,1)S(1)} %get-tuple-element.52.refs_2_, ...), custom_call_target="tpu_custom_call" | custom-call | flops 10000000000 | bytes 1 | tf_op jit(solution)/shard_map/victims/pallas_call | solution.py:447
  41.9 0.7 collective-permute-start.3
  42.7 2.0 %collective-permute-done.5.refs_7_.refs_10_ = bf16[512,256]{1,0:T(8,128)(2,1)S(1)} collective-permute-done((bf16[512,256]{1,0:T(8,128)(2,1)S(1)}, bf16[512,256]{1,0:T(8,128)(2,1)S(1)}, u32[]{:S(2)}, u32[]{:S(2)}) %collective-permute-start.5) | collective-permute-done | bytes 262176 | tf_op jit(solution)/shard_map/ppermute | solution.py:498
  44.7 2.5 %pairs.2 = (bf16[2,512,256]{2,1,0:T(8,128)(2,1)}, f32[8,256]{1,0:T(8,128)S(1)}, bf16[512,256]{1,0:T(8,128)(2,1)S(1)}, bf16[512,256]{1,0:T(8,128)(2,1)S(1)}) custom-call(s32[1]{0:T(128)} %bitcast.1.refs_0_, s32[1,4]{1,0:T(1,128)S(1)} %copy-done.9, f32[4,512]{1,0:T(4,128)S(1)} %copy-done.8, f32[4,512,256]{2,1,0:T(8,128)S(1)} %get-tuple-element.54.refs_3_, ...), custom_call_target="tpu_custom_call" | custom-call | flops 2000000000 | bytes 1 | tf_op jit(solution)/shard_map/pairs/pallas_call | solution.py:447
  47.2 0.6 collective-permute-start.8
  47.8 1.6 %collective-permute-start.9 = (bf16[512,256]{1,0:T(8,128)(2,1)S(1)}, bf16[512,256]{1,0:T(8,128)(2,1)S(1)}, u32[]{:S(2)}, u32[]{:S(2)}) collective-permute-start(bf16[512,256]{1,0:T(8,128)(2,1)S(1)} %get-tuple-element.71), channel_id=1, source_target_pairs={{0,24},{8,16},{16,8},{24,0},{1,25},{9,17},{17,9},{25,1},{2,26},{10... | collective-permute-start | bytes 786440 | tf_op jit(solution)/shard_map/ppermute | solution.py:498
  49.4 0.0 collective-permute-done.3.refs_7_
  49.4 4.6 %pairs.3 = (bf16[2,512,256]{2,1,0:T(8,128)(2,1)}, bf16[32,24,256]{2,1,0:T(8,128)(2,1)}, bf16[256,256]{1,0:T(8,128)(2,1)S(1)}, bf16[256,256]{1,0:T(8,128)(2,1)S(1...) custom-call(s32[1]{0:T(128)} %bitcast.1.refs_0_, s32[1,4]{1,0:T(1,128)S(1)} %copy-done.9, ...), custom_call_target="tpu_custom_call" | custom-call | flops 2000000000 | bytes 1 | tf_op jit(solution)/shard_map/pairs/pallas_call | solution.py:447
  54.1 0.1 collective-permute-start.6
  54.1 0.5 collective-permute-start.7
  54.6 5.2 %all-to-all-start.1 = ((bf16[32,24,256]{2,1,0:T(8,128)(2,1)}), bf16[32,24,256]{2,1,0:T(8,128)(2,1)S(1)}, u32[]{:S(2)}, u32[]{:S(2)}) async-start(bf16[32,24,256]{2,1,0:T(8,128)(2,1)} %get-tuple-element.62.refs_3_), calls=%async_computation.1 | async-start | bytes 786432 | tf_op jit(solution)/shard_map/all_to_all | solution.py:467
  59.8 0.0 collective-permute-done.7.refs_9_
  59.8 6.2 %local_grads.1.refs_1_ = f32[2048,256]{1,0:T(8,128)} custom-call(s32[1]{0:T(128)} %bitcast.1.refs_0_, s32[4,512]{1,0:T(4,128)S(1)} %copy-done.4, bf16[512,256]{1,0:T(8,128)(2,1)} %refs_2_.8, bf16[32,24,256]{2,1,0:T(8,128)(2,1)} %get-tuple-element.62.refs_3_, s32[1,512]{1,0:T(1,128)S(1)} %get-tuple-element.98.refs_5_.refs_4_, ...), custom_call_target="tpu_custom_call" | custom-call | flops 1 | bytes 1 | tf_op jit(solution)/shard_map/local_grads/pallas_call | solution.py:447
  66.0 0.0 collective-permute-done.8.refs_9_
  66.0 0.0 copy-start.5
  66.0 7.7 %layer_grad.1 = (bf16[2048,256]{1,0:T(8,128)(2,1)}, bf16[2048,256]{1,0:T(8,128)(2,1)}, bf16[512,256]{1,0:T(8,128)(2,1)}, bf16[128,256]{1,0:T(8,128)(2,1)S(1)}, b...) custom-call(s32[1]{0:T(128)} %bitcast.refs_0_, ...), custom_call_target="tpu_custom_call" | custom-call | flops 10000000000 | bytes 1 | tf_op jit(solution)/shard_map/layer_grad/pallas_call | solution.py:447
  73.7 0.0 all-to-all-done.1.refs_0_
  73.7 5.8 %all-to-all-start.2 = ((bf16[32,16,256]{2,1,0:T(8,128)(2,1)}), bf16[32,16,256]{2,1,0:T(8,128)(2,1)S(1)}, u32[]{:S(2)}, u32[]{:S(2)}) async-start(bf16[32,16,256]{2,1,0:T(8,128)(2,1)} %bitcast.10), calls=%async_computation.2 | async-start | bytes 524288 | tf_op jit(solution)/shard_map/all_to_all | solution.py:467
  79.6 1.8 %collective-permute-start.10 = (bf16[128,256]{1,0:T(8,128)(2,1)S(1)}, bf16[128,256]{1,0:T(8,128)(2,1)S(1)}, u32[]{:S(2)}, u32[]{:S(2)}) collective-permute-start(bf16[128,256]{1,0:T(8,128)(2,1)S(1)} %get-tuple-element.80), channel_id=1, source_target_pairs={{0,1},{1,0},{2,3},{3,2},{4,5},{5,4},{6,7},{7,6},{8,9},{9,8},{10,11... | collective-permute-start | bytes 196616 | tf_op jit(solution)/shard_map/ppermute | solution.py:498
  81.4 1.5 %collective-permute-start.11 = (bf16[128,256]{1,0:T(8,128)(2,1)S(1)}, bf16[128,256]{1,0:T(8,128)(2,1)S(1)}, u32[]{:S(2)}, u32[]{:S(2)}) collective-permute-start(bf16[128,256]{1,0:T(8,128)(2,1)S(1)} %get-tuple-element.81), channel_id=1, source_target_pairs={{0,2},{1,3},{2,0},{3,1},{4,6},{5,7},{6,4},{7,5},{8,10},{9,11},{10,... | collective-permute-start | bytes 196616 | tf_op jit(solution)/shard_map/ppermute | solution.py:498
  82.9 0.3 collective-permute-start.12
  83.1 2.7 %collective-permute-start.13 = (bf16[128,256]{1,0:T(8,128)(2,1)S(1)}, bf16[128,256]{1,0:T(8,128)(2,1)S(1)}, u32[]{:S(2)}, u32[]{:S(2)}) collective-permute-start(bf16[128,256]{1,0:T(8,128)(2,1)S(1)} %get-tuple-element.83), channel_id=1, source_target_pairs={{0,4},{1,5},{2,6},{3,7},{4,0},{5,1},{6,2},{7,3},{8,12},{9,13},{10,... | collective-permute-start | bytes 196616 | tf_op jit(solution)/shard_map/ppermute | solution.py:498
  85.8 1.5 %collective-permute-start.14 = (bf16[128,256]{1,0:T(8,128)(2,1)S(1)}, bf16[128,256]{1,0:T(8,128)(2,1)S(1)}, u32[]{:S(2)}, u32[]{:S(2)}) collective-permute-start(bf16[128,256]{1,0:T(8,128)(2,1)S(1)} %get-tuple-element.84), channel_id=1, source_target_pairs={{0,5},{1,4},{2,7},{3,6},{4,1},{5,0},{6,3},{7,2},{8,13},{9,12},{10,... | collective-permute-start | bytes 196616 | tf_op jit(solution)/shard_map/ppermute | solution.py:498
  87.3 0.0 collective-permute-done.10.refs_7_
  87.3 3.3 %collective-permute-start.15 = (bf16[128,256]{1,0:T(8,128)(2,1)S(1)}, bf16[128,256]{1,0:T(8,128)(2,1)S(1)}, u32[]{:S(2)}, u32[]{:S(2)}) collective-permute-start(bf16[128,256]{1,0:T(8,128)(2,1)S(1)} %get-tuple-element.85), channel_id=1, source_target_pairs={{0,6},{1,7},{2,4},{3,5},{4,2},{5,3},{6,0},{7,1},{8,14},{9,15},{10,... | collective-permute-start | bytes 196616 | tf_op jit(solution)/shard_map/ppermute | solution.py:498
  90.6 2.0 %collective-permute-start.16 = (bf16[128,256]{1,0:T(8,128)(2,1)S(1)}, bf16[128,256]{1,0:T(8,128)(2,1)S(1)}, u32[]{:S(2)}, u32[]{:S(2)}) collective-permute-start(bf16[128,256]{1,0:T(8,128)(2,1)S(1)} %get-tuple-element.86), channel_id=1, source_target_pairs={{0,7},{1,6},{2,5},{3,4},{4,3},{5,2},{6,1},{7,0},{8,15},{9,14},{10,... | collective-permute-start | bytes 196616 | tf_op jit(solution)/shard_map/ppermute | solution.py:498
  92.6 0.8 shares.1
  93.4 4.0 %all-to-all-start.3 = ((bf16[32,16,256]{2,1,0:T(8,128)(2,1)}), bf16[32,16,256]{2,1,0:T(8,128)(2,1)S(1)}, u32[]{:S(2)}, u32[]{:S(2)}) async-start(bf16[32,16,256]{2,1,0:T(8,128)(2,1)} %get-tuple-element.88), calls=%async_computation.3 | async-start | bytes 524288 | tf_op jit(solution)/shard_map/all_to_all | solution.py:467
  97.5 1.3 %collective-permute-done.14.refs_11_ = bf16[128,256]{1,0:T(8,128)(2,1)S(1)} collective-permute-done((bf16[128,256]{1,0:T(8,128)(2,1)S(1)}, bf16[128,256]{1,0:T(8,128)(2,1)S(1)}, u32[]{:S(2)}, u32[]{:S(2)}) %collective-permute-start.14) | collective-permute-done | bytes 65568 | tf_op jit(solution)/shard_map/ppermute | solution.py:498
  98.8 9.1 %embeds_grads.1 = (bf16[2048,256]{1,0:T(8,128)(2,1)}, f32[1,256]{1,0:T(1,128)}, f32[1,256]{1,0:T(1,128)S(1)}) custom-call(s32[1]{0:T(128)} %bitcast.refs_0_, f32[8,256]{1,0:T(8,128)S(1)} %get-tuple-element.75.refs_1_, s32[8,128]{1,0:T(8,128)S(1)} %copy-done.5, bf16[2048,256]{1,0:T(8,128)(2,1)} %get-tuple-element.76.refs_3_, ...), custom_call_target="tpu_custom_call" | custom-call | flops 20000000000 | bytes 1 | tf_op jit(solution)/shard_map/embeds_grads/pallas_call | solution.py:447
  107.9 0.2 all-to-all-done.3.refs_1_
  108.1 0.5 slice.3
  108.6 1.0 collective-permute-done.17.refs_2_
  109.6 1.1 %unpack.1 = (f32[512,256]{1,0:T(8,128)}, f32[512,256]{1,0:T(8,128)}) custom-call(s32[1]{0:T(128)} %bitcast.1.refs_0_, bf16[32,16,256]{2,1,0:T(8,128)(2,1)S(1)} %all-to-all-done.3.refs_1_, bf16[32,16,256]{2,1,0:T(8,128)(2,1)S(1)} %collective-permute-done.17.refs_2_), custom_call_target="tpu_custom_call" | custom-call | flops 1 | bytes 1 | tf_op jit(solution)/shard_map/unpack/pallas_call | solution.py:447
  (34 shorter events, 0.1 us)
Async XLA Ops:
  0.6 13.1 %copy-start = (bf16[2048,256]{1,0:T(8,128)(2,1)S(1)}, bf16[2048,256]{1,0:T(8,128)(2,1)}, u32[]{:S(2)}) copy-start(bf16[2048,256]{1,0:T(8,128)(2,1)} %refs_4_.5) | copy-start | bytes 3145732
  0.6 10.9 %copy-start.10 = (s32[4,512]{1,0:T(4,128)S(1)}, s32[4,512]{1,0:T(4,128)}, u32[]{:S(2)}) copy-start(s32[4,512]{1,0:T(4,128)} %param.15) | copy-start | bytes 24580
  0.7 13.1 %copy-start.3 = (s32[2048,8]{0,1:T(8,128)S(1)}, s32[2048,8]{0,1:T(8,128)}, u32[]{:S(2)}) copy-start(s32[2048,8]{0,1:T(8,128)} %param.11) | copy-start | bytes 196612
  0.7 25.3 %copy-start.1 = (bf16[512,256]{1,0:T(8,128)(2,1)S(1)}, bf16[512,256]{1,0:T(8,128)(2,1)}, u32[]{:S(2)}) copy-start(bf16[512,256]{1,0:T(8,128)(2,1)} %refs_3_.5) | copy-start | bytes 786436
  4.2 21.8 %all-to-all-start = ((bf16[8,128,256]{2,1,0:T(8,128)(2,1)}), bf16[8,128,256]{2,1,0:T(8,128)(2,1)S(1)}, u32[]{:S(2)}, u32[]{:S(2)}) async-start(bf16[8,128,256]{2,1,0:T(8,128)(2,1)} %bitcast.3), calls=%async_computation | async-start | bytes 1048576 | tf_op jit(solution)/shard_map/all_to_all | solution.py:467
  11.5 10.8 %collective-permute-start = (s32[1,512]{1,0:T(1,128)S(1)}, s32[1,512]{1,0:T(1,128)S(1)}, u32[]{:S(2)}, u32[]{:S(2)}) collective-permute-start(s32[1,512]{1,0:T(1,128)S(1)} %get-tuple-element.97), channel_id=1, source_target_pairs={{0,16},{8,24},{16,0},{24,8},{1,17},{9,25},{17,1},{25,9},{2,18},{10... | collective-permute-start | bytes 6152 | tf_op jit(solution)/shard_map/ppermute | solution.py:498
  13.1 9.2 %collective-permute-start.1 = (s32[1,512]{1,0:T(1,128)S(1)}, s32[1,512]{1,0:T(1,128)S(1)}, u32[]{:S(2)}, u32[]{:S(2)}) collective-permute-start(s32[1,512]{1,0:T(1,128)S(1)} %get-tuple-element.96), channel_id=1, source_target_pairs={{0,24},{8,16},{16,8},{24,0},{1,25},{9,17},{17,9},{25,1},{2,26},{10... | collective-permute-start | bytes 6152 | tf_op jit(solution)/shard_map/ppermute | solution.py:498
  13.1 21.8 %collective-permute-start.2 = (s32[1,512]{1,0:T(1,128)S(1)}, s32[1,512]{1,0:T(1,128)S(1)}, u32[]{:S(2)}, u32[]{:S(2)}) collective-permute-start(s32[1,512]{1,0:T(1,128)S(1)} %get-tuple-element.95), channel_id=1, source_target_pairs={{0,8},{8,0},{16,24},{24,16},{1,9},{9,1},{17,25},{25,17},{2,10},{10... | collective-permute-start | bytes 6152 | tf_op jit(solution)/shard_map/ppermute | solution.py:498
  26.0 8.9 %copy-start.4 = (s32[4,512]{1,0:T(4,128)S(1)}, s32[4,512]{1,0:T(4,128)}, u32[]{:S(2)}) copy-start(s32[4,512]{1,0:T(4,128)} %refs_1_.9) | copy-start | bytes 24580
  33.3 9.4 %collective-permute-start.4 = (bf16[512,256]{1,0:T(8,128)(2,1)S(1)}, bf16[512,256]{1,0:T(8,128)(2,1)S(1)}, u32[]{:S(2)}, u32[]{:S(2)}) collective-permute-start(bf16[512,256]{1,0:T(8,128)(2,1)S(1)} %get-tuple-element.58), channel_id=1, source_target_pairs={{0,16},{8,24},{16,0},{24,8},{1,17},{9,25},{17,1},{25,9},{2,18},{10... | collective-permute-start | bytes 786440 | tf_op jit(solution)/shard_map/ppermute | solution.py:498
  34.8 9.8 %collective-permute-start.5 = (bf16[512,256]{1,0:T(8,128)(2,1)S(1)}, bf16[512,256]{1,0:T(8,128)(2,1)S(1)}, u32[]{:S(2)}, u32[]{:S(2)}) collective-permute-start(bf16[512,256]{1,0:T(8,128)(2,1)S(1)} %get-tuple-element.59), channel_id=1, source_target_pairs={{0,24},{8,16},{16,8},{24,0},{1,25},{9,17},{17,9},{25,1},{2,26},{10... | collective-permute-start | bytes 786440 | tf_op jit(solution)/shard_map/ppermute | solution.py:498
  34.8 7.8 %copy-start.11 = (bf16[256]{0:T(256)(128)(2,1)S(1)}, bf16[256]{0:T(256)(128)(2,1)}, u32[]{:S(2)}) copy-start(bf16[256]{0:T(256)(128)(2,1)} %param.19) | copy-start | bytes 1540
  34.9 9.8 %copy-start.2 = (bf16[512,256]{1,0:T(8,128)(2,1)S(1)}, bf16[512,256]{1,0:T(8,128)(2,1)}, u32[]{:S(2)}) copy-start(bf16[512,256]{1,0:T(8,128)(2,1)} %refs_2_.8) | copy-start | bytes 786436
  34.9 9.8 %copy-start.8 = (f32[4,512]{1,0:T(4,128)S(1)}, f32[4,512]{1,0:T(4,128)}, u32[]{:S(2)}) copy-start(f32[4,512]{1,0:T(4,128)} %refs_2_.7) | copy-start | bytes 24580
  34.9 9.8 %copy-start.9 = (s32[1,4]{1,0:T(1,128)S(1)}, s32[1,4]{1,0:T(1,128)}, u32[]{:S(2)}) copy-start(s32[1,4]{1,0:T(1,128)} %refs_1_.8) | copy-start | bytes 52
  41.9 7.5 %collective-permute-start.3 = (bf16[512,256]{1,0:T(8,128)(2,1)S(1)}, bf16[512,256]{1,0:T(8,128)(2,1)S(1)}, u32[]{:S(2)}, u32[]{:S(2)}) collective-permute-start(bf16[512,256]{1,0:T(8,128)(2,1)S(1)} %get-tuple-element.56), channel_id=1, source_target_pairs={{0,8},{8,0},{16,24},{24,16},{1,9},{9,1},{17,25},{25,17},{2,10},{10... | collective-permute-start | bytes 786440 | tf_op jit(solution)/shard_map/ppermute | solution.py:498
  42.7 4.5 %copy-start.6 = (bf16[512,256]{1,0:T(8,128)(2,1)}, bf16[512,256]{1,0:T(8,128)(2,1)S(1)}, u32[]{:S(2)}) copy-start(bf16[512,256]{1,0:T(8,128)(2,1)S(1)} %collective-permute-done.4.refs_6_.refs_9_) | copy-start | bytes 786436
  44.7 2.5 %copy-start.7 = (bf16[512,256]{1,0:T(8,128)(2,1)}, bf16[512,256]{1,0:T(8,128)(2,1)S(1)}, u32[]{:S(2)}) copy-start(bf16[512,256]{1,0:T(8,128)(2,1)S(1)} %collective-permute-done.5.refs_7_.refs_10_) | copy-start | bytes 786436
  47.2 18.8 %collective-permute-start.8 = (bf16[512,256]{1,0:T(8,128)(2,1)S(1)}, bf16[512,256]{1,0:T(8,128)(2,1)S(1)}, u32[]{:S(2)}, u32[]{:S(2)}) collective-permute-start(bf16[512,256]{1,0:T(8,128)(2,1)S(1)} %get-tuple-element.70), channel_id=1, source_target_pairs={{0,16},{8,24},{16,0},{24,8},{1,17},{9,25},{17,1},{25,9},{2,18},{10... | collective-permute-start | bytes 786440 | tf_op jit(solution)/shard_map/ppermute | solution.py:498
  47.8 18.2 %collective-permute-start.9 = (bf16[512,256]{1,0:T(8,128)(2,1)S(1)}, bf16[512,256]{1,0:T(8,128)(2,1)S(1)}, u32[]{:S(2)}, u32[]{:S(2)}) collective-permute-start(bf16[512,256]{1,0:T(8,128)(2,1)S(1)} %get-tuple-element.71), channel_id=1, source_target_pairs={{0,24},{8,16},{16,8},{24,0},{1,25},{9,17},{17,9},{25,1},{2,26},{10... | collective-permute-start | bytes 786440 | tf_op jit(solution)/shard_map/ppermute | solution.py:498
  54.1 5.8 %collective-permute-start.6 = (bf16[256,256]{1,0:T(8,128)(2,1)}, bf16[256,256]{1,0:T(8,128)(2,1)S(1)}, u32[]{:S(2)}, u32[]{:S(2)}) collective-permute-start(bf16[256,256]{1,0:T(8,128)(2,1)} %get-tuple-element.65), channel_id=1, source_target_pairs={{0,8},{8,0},{16,24},{24,16},{1,9},{9,1},{17,25},{25,17},{2,10},{10... | collective-permute-start | bytes 393224 | tf_op jit(solution)/shard_map/ppermute | solution.py:498
  54.1 5.7 %collective-permute-start.7 = (bf16[256,256]{1,0:T(8,128)(2,1)S(1)}, bf16[256,256]{1,0:T(8,128)(2,1)S(1)}, u32[]{:S(2)}, u32[]{:S(2)}) collective-permute-start(bf16[256,256]{1,0:T(8,128)(2,1)S(1)} %get-tuple-element.66), channel_id=1, source_target_pairs={{0,8},{8,0},{16,24},{24,16},{1,9},{9,1},{17,25},{25,17},{2,10},{10... | collective-permute-start | bytes 393224 | tf_op jit(solution)/shard_map/ppermute | solution.py:498
  54.6 19.1 %all-to-all-start.1 = ((bf16[32,24,256]{2,1,0:T(8,128)(2,1)}), bf16[32,24,256]{2,1,0:T(8,128)(2,1)S(1)}, u32[]{:S(2)}, u32[]{:S(2)}) async-start(bf16[32,24,256]{2,1,0:T(8,128)(2,1)} %get-tuple-element.62.refs_3_), calls=%async_computation.1 | async-start | bytes 786432 | tf_op jit(solution)/shard_map/all_to_all | solution.py:467
  66.0 32.8 %copy-start.5 = (s32[8,128]{1,0:T(8,128)S(1)}, s32[8,128]{1,0:T(8,128)}, u32[]{:S(2)}) copy-start(s32[8,128]{1,0:T(8,128)} %refs_2_.9) | copy-start | bytes 12292
  73.7 18.9 %all-to-all-start.2 = ((bf16[32,16,256]{2,1,0:T(8,128)(2,1)}), bf16[32,16,256]{2,1,0:T(8,128)(2,1)S(1)}, u32[]{:S(2)}, u32[]{:S(2)}) async-start(bf16[32,16,256]{2,1,0:T(8,128)(2,1)} %bitcast.10), calls=%async_computation.2 | async-start | bytes 524288 | tf_op jit(solution)/shard_map/all_to_all | solution.py:467
  79.6 7.7 %collective-permute-start.10 = (bf16[128,256]{1,0:T(8,128)(2,1)S(1)}, bf16[128,256]{1,0:T(8,128)(2,1)S(1)}, u32[]{:S(2)}, u32[]{:S(2)}) collective-permute-start(bf16[128,256]{1,0:T(8,128)(2,1)S(1)} %get-tuple-element.80), channel_id=1, source_target_pairs={{0,1},{1,0},{2,3},{3,2},{4,5},{5,4},{6,7},{7,6},{8,9},{9,8},{10,11... | collective-permute-start | bytes 196616 | tf_op jit(solution)/shard_map/ppermute | solution.py:498
  81.4 9.2 %collective-permute-start.11 = (bf16[128,256]{1,0:T(8,128)(2,1)S(1)}, bf16[128,256]{1,0:T(8,128)(2,1)S(1)}, u32[]{:S(2)}, u32[]{:S(2)}) collective-permute-start(bf16[128,256]{1,0:T(8,128)(2,1)S(1)} %get-tuple-element.81), channel_id=1, source_target_pairs={{0,2},{1,3},{2,0},{3,1},{4,6},{5,7},{6,4},{7,5},{8,10},{9,11},{10,... | collective-permute-start | bytes 196616 | tf_op jit(solution)/shard_map/ppermute | solution.py:498
  82.9 14.6 %collective-permute-start.12 = (bf16[128,256]{1,0:T(8,128)(2,1)S(1)}, bf16[128,256]{1,0:T(8,128)(2,1)S(1)}, u32[]{:S(2)}, u32[]{:S(2)}) collective-permute-start(bf16[128,256]{1,0:T(8,128)(2,1)S(1)} %get-tuple-element.82), channel_id=1, source_target_pairs={{0,3},{1,2},{2,1},{3,0},{4,7},{5,6},{6,5},{7,4},{8,11},{9,10},{10,... | collective-permute-start | bytes 196616 | tf_op jit(solution)/shard_map/ppermute | solution.py:498
  83.1 14.3 %collective-permute-start.13 = (bf16[128,256]{1,0:T(8,128)(2,1)S(1)}, bf16[128,256]{1,0:T(8,128)(2,1)S(1)}, u32[]{:S(2)}, u32[]{:S(2)}) collective-permute-start(bf16[128,256]{1,0:T(8,128)(2,1)S(1)} %get-tuple-element.83), channel_id=1, source_target_pairs={{0,4},{1,5},{2,6},{3,7},{4,0},{5,1},{6,2},{7,3},{8,12},{9,13},{10,... | collective-permute-start | bytes 196616 | tf_op jit(solution)/shard_map/ppermute | solution.py:498
  85.8 13.0 %collective-permute-start.14 = (bf16[128,256]{1,0:T(8,128)(2,1)S(1)}, bf16[128,256]{1,0:T(8,128)(2,1)S(1)}, u32[]{:S(2)}, u32[]{:S(2)}) collective-permute-start(bf16[128,256]{1,0:T(8,128)(2,1)S(1)} %get-tuple-element.84), channel_id=1, source_target_pairs={{0,5},{1,4},{2,7},{3,6},{4,1},{5,0},{6,3},{7,2},{8,13},{9,12},{10,... | collective-permute-start | bytes 196616 | tf_op jit(solution)/shard_map/ppermute | solution.py:498
  87.3 11.5 %collective-permute-start.15 = (bf16[128,256]{1,0:T(8,128)(2,1)S(1)}, bf16[128,256]{1,0:T(8,128)(2,1)S(1)}, u32[]{:S(2)}, u32[]{:S(2)}) collective-permute-start(bf16[128,256]{1,0:T(8,128)(2,1)S(1)} %get-tuple-element.85), channel_id=1, source_target_pairs={{0,6},{1,7},{2,4},{3,5},{4,2},{5,3},{6,0},{7,1},{8,14},{9,15},{10,... | collective-permute-start | bytes 196616 | tf_op jit(solution)/shard_map/ppermute | solution.py:498
  90.6 8.2 %collective-permute-start.16 = (bf16[128,256]{1,0:T(8,128)(2,1)S(1)}, bf16[128,256]{1,0:T(8,128)(2,1)S(1)}, u32[]{:S(2)}, u32[]{:S(2)}) collective-permute-start(bf16[128,256]{1,0:T(8,128)(2,1)S(1)} %get-tuple-element.86), channel_id=1, source_target_pairs={{0,7},{1,6},{2,5},{3,4},{4,3},{5,2},{6,1},{7,0},{8,15},{9,14},{10,... | collective-permute-start | bytes 196616 | tf_op jit(solution)/shard_map/ppermute | solution.py:498
  93.4 14.7 %all-to-all-start.3 = ((bf16[32,16,256]{2,1,0:T(8,128)(2,1)}), bf16[32,16,256]{2,1,0:T(8,128)(2,1)S(1)}, u32[]{:S(2)}, u32[]{:S(2)}) async-start(bf16[32,16,256]{2,1,0:T(8,128)(2,1)} %get-tuple-element.88), calls=%async_computation.3 | async-start | bytes 524288 | tf_op jit(solution)/shard_map/all_to_all | solution.py:467
  108.1 1.5 %collective-permute-start.17 = (bf16[32,16,256]{2,1,0:T(8,128)(2,1)S(1)}, bf16[32,16,256]{2,1,0:T(8,128)(2,1)S(1)}, u32[]{:S(2)}, u32[]{:S(2)}) collective-permute-start(bf16[32,16,256]{2,1,0:T(8,128)(2,1)S(1)} %all-to-all-done.3.refs_1_), channel_id=1, source_target_pairs={{0,8},{8,0},{16,24},{24,16},{1,9},{9,1},{17,25},{25,17},{2,10},{10... | collective-permute-start | bytes 786440 | tf_op jit(solution)/shard_map/ppermute | solution.py:498

commit v5 on v4

--- a/solution.py
+++ b/solution.py
@@ -130,11 +130,15 @@
         hot_ref[k] = onehot_rows(asked_ref[...], nets)
     for at in range(0, nets, STEP):
         rows = pl.ds(at, STEP)
-        total = sum_ref[rows, :] + mm(across, halo_ref[at // STEP]).T
+        pre_ref[rows, :] = mm(embeds_ref[rows, :], gnn_ref[:feat, :])
+    for at in range(0, nets, STEP):
+        rows = pl.ds(at, STEP)
+        total = mm(across, halo_ref[at // STEP]).T
+        total = total + sum_ref[rows, :]
         agg = (total * (1.0 / degree)).astype(bf16)
         agg_ref[rows, :] = agg
         agg_ref.flush(at + STEP)
-        pre = mm(embeds_ref[rows, :], gnn_ref[:feat, :]) + mm(agg, gnn_ref[feat:, :])
+        pre = pre_ref[rows, :] + mm(agg, gnn_ref[feat:, :])
         pre_ref[rows, :] = pre
         nets_ref[rows, :] = (embeds_ref[rows, :].astype(f32) + gelu_of(pre)).astype(bf16)
     for k, send_ref in enumerate(send_refs):
@@ -260,22 +264,23 @@
 
 
 def layer_grad_kernel(
-    cid_ref, grad_ref, slope_ref, gnn_ref, embeds_ref, agg_ref, halo_ref, *refs, far, peers, degree
+    cid_ref, grad_ref, slope_ref, gnn_ref, embeds_ref, agg_ref, halo_ref, *refs, far, order, degree
 ):
     asked_refs, refs = refs[:far], refs[far:]
     far_refs, refs = refs[:far], refs[far:]
     (rest_ref, agg_grad_ref, gnn_out_ref), refs = refs[:3], refs[3:]
-    back_refs, back_ref = refs[:-1], refs[-1]
+    back_refs, (back_ref, total_ref) = refs[:-2], refs[-2:]
     nets, feat = grad_ref.shape
     halo = back_refs[0].shape[0]
     top = jnp.zeros((feat, feat), f32)
     low = jnp.zeros((feat, feat), f32)
     returned = jnp.concatenate([ref[...] for ref in far_refs], 0)
     for at in range(0, nets, STEP):
+        hot = jnp.concatenate([onehot_cols(ref[...], at, STEP) for ref in asked_refs], 1)
+        total_ref[pl.ds(at, STEP), :] = mm(hot, returned)
+    for at in range(0, nets, STEP):
         rows = pl.ds(at, STEP)
-        hot = jnp.concatenate([onehot_cols(ref[...], at, STEP) for ref in asked_refs], 1)
-        total = mm(hot, returned)
-        total = total + grad_ref[rows, :]
+        total = total_ref[rows, :] + grad_ref[rows, :]
         pre_grad = (total * slope_ref[rows, :].astype(f32)).astype(bf16)
         agg_grad = mm_dims(pre_grad, gnn_ref[feat:, :], NT)
         agg_grad = (agg_grad * (1.0 / degree)).astype(bf16)
@@ -294,7 +299,7 @@
         back = back + mm(halo_ref[at // STEP], agg_grad_ref[pl.ds(at, STEP), :])
     back_ref[...] = back.astype(bf16)
     me = cid_ref[0]
-    for k, out_ref in enumerate(back_refs):
+    for k, out_ref in zip(order, back_refs, strict=True):
         out_ref[...] = back_ref[pl.ds(pl.multiple_of((me ^ k) * halo, halo), halo), :]
 
 
@@ -328,8 +333,8 @@
             gnn_ref.flush((d + 1) * share)
 
 
-def final_kernel(cid_ref, short_ref, send_ref, rest_ref, agg_grad_ref, own_ref, *refs):
-    got_refs, (out_ref, w2_ref, loss_ref, given_ref) = refs[:-4], refs[-4:]
+def final_kernel(cid_ref, short_ref, send_ref, agg_grad_ref, own_ref, rest_ref, *refs):
+    got_refs, (out_ref, w2_ref, loss_ref, sum_ref) = refs[:-4], refs[-4:]
     w2_ref[...] = short_ref[0:1, :]
     loss_ref[...] = short_ref[1:2, :]
     nets = out_ref.shape[0]
@@ -337,19 +342,23 @@
     scale = short_ref[2:3, :]
     got = jnp.concatenate([ref[...] for ref in got_refs], 0)
     sent = [send_ref[pl.ds(me ^ k, 1), :] for k in range(len(got_refs))]
-    given_ref[: got.shape[0], :] = got
-    hots = [
-        jnp.concatenate([onehot_cols(row, at, BLOCK) for row in sent], 1)
-        for at in range(0, nets, BLOCK)
-    ]
-    given_ref[got.shape[0] :, :] = agg_grad_ref[...]
     for at in range(0, nets, BLOCK):
-        rows = pl.ds(at, BLOCK)
-        parts = [own_ref[i, rows, :] for i in range(own_ref.shape[0])]
-        total = mm(jnp.concatenate([hots[at // BLOCK]] + parts, 1), given_ref[...])
-        out_ref[rows, :] = ((total + rest_ref[rows, :]) * scale).astype(bf16)
-        if (at + BLOCK) * PARTS % nets == 0:
-            out_ref.flush(at + BLOCK)
+        hot = jnp.concatenate([onehot_cols(row, at, BLOCK) for row in sent], 1)
+        sum_ref[at : at + BLOCK, :] = mm(hot, got)
+    steps = own_ref.shape[0]
+    for half in range(2):
+        mine = range(half * steps // 2, (half + 1) * steps // 2)
+        given = agg_grad_ref[pl.ds(half * nets // 2, nets // 2), :]
+        for at in range(0, nets, BLOCK):
+            rows = pl.ds(at, BLOCK)
+            parts = jnp.concatenate([own_ref[i, rows, :] for i in mine], 1)
+            total = sum_ref[rows, :] + mm(parts, given)
+            if half == 0:
+                sum_ref[rows, :] = total
+                continue
+            out_ref[rows, :] = ((total + rest_ref[rows, :]) * scale).astype(bf16)
+            if (at + BLOCK) * PARTS % nets == 0:
+                out_ref.flush(at + BLOCK)
 
 
 SM = pl.BlockSpec(memory_space=pltpu.SMEM)
@@ -368,18 +377,26 @@
 
 
 class Load:
-    def __init__(self, source, target, sem):
-        self.target, self.shape, self.waited = target, source.shape, False
-        self.copy = pltpu.make_async_copy(source, target, sem)
-        self.copy.start()
-
-    def wait(self):
-        if not self.waited:
-            self.copy.wait()
-        self.waited = True
+    def __init__(self, source, target, sems, parts):
+        self.target, self.shape, self.waited = target, source.shape, 0
+        self.rows = source.shape[0] // parts
+        self.copies = []
+        for at in range(parts):
+            part = pl.ds(at * self.rows, self.rows)
+            self.copies.append(
+                pltpu.make_async_copy(source.at[part], target.at[part], sems.at[at])
+            )
+            self.copies[-1].start()
+
+    def wait(self, upto=None):
+        upto = self.shape[0] if upto is None else upto
+        while self.waited * self.rows < upto:
+            self.copies[self.waited].wait()
+            self.waited += 1
 
     def __getitem__(self, index):
-        self.wait()
+        first = index[0] if isinstance(index, tuple) else index
+        self.wait(first + 1 if isinstance(first, int) else None)
         return self.target[index]
 
 
@@ -413,7 +430,7 @@
             copy.wait()
 
 
-def call(kernel, name, outs, args, scratch=(), mib=32, flops=1):
+def call(kernel, name, outs, args, scratch=(), mib=32, flops=1, halves=-1):
     ins = [kind for _, kind in args]
     kinds = [kind for _, _, kind in outs]
     staged = [pltpu.VMEM(value.shape, value.dtype) for value, kind in args if kind == "H"]
@@ -429,7 +446,8 @@
         at = 0
         for i, kind in enumerate(ins):
             if kind == "H":
-                operands[i] = Load(operands[i], buffers[at], sems.at[at, 0])
+                parts = 2 if i == halves else 1
+                operands[i] = Load(operands[i], buffers[at], sems.at[at], parts)
                 at += 1
         for i, kind in enumerate(kinds):
             if kind == "H":
@@ -605,8 +623,9 @@
         [pltpu.VMEM((regions * slots, feat), bf16)],
         flops=LOCAL,
     )
+    order = [0, 1, *range(peers - 1, 1, -1)]
     rest, agg_grad, gnn_part, *backs = call(
-        functools.partial(layer_grad_kernel, far=far, peers=peers, degree=degree),
+        functools.partial(layer_grad_kernel, far=far, order=order, degree=degree),
         "layer_grad",
         out("H", bf16, nets, feat) * 2
         + out("H", bf16, 2 * feat, feat)
@@ -616,13 +635,13 @@
         + v(gnn_weight, embeds)
         + h(aggregate, from_halo)
         + v(*asked[near:], *sum(returned[near:], [])),
-        [pltpu.VMEM((halo_rows, feat), bf16)],
+        [pltpu.VMEM((halo_rows, feat), bf16), pltpu.VMEM((nets, feat), f32)],
         flops=10**10,
     )
     gnn_part, w1_got = lax.optimization_barrier((gnn_part, w1_got))
     gnn_got = exchange(gnn_part.reshape(devices, share, feat), BOTH)
-    returned_halo = {k: permute(backs[k], k, "dom") for k in range(peers - 1, 0, -1)}
-    returned_halo = [backs[0]] + [returned_halo[k] for k in range(1, peers)]
+    backs = dict(zip(order, backs, strict=True))
+    returned_halo = [backs[0]] + [permute(backs[k], k, "dom") for k in range(1, peers)]
 
     wide, short = call(
         functools.partial(share_kernel, nets_total=nets * devices, doms=peers),
@@ -637,9 +656,10 @@
         final_kernel,
         "embeds_grads",
         out("H", bf16, nets, feat) + out("V", f32, 1, hid) * 2,
-        [(cid, "S")] + v(short, halo_send) + h(rest, agg_grad, own) + v(*returned_halo),
-        [pltpu.VMEM((halo_rows + nets, feat), bf16)],
+        [(cid, "S")] + v(short, halo_send) + h(agg_grad, own, rest) + v(*returned_halo),
+        [pltpu.VMEM((nets, feat), f32)],
         flops=FINAL,
+        halves=4,
     )
     spread, w2_grad = lax.optimization_barrier((spread, w2_grad))
     w1_grad, gnn_grad = call(

time: 111 us -> 109 us (0.982)
  Pallas kernels: 58.4 us -> 54.8 us
  waiting for transfers between devices: 8.27 us -> 10.4 us
    pallas_call x10, Pallas kernels: 49.8 us -> 46.2 us  [call(): pl.pallas_call(body, out_shape=[(in_hbm if kind == 'H' else shape)(dims,...]
    all_to_all x4, waiting for transfers between devices: 3.91 us -> 6.02 us  [exchange(): return lax.all_to_all(value, axis, split_axis=0, concat_axis=0, tiled=True)]
  transfers between devices with their start and end apart: 22 -> 22, of which waited for: 5 -> 6; matrix products, arithmetic and copies ran while one was open for 0% -> 0% of each run, Pallas kernels for 48% -> 46%
where the time goes in v5:
time: 109 us; the launch traced here: 108 us
  Pallas kernels  54.8 us (50%)
  starting transfers between devices  41.5 us (38%)
  waiting for transfers between devices  10.4 us (10%)
  between operations  1.1 us (1%)
    pallas_call x10, Pallas kernels, call(): pl.pallas_call(body, out_shape=[(in_hbm if kind == 'H' else shape)(dims,...  46.2 us
    all_to_all x4, starting transfers between devices, exchange(): return lax.all_to_all(value, axis, split_axis=0, concat_axis=0, tiled=True)  21.3 us
    ppermute x18, starting transfers between devices, permute(): return lax.ppermute(value, axis, [(i, i ^ k) for i in range(size)])  20.3 us
    pallas_call x1, Pallas kernels, local(): pl.pallas_call(adjacency_kernel, grid=(steps,), in_specs=[pl.BlockSpec((d...  8.57 us
    all_to_all x4, waiting for transfers between devices, exchange(): return lax.all_to_all(value, axis, split_axis=0, concat_axis=0, tiled=True)  6.02 us
    ppermute x18, waiting for transfers between devices, permute(): return lax.ppermute(value, axis, [(i, i ^ k) for i in range(size)])  4.38 us
  transfers between devices with their start and end apart: 22, of which 6 were waited for; matrix products, arithmetic and copies ran while one was open for 0% of the time, Pallas kernels for 46%

profile of v5, /device:TPU:0, one launch (start us, length us, event | category | flops | bytes accessed | tf_op | source)
XLA Modules:
  0.0 108.4 jit_solution(18086843304194463433)
XLA Ops:
  0.7 3.5 %halo_gather.1 = bf16[1024,256]{1,0:T(8,128)(2,1)} custom-call(s32[8,128]{1,0:T(8,128)} %refs_2_.9, bf16[2048,256]{1,0:T(8,128)(2,1)} %refs_4_.5), custom_call_target="tpu_custom_call" | custom-call | flops 1 | bytes 1 | tf_op jit(solution)/shard_map/halo_gather/pallas_call | solution.py:465
  4.2 7.3 %all-to-all-start = ((bf16[8,128,256]{2,1,0:T(8,128)(2,1)}), bf16[8,128,256]{2,1,0:T(8,128)(2,1)S(1)}, u32[]{:S(2)}, u32[]{:S(2)}) async-start(bf16[8,128,256]{2,1,0:T(8,128)(2,1)} %bitcast.3), calls=%async_computation | async-start | bytes 1048576 | tf_op jit(solution)/shard_map/all_to_all | solution.py:485
  11.5 1.6 %collective-permute-start = (s32[1,512]{1,0:T(1,128)S(1)}, s32[1,512]{1,0:T(1,128)S(1)}, u32[]{:S(2)}, u32[]{:S(2)}) collective-permute-start(s32[1,512]{1,0:T(1,128)S(1)} %get-tuple-element.97), channel_id=1, source_target_pairs={{0,16},{8,24},{16,0},{24,8},{1,17},{9,25},{17,1},{25,9},{2,18},{10... | collective-permute-start | bytes 6152 | tf_op jit(solution)/shard_map/ppermute | solution.py:516
  13.1 0.6 collective-permute-start.2
  13.7 8.6 %adjacency.1 = (bf16[4,2048,512]{2,1,0:T(8,128)(2,1)}, bf16[4,1024,512]{2,1,0:T(8,128)(2,1)}, f32[2048,256]{1,0:T(8,128)}) custom-call(s32[8,2048]{1,0:T(8,128)S(1)} %bitcast.9, bf16[2048,256]{1,0:T(8,128)(2,1)S(1)} %copy-done), custom_call_target="tpu_custom_call" | custom-call | flops 1 | bytes 1 | tf_op jit(solution)/shard_map/adjacency/pallas_call | solution.py:539
  22.3 0.0 collective-permute-done.refs_5_.refs_7_
  22.3 0.0 collective-permute-done.1.refs_6_.refs_8_
  22.3 3.7 %all-to-all-done = bf16[8,128,256]{2,1,0:T(8,128)(2,1)S(1)} async-done(((bf16[8,128,256]{2,1,0:T(8,128)(2,1)}), bf16[8,128,256]{2,1,0:T(8,128)(2,1)S(1)}, u32[]{:S(2)}, u32[]{:S(2)}) %all-to-all-start) | async-done | bytes 524320 | tf_op jit(solution)/shard_map/all_to_all | solution.py:485
  26.0 6.2 %layer.1 = (f32[2048,256]{1,0:T(8,128)S(1)}, bf16[2048,256]{1,0:T(8,128)(2,1)}, bf16[2048,256]{1,0:T(8,128)(2,1)S(1)}, bf16[512,256]{1,0:T(8,128)(2,1)S(1)}, bf16[512,256]{1,0:T(8,128)(2,1)S(1)}) custom-call(bf16[4,1024,512]{2,1,0:T(8,128)(2,1)} %get-tuple-element.50.refs_0_.refs_6_, f32[2048,256]{1,0:T(8,128)} %get-tuple-element.51.refs_1_, ...), custom_call_target="tpu_custom_call" | custom-call | flops 1 | bytes 1 | tf_op jit(solution)/shard_map/layer/pallas_call | solution.py:465
  32.2 1.6 %collective-permute-start.4 = (bf16[512,256]{1,0:T(8,128)(2,1)S(1)}, bf16[512,256]{1,0:T(8,128)(2,1)S(1)}, u32[]{:S(2)}, u32[]{:S(2)}) collective-permute-start(bf16[512,256]{1,0:T(8,128)(2,1)S(1)} %get-tuple-element.58), channel_id=1, source_target_pairs={{0,16},{8,24},{16,0},{24,8},{1,17},{9,25},{17,1},{25,9},{2,18},{10... | collective-permute-start | bytes 786440 | tf_op jit(solution)/shard_map/ppermute | solution.py:516
  33.7 0.0 collective-permute-start.5
  33.7 0.0 collective-permute-done.2.refs_6_.refs_5_
  33.7 0.0 copy-start.11
  33.7 0.0 copy-start.2
  33.7 0.0 copy-start.8
  33.8 0.0 copy-start.9
  33.8 7.0 %victims.1 = (bf16[4,512,256]{2,1,0:T(8,128)(2,1)}, f32[4,512,256]{2,1,0:T(8,128)S(1)}, bf16[2048,256]{1,0:T(8,128)(2,1)}, bf16[512,256]{1,0:T(8,128)(2,1)S(1)}, bf16[512,256]{1,0:T(8,128)(2,1)S(1)}) custom-call(s32[1]{0:T(128)} %bitcast.1.refs_0_, s32[4,512]{1,0:T(4,128)S(1)} %copy-done.4, bf16[2048,256]{1,0:T(8,128)(2,1)S(1)} %get-tuple-element.52.refs_2_, ...), custom_call_target="tpu_custom_call" | custom-call | flops 10000000000 | bytes 1 | tf_op jit(solution)/shard_map/victims/pallas_call | solution.py:465
  40.8 0.7 collective-permute-start.3
  41.5 2.0 %collective-permute-done.5.refs_7_.refs_10_ = bf16[512,256]{1,0:T(8,128)(2,1)S(1)} collective-permute-done((bf16[512,256]{1,0:T(8,128)(2,1)S(1)}, bf16[512,256]{1,0:T(8,128)(2,1)S(1)}, u32[]{:S(2)}, u32[]{:S(2)}) %collective-permute-start.5) | collective-permute-done | bytes 262176 | tf_op jit(solution)/shard_map/ppermute | solution.py:516
  43.6 2.5 %pairs.2 = (bf16[2,512,256]{2,1,0:T(8,128)(2,1)}, f32[8,256]{1,0:T(8,128)S(1)}, bf16[512,256]{1,0:T(8,128)(2,1)S(1)}, bf16[512,256]{1,0:T(8,128)(2,1)S(1)}) custom-call(s32[1]{0:T(128)} %bitcast.1.refs_0_, s32[1,4]{1,0:T(1,128)S(1)} %copy-done.9, f32[4,512]{1,0:T(4,128)S(1)} %copy-done.8, f32[4,512,256]{2,1,0:T(8,128)S(1)} %get-tuple-element.54.refs_3_, ...), custom_call_target="tpu_custom_call" | custom-call | flops 2000000000 | bytes 1 | tf_op jit(solution)/shard_map/pairs/pallas_call | solution.py:465
  46.1 0.6 collective-permute-start.8
  46.7 1.6 %collective-permute-start.9 = (bf16[512,256]{1,0:T(8,128)(2,1)S(1)}, bf16[512,256]{1,0:T(8,128)(2,1)S(1)}, u32[]{:S(2)}, u32[]{:S(2)}) collective-permute-start(bf16[512,256]{1,0:T(8,128)(2,1)S(1)} %get-tuple-element.71), channel_id=1, source_target_pairs={{0,24},{8,16},{16,8},{24,0},{1,25},{9,17},{17,9},{25,1},{2,26},{10... | collective-permute-start | bytes 786440 | tf_op jit(solution)/shard_map/ppermute | solution.py:516
  48.3 0.0 collective-permute-done.3.refs_7_
  48.3 4.6 %pairs.3 = (bf16[2,512,256]{2,1,0:T(8,128)(2,1)}, bf16[32,24,256]{2,1,0:T(8,128)(2,1)}, bf16[256,256]{1,0:T(8,128)(2,1)S(1)}, bf16[256,256]{1,0:T(8,128)(2,1)S(1...) custom-call(s32[1]{0:T(128)} %bitcast.1.refs_0_, s32[1,4]{1,0:T(1,128)S(1)} %copy-done.9, ...), custom_call_target="tpu_custom_call" | custom-call | flops 2000000000 | bytes 1 | tf_op jit(solution)/shard_map/pairs/pallas_call | solution.py:465
  52.9 0.1 collective-permute-start.6
  53.0 0.5 collective-permute-start.7
  53.5 5.2 %all-to-all-start.1 = ((bf16[32,24,256]{2,1,0:T(8,128)(2,1)}), bf16[32,24,256]{2,1,0:T(8,128)(2,1)S(1)}, u32[]{:S(2)}, u32[]{:S(2)}) async-start(bf16[32,24,256]{2,1,0:T(8,128)(2,1)} %get-tuple-element.62.refs_3_), calls=%async_computation.1 | async-start | bytes 786432 | tf_op jit(solution)/shard_map/all_to_all | solution.py:485
  58.7 6.2 %local_grads.1.refs_1_ = f32[2048,256]{1,0:T(8,128)} custom-call(s32[1]{0:T(128)} %bitcast.1.refs_0_, s32[4,512]{1,0:T(4,128)S(1)} %copy-done.4, bf16[512,256]{1,0:T(8,128)(2,1)} %refs_2_.8, bf16[32,24,256]{2,1,0:T(8,128)(2,1)} %get-tuple-element.62.refs_3_, s32[1,512]{1,0:T(1,128)S(1)} %get-tuple-element.98.refs_5_.refs_4_, ...), custom_call_target="tpu_custom_call" | custom-call | flops 1 | bytes 1 | tf_op jit(solution)/shard_map/local_grads/pallas_call | solution.py:465
  64.9 0.0 collective-permute-done.8.refs_9_
  64.9 0.0 copy-start.5
  64.9 6.2 %layer_grad.1 = (bf16[2048,256]{1,0:T(8,128)(2,1)}, bf16[2048,256]{1,0:T(8,128)(2,1)}, bf16[512,256]{1,0:T(8,128)(2,1)}, bf16[128,256]{1,0:T(8,128)(2,1)S(1)}, b...) custom-call(s32[1]{0:T(128)} %bitcast.refs_0_, ...), custom_call_target="tpu_custom_call" | custom-call | flops 10000000000 | bytes 1 | tf_op jit(solution)/shard_map/layer_grad/pallas_call | solution.py:465
  71.2 1.1 all-to-all-done.1.refs_0_
  72.2 4.8 %all-to-all-start.2 = ((bf16[32,16,256]{2,1,0:T(8,128)(2,1)}), bf16[32,16,256]{2,1,0:T(8,128)(2,1)S(1)}, u32[]{:S(2)}, u32[]{:S(2)}) async-start(bf16[32,16,256]{2,1,0:T(8,128)(2,1)} %bitcast.10), calls=%async_computation.2 | async-start | bytes 524288 | tf_op jit(solution)/shard_map/all_to_all | solution.py:485
  77.0 1.8 %collective-permute-start.10 = (bf16[128,256]{1,0:T(8,128)(2,1)S(1)}, bf16[128,256]{1,0:T(8,128)(2,1)S(1)}, u32[]{:S(2)}, u32[]{:S(2)}) collective-permute-start(bf16[128,256]{1,0:T(8,128)(2,1)S(1)} %get-tuple-element.80), channel_id=1, source_target_pairs={{0,1},{1,0},{2,3},{3,2},{4,5},{5,4},{6,7},{7,6},{8,9},{9,8},{10,11... | collective-permute-start | bytes 196616 | tf_op jit(solution)/shard_map/ppermute | solution.py:516
  78.9 1.5 %collective-permute-start.11 = (bf16[128,256]{1,0:T(8,128)(2,1)S(1)}, bf16[128,256]{1,0:T(8,128)(2,1)S(1)}, u32[]{:S(2)}, u32[]{:S(2)}) collective-permute-start(bf16[128,256]{1,0:T(8,128)(2,1)S(1)} %get-tuple-element.81), channel_id=1, source_target_pairs={{0,2},{1,3},{2,0},{3,1},{4,6},{5,7},{6,4},{7,5},{8,10},{9,11},{10,... | collective-permute-start | bytes 196616 | tf_op jit(solution)/shard_map/ppermute | solution.py:516
  80.3 0.3 collective-permute-start.12
  80.6 2.7 %collective-permute-start.13 = (bf16[128,256]{1,0:T(8,128)(2,1)S(1)}, bf16[128,256]{1,0:T(8,128)(2,1)S(1)}, u32[]{:S(2)}, u32[]{:S(2)}) collective-permute-start(bf16[128,256]{1,0:T(8,128)(2,1)S(1)} %get-tuple-element.83), channel_id=1, source_target_pairs={{0,4},{1,5},{2,6},{3,7},{4,0},{5,1},{6,2},{7,3},{8,12},{9,13},{10,... | collective-permute-start | bytes 196616 | tf_op jit(solution)/shard_map/ppermute | solution.py:516
  83.3 1.5 %collective-permute-start.14 = (bf16[128,256]{1,0:T(8,128)(2,1)S(1)}, bf16[128,256]{1,0:T(8,128)(2,1)S(1)}, u32[]{:S(2)}, u32[]{:S(2)}) collective-permute-start(bf16[128,256]{1,0:T(8,128)(2,1)S(1)} %get-tuple-element.84), channel_id=1, source_target_pairs={{0,5},{1,4},{2,7},{3,6},{4,1},{5,0},{6,3},{7,2},{8,13},{9,12},{10,... | collective-permute-start | bytes 196616 | tf_op jit(solution)/shard_map/ppermute | solution.py:516
  84.7 3.3 %collective-permute-start.15 = (bf16[128,256]{1,0:T(8,128)(2,1)S(1)}, bf16[128,256]{1,0:T(8,128)(2,1)S(1)}, u32[]{:S(2)}, u32[]{:S(2)}) collective-permute-start(bf16[128,256]{1,0:T(8,128)(2,1)S(1)} %get-tuple-element.85), channel_id=1, source_target_pairs={{0,6},{1,7},{2,4},{3,5},{4,2},{5,3},{6,0},{7,1},{8,14},{9,15},{10,... | collective-permute-start | bytes 196616 | tf_op jit(solution)/shard_map/ppermute | solution.py:516
  88.1 2.0 %collective-permute-start.16 = (bf16[128,256]{1,0:T(8,128)(2,1)S(1)}, bf16[128,256]{1,0:T(8,128)(2,1)S(1)}, u32[]{:S(2)}, u32[]{:S(2)}) collective-permute-start(bf16[128,256]{1,0:T(8,128)(2,1)S(1)} %get-tuple-element.86), channel_id=1, source_target_pairs={{0,7},{1,6},{2,5},{3,4},{4,3},{5,2},{6,1},{7,0},{8,15},{9,14},{10,... | collective-permute-start | bytes 196616 | tf_op jit(solution)/shard_map/ppermute | solution.py:516
  90.1 0.8 shares.1
  90.9 4.0 %all-to-all-start.3 = ((bf16[32,16,256]{2,1,0:T(8,128)(2,1)}), bf16[32,16,256]{2,1,0:T(8,128)(2,1)S(1)}, u32[]{:S(2)}, u32[]{:S(2)}) async-start(bf16[32,16,256]{2,1,0:T(8,128)(2,1)} %get-tuple-element.88), calls=%async_computation.3 | async-start | bytes 524288 | tf_op jit(solution)/shard_map/all_to_all | solution.py:485
  94.9 1.3 %collective-permute-done.14.refs_11_ = bf16[128,256]{1,0:T(8,128)(2,1)S(1)} collective-permute-done((bf16[128,256]{1,0:T(8,128)(2,1)S(1)}, bf16[128,256]{1,0:T(8,128)(2,1)S(1)}, u32[]{:S(2)}, u32[]{:S(2)}) %collective-permute-start.14) | collective-permute-done | bytes 65568 | tf_op jit(solution)/shard_map/ppermute | solution.py:516
  96.2 8.0 %embeds_grads.1 = (bf16[2048,256]{1,0:T(8,128)(2,1)}, f32[1,256]{1,0:T(1,128)}, f32[1,256]{1,0:T(1,128)S(1)}) custom-call(s32[1]{0:T(128)} %bitcast.refs_0_, f32[8,256]{1,0:T(8,128)S(1)} %get-tuple-element.75.refs_1_, s32[8,128]{1,0:T(8,128)S(1)} %copy-done.5, bf16[2048,256]{1,0:T(8,128)(2,1)} %get-tuple-element.76.refs_3_, ...), custom_call_target="tpu_custom_call" | custom-call | flops 20000000000 | bytes 1 | tf_op jit(solution)/shard_map/embeds_grads/pallas_call | solution.py:465
  104.3 1.3 %all-to-all-done.3.refs_1_ = bf16[32,16,256]{2,1,0:T(8,128)(2,1)S(1)} async-done(((bf16[32,16,256]{2,1,0:T(8,128)(2,1)}), bf16[32,16,256]{2,1,0:T(8,128)(2,1)S(1)}, u32[]{:S(2)}, u32[]{:S(2)}) %all-to-all-start.3) | async-done | bytes 262176 | tf_op jit(solution)/shard_map/all_to_all | solution.py:485
  105.6 0.5 slice.3
  106.1 1.0 collective-permute-done.17.refs_2_
  107.1 1.1 %unpack.1 = (f32[512,256]{1,0:T(8,128)}, f32[512,256]{1,0:T(8,128)}) custom-call(s32[1]{0:T(128)} %bitcast.1.refs_0_, bf16[32,16,256]{2,1,0:T(8,128)(2,1)S(1)} %all-to-all-done.3.refs_1_, bf16[32,16,256]{2,1,0:T(8,128)(2,1)S(1)} %collective-permute-done.17.refs_2_), custom_call_target="tpu_custom_call" | custom-call | flops 1 | bytes 1 | tf_op jit(solution)/shard_map/unpack/pallas_call | solution.py:465
  (34 shorter events, 0.1 us)
Async XLA Ops:
  0.6 13.1 %copy-start = (bf16[2048,256]{1,0:T(8,128)(2,1)S(1)}, bf16[2048,256]{1,0:T(8,128)(2,1)}, u32[]{:S(2)}) copy-start(bf16[2048,256]{1,0:T(8,128)(2,1)} %refs_4_.5) | copy-start | bytes 3145732
  0.6 10.9 %copy-start.10 = (s32[4,512]{1,0:T(4,128)S(1)}, s32[4,512]{1,0:T(4,128)}, u32[]{:S(2)}) copy-start(s32[4,512]{1,0:T(4,128)} %param.15) | copy-start | bytes 24580
  0.7 13.1 %copy-start.3 = (s32[2048,8]{0,1:T(8,128)S(1)}, s32[2048,8]{0,1:T(8,128)}, u32[]{:S(2)}) copy-start(s32[2048,8]{0,1:T(8,128)} %param.11) | copy-start | bytes 196612
  0.7 25.3 %copy-start.1 = (bf16[512,256]{1,0:T(8,128)(2,1)S(1)}, bf16[512,256]{1,0:T(8,128)(2,1)}, u32[]{:S(2)}) copy-start(bf16[512,256]{1,0:T(8,128)(2,1)} %refs_3_.5) | copy-start | bytes 786436
  4.2 21.8 %all-to-all-start = ((bf16[8,128,256]{2,1,0:T(8,128)(2,1)}), bf16[8,128,256]{2,1,0:T(8,128)(2,1)S(1)}, u32[]{:S(2)}, u32[]{:S(2)}) async-start(bf16[8,128,256]{2,1,0:T(8,128)(2,1)} %bitcast.3), calls=%async_computation | async-start | bytes 1048576 | tf_op jit(solution)/shard_map/all_to_all | solution.py:485
  11.5 10.8 %collective-permute-start = (s32[1,512]{1,0:T(1,128)S(1)}, s32[1,512]{1,0:T(1,128)S(1)}, u32[]{:S(2)}, u32[]{:S(2)}) collective-permute-start(s32[1,512]{1,0:T(1,128)S(1)} %get-tuple-element.97), channel_id=1, source_target_pairs={{0,16},{8,24},{16,0},{24,8},{1,17},{9,25},{17,1},{25,9},{2,18},{10... | collective-permute-start | bytes 6152 | tf_op jit(solution)/shard_map/ppermute | solution.py:516
  13.1 9.2 %collective-permute-start.1 = (s32[1,512]{1,0:T(1,128)S(1)}, s32[1,512]{1,0:T(1,128)S(1)}, u32[]{:S(2)}, u32[]{:S(2)}) collective-permute-start(s32[1,512]{1,0:T(1,128)S(1)} %get-tuple-element.96), channel_id=1, source_target_pairs={{0,24},{8,16},{16,8},{24,0},{1,25},{9,17},{17,9},{25,1},{2,26},{10... | collective-permute-start | bytes 6152 | tf_op jit(solution)/shard_map/ppermute | solution.py:516
  13.1 20.6 %collective-permute-start.2 = (s32[1,512]{1,0:T(1,128)S(1)}, s32[1,512]{1,0:T(1,128)S(1)}, u32[]{:S(2)}, u32[]{:S(2)}) collective-permute-start(s32[1,512]{1,0:T(1,128)S(1)} %get-tuple-element.95), channel_id=1, source_target_pairs={{0,8},{8,0},{16,24},{24,16},{1,9},{9,1},{17,25},{25,17},{2,10},{10... | collective-permute-start | bytes 6152 | tf_op jit(solution)/shard_map/ppermute | solution.py:516
  26.0 7.7 %copy-start.4 = (s32[4,512]{1,0:T(4,128)S(1)}, s32[4,512]{1,0:T(4,128)}, u32[]{:S(2)}) copy-start(s32[4,512]{1,0:T(4,128)} %refs_1_.9) | copy-start | bytes 24580
  32.2 9.4 %collective-permute-start.4 = (bf16[512,256]{1,0:T(8,128)(2,1)S(1)}, bf16[512,256]{1,0:T(8,128)(2,1)S(1)}, u32[]{:S(2)}, u32[]{:S(2)}) collective-permute-start(bf16[512,256]{1,0:T(8,128)(2,1)S(1)} %get-tuple-element.58), channel_id=1, source_target_pairs={{0,16},{8,24},{16,0},{24,8},{1,17},{9,25},{17,1},{25,9},{2,18},{10... | collective-permute-start | bytes 786440 | tf_op jit(solution)/shard_map/ppermute | solution.py:516
  33.7 9.8 %collective-permute-start.5 = (bf16[512,256]{1,0:T(8,128)(2,1)S(1)}, bf16[512,256]{1,0:T(8,128)(2,1)S(1)}, u32[]{:S(2)}, u32[]{:S(2)}) collective-permute-start(bf16[512,256]{1,0:T(8,128)(2,1)S(1)} %get-tuple-element.59), channel_id=1, source_target_pairs={{0,24},{8,16},{16,8},{24,0},{1,25},{9,17},{17,9},{25,1},{2,26},{10... | collective-permute-start | bytes 786440 | tf_op jit(solution)/shard_map/ppermute | solution.py:516
  33.7 7.8 %copy-start.11 = (bf16[256]{0:T(256)(128)(2,1)S(1)}, bf16[256]{0:T(256)(128)(2,1)}, u32[]{:S(2)}) copy-start(bf16[256]{0:T(256)(128)(2,1)} %param.19) | copy-start | bytes 1540
  33.7 9.8 %copy-start.2 = (bf16[512,256]{1,0:T(8,128)(2,1)S(1)}, bf16[512,256]{1,0:T(8,128)(2,1)}, u32[]{:S(2)}) copy-start(bf16[512,256]{1,0:T(8,128)(2,1)} %refs_2_.8) | copy-start | bytes 786436
  33.7 9.8 %copy-start.8 = (f32[4,512]{1,0:T(4,128)S(1)}, f32[4,512]{1,0:T(4,128)}, u32[]{:S(2)}) copy-start(f32[4,512]{1,0:T(4,128)} %refs_2_.7) | copy-start | bytes 24580
  33.8 9.8 %copy-start.9 = (s32[1,4]{1,0:T(1,128)S(1)}, s32[1,4]{1,0:T(1,128)}, u32[]{:S(2)}) copy-start(s32[1,4]{1,0:T(1,128)} %refs_1_.8) | copy-start | bytes 52
  40.8 7.5 %collective-permute-start.3 = (bf16[512,256]{1,0:T(8,128)(2,1)S(1)}, bf16[512,256]{1,0:T(8,128)(2,1)S(1)}, u32[]{:S(2)}, u32[]{:S(2)}) collective-permute-start(bf16[512,256]{1,0:T(8,128)(2,1)S(1)} %get-tuple-element.56), channel_id=1, source_target_pairs={{0,8},{8,0},{16,24},{24,16},{1,9},{9,1},{17,25},{25,17},{2,10},{10... | collective-permute-start | bytes 786440 | tf_op jit(solution)/shard_map/ppermute | solution.py:516
  41.5 4.5 %copy-start.6 = (bf16[512,256]{1,0:T(8,128)(2,1)}, bf16[512,256]{1,0:T(8,128)(2,1)S(1)}, u32[]{:S(2)}) copy-start(bf16[512,256]{1,0:T(8,128)(2,1)S(1)} %collective-permute-done.4.refs_6_.refs_9_) | copy-start | bytes 786436
  43.6 2.5 %copy-start.7 = (bf16[512,256]{1,0:T(8,128)(2,1)}, bf16[512,256]{1,0:T(8,128)(2,1)S(1)}, u32[]{:S(2)}) copy-start(bf16[512,256]{1,0:T(8,128)(2,1)S(1)} %collective-permute-done.5.refs_7_.refs_10_) | copy-start | bytes 786436
  46.1 18.8 %collective-permute-start.8 = (bf16[512,256]{1,0:T(8,128)(2,1)S(1)}, bf16[512,256]{1,0:T(8,128)(2,1)S(1)}, u32[]{:S(2)}, u32[]{:S(2)}) collective-permute-start(bf16[512,256]{1,0:T(8,128)(2,1)S(1)} %get-tuple-element.70), channel_id=1, source_target_pairs={{0,16},{8,24},{16,0},{24,8},{1,17},{9,25},{17,1},{25,9},{2,18},{10... | collective-permute-start | bytes 786440 | tf_op jit(solution)/shard_map/ppermute | solution.py:516
  46.7 18.2 %collective-permute-start.9 = (bf16[512,256]{1,0:T(8,128)(2,1)S(1)}, bf16[512,256]{1,0:T(8,128)(2,1)S(1)}, u32[]{:S(2)}, u32[]{:S(2)}) collective-permute-start(bf16[512,256]{1,0:T(8,128)(2,1)S(1)} %get-tuple-element.71), channel_id=1, source_target_pairs={{0,24},{8,16},{16,8},{24,0},{1,25},{9,17},{17,9},{25,1},{2,26},{10... | collective-permute-start | bytes 786440 | tf_op jit(solution)/shard_map/ppermute | solution.py:516
  52.9 5.8 %collective-permute-start.6 = (bf16[256,256]{1,0:T(8,128)(2,1)}, bf16[256,256]{1,0:T(8,128)(2,1)S(1)}, u32[]{:S(2)}, u32[]{:S(2)}) collective-permute-start(bf16[256,256]{1,0:T(8,128)(2,1)} %get-tuple-element.65), channel_id=1, source_target_pairs={{0,8},{8,0},{16,24},{24,16},{1,9},{9,1},{17,25},{25,17},{2,10},{10... | collective-permute-start | bytes 393224 | tf_op jit(solution)/shard_map/ppermute | solution.py:516
  53.0 5.7 %collective-permute-start.7 = (bf16[256,256]{1,0:T(8,128)(2,1)S(1)}, bf16[256,256]{1,0:T(8,128)(2,1)S(1)}, u32[]{:S(2)}, u32[]{:S(2)}) collective-permute-start(bf16[256,256]{1,0:T(8,128)(2,1)S(1)} %get-tuple-element.66), channel_id=1, source_target_pairs={{0,8},{8,0},{16,24},{24,16},{1,9},{9,1},{17,25},{25,17},{2,10},{10... | collective-permute-start | bytes 393224 | tf_op jit(solution)/shard_map/ppermute | solution.py:516
  53.5 18.7 %all-to-all-start.1 = ((bf16[32,24,256]{2,1,0:T(8,128)(2,1)}), bf16[32,24,256]{2,1,0:T(8,128)(2,1)S(1)}, u32[]{:S(2)}, u32[]{:S(2)}) async-start(bf16[32,24,256]{2,1,0:T(8,128)(2,1)} %get-tuple-element.62.refs_3_), calls=%async_computation.1 | async-start | bytes 786432 | tf_op jit(solution)/shard_map/all_to_all | solution.py:485
  64.9 31.3 %copy-start.5 = (s32[8,128]{1,0:T(8,128)S(1)}, s32[8,128]{1,0:T(8,128)}, u32[]{:S(2)}) copy-start(s32[8,128]{1,0:T(8,128)} %refs_2_.9) | copy-start | bytes 12292
  72.2 17.8 %all-to-all-start.2 = ((bf16[32,16,256]{2,1,0:T(8,128)(2,1)}), bf16[32,16,256]{2,1,0:T(8,128)(2,1)S(1)}, u32[]{:S(2)}, u32[]{:S(2)}) async-start(bf16[32,16,256]{2,1,0:T(8,128)(2,1)} %bitcast.10), calls=%async_computation.2 | async-start | bytes 524288 | tf_op jit(solution)/shard_map/all_to_all | solution.py:485
  77.0 7.7 %collective-permute-start.10 = (bf16[128,256]{1,0:T(8,128)(2,1)S(1)}, bf16[128,256]{1,0:T(8,128)(2,1)S(1)}, u32[]{:S(2)}, u32[]{:S(2)}) collective-permute-start(bf16[128,256]{1,0:T(8,128)(2,1)S(1)} %get-tuple-element.80), channel_id=1, source_target_pairs={{0,1},{1,0},{2,3},{3,2},{4,5},{5,4},{6,7},{7,6},{8,9},{9,8},{10,11... | collective-permute-start | bytes 196616 | tf_op jit(solution)/shard_map/ppermute | solution.py:516
  78.9 9.2 %collective-permute-start.11 = (bf16[128,256]{1,0:T(8,128)(2,1)S(1)}, bf16[128,256]{1,0:T(8,128)(2,1)S(1)}, u32[]{:S(2)}, u32[]{:S(2)}) collective-permute-start(bf16[128,256]{1,0:T(8,128)(2,1)S(1)} %get-tuple-element.81), channel_id=1, source_target_pairs={{0,2},{1,3},{2,0},{3,1},{4,6},{5,7},{6,4},{7,5},{8,10},{9,11},{10,... | collective-permute-start | bytes 196616 | tf_op jit(solution)/shard_map/ppermute | solution.py:516
  80.3 14.6 %collective-permute-start.12 = (bf16[128,256]{1,0:T(8,128)(2,1)S(1)}, bf16[128,256]{1,0:T(8,128)(2,1)S(1)}, u32[]{:S(2)}, u32[]{:S(2)}) collective-permute-start(bf16[128,256]{1,0:T(8,128)(2,1)S(1)} %get-tuple-element.82), channel_id=1, source_target_pairs={{0,3},{1,2},{2,1},{3,0},{4,7},{5,6},{6,5},{7,4},{8,11},{9,10},{10,... | collective-permute-start | bytes 196616 | tf_op jit(solution)/shard_map/ppermute | solution.py:516
  80.6 14.3 %collective-permute-start.13 = (bf16[128,256]{1,0:T(8,128)(2,1)S(1)}, bf16[128,256]{1,0:T(8,128)(2,1)S(1)}, u32[]{:S(2)}, u32[]{:S(2)}) collective-permute-start(bf16[128,256]{1,0:T(8,128)(2,1)S(1)} %get-tuple-element.83), channel_id=1, source_target_pairs={{0,4},{1,5},{2,6},{3,7},{4,0},{5,1},{6,2},{7,3},{8,12},{9,13},{10,... | collective-permute-start | bytes 196616 | tf_op jit(solution)/shard_map/ppermute | solution.py:516
  83.3 13.0 %collective-permute-start.14 = (bf16[128,256]{1,0:T(8,128)(2,1)S(1)}, bf16[128,256]{1,0:T(8,128)(2,1)S(1)}, u32[]{:S(2)}, u32[]{:S(2)}) collective-permute-start(bf16[128,256]{1,0:T(8,128)(2,1)S(1)} %get-tuple-element.84), channel_id=1, source_target_pairs={{0,5},{1,4},{2,7},{3,6},{4,1},{5,0},{6,3},{7,2},{8,13},{9,12},{10,... | collective-permute-start | bytes 196616 | tf_op jit(solution)/shard_map/ppermute | solution.py:516
  84.7 11.5 %collective-permute-start.15 = (bf16[128,256]{1,0:T(8,128)(2,1)S(1)}, bf16[128,256]{1,0:T(8,128)(2,1)S(1)}, u32[]{:S(2)}, u32[]{:S(2)}) collective-permute-start(bf16[128,256]{1,0:T(8,128)(2,1)S(1)} %get-tuple-element.85), channel_id=1, source_target_pairs={{0,6},{1,7},{2,4},{3,5},{4,2},{5,3},{6,0},{7,1},{8,14},{9,15},{10,... | collective-permute-start | bytes 196616 | tf_op jit(solution)/shard_map/ppermute | solution.py:516
  88.1 8.2 %collective-permute-start.16 = (bf16[128,256]{1,0:T(8,128)(2,1)S(1)}, bf16[128,256]{1,0:T(8,128)(2,1)S(1)}, u32[]{:S(2)}, u32[]{:S(2)}) collective-permute-start(bf16[128,256]{1,0:T(8,128)(2,1)S(1)} %get-tuple-element.86), channel_id=1, source_target_pairs={{0,7},{1,6},{2,5},{3,4},{4,3},{5,2},{6,1},{7,0},{8,15},{9,14},{10,... | collective-permute-start | bytes 196616 | tf_op jit(solution)/shard_map/ppermute | solution.py:516
  90.9 14.7 %all-to-all-start.3 = ((bf16[32,16,256]{2,1,0:T(8,128)(2,1)}), bf16[32,16,256]{2,1,0:T(8,128)(2,1)S(1)}, u32[]{:S(2)}, u32[]{:S(2)}) async-start(bf16[32,16,256]{2,1,0:T(8,128)(2,1)} %get-tuple-element.88), calls=%async_computation.3 | async-start | bytes 524288 | tf_op jit(solution)/shard_map/all_to_all | solution.py:485
  105.6 1.5 %collective-permute-start.17 = (bf16[32,16,256]{2,1,0:T(8,128)(2,1)S(1)}, bf16[32,16,256]{2,1,0:T(8,128)(2,1)S(1)}, u32[]{:S(2)}, u32[]{:S(2)}) collective-permute-start(bf16[32,16,256]{2,1,0:T(8,128)(2,1)S(1)} %all-to-all-done.3.refs_1_), channel_id=1, source_target_pairs={{0,8},{8,0},{16,24},{24,16},{1,9},{9,1},{17,25},{25,17},{2,10},{10... | collective-permute-start | bytes 786440 | tf_op jit(solution)/shard_map/ppermute | solution.py:516

commit v6 on v5

--- a/solution.py
+++ b/solution.py
@@ -243,13 +243,13 @@
     regions, slots = local_ref.shape
     asked_refs, refs = refs[:near], refs[near:]
     near_refs, refs = refs[: 2 * near], refs[2 * near :]
-    lin_refs, (grad_ref, vg_ref) = refs[: len(groups)], refs[len(groups) :]
+    lin_refs, (grad_ref, vg_ref, sum_ref) = refs[: len(groups)], refs[len(groups) :]
     nets, feat = grad_ref.shape
     me = rid_ref[0]
     returned = jnp.concatenate([near_ref[...] for near_ref in near_refs], 0)
     for at in range(0, nets, BLOCK):
         hot = jnp.concatenate([onehot_cols(ref[...], at, BLOCK) for ref in asked_refs], 1)
-        grad_ref[at : at + BLOCK, :] = mm(hot, returned)
+        sum_ref[at : at + BLOCK, :] = mm(hot, returned)
     for ref, ks in zip(lin_refs, groups, strict=True):
         for at, k in enumerate(ks):
             vg_ref[k * slots : (k + 1) * slots, :] = mm_dims(ref[at], w1_ref[:feat, :], NT).astype(
@@ -258,7 +258,8 @@
     listed = [local_ref[pl.ds(me ^ k, 1), :] for k in range(regions)]
     for at in range(0, nets, BLOCK):
         hot = jnp.concatenate([onehot_cols(row, at, BLOCK) for row in listed], 1)
-        grad_ref[at : at + BLOCK, :] += mm(hot, vg_ref[...])
+        total = sum_ref[at : at + BLOCK, :] + mm(hot, vg_ref[...])
+        grad_ref[at : at + BLOCK, :] = total.astype(bf16)
         if (at + BLOCK) * PARTS % nets == 0:
             grad_ref.flush(at + BLOCK)
 
@@ -280,7 +281,7 @@
         total_ref[pl.ds(at, STEP), :] = mm(hot, returned)
     for at in range(0, nets, STEP):
         rows = pl.ds(at, STEP)
-        total = total_ref[rows, :] + grad_ref[rows, :]
+        total = total_ref[rows, :] + grad_ref[rows, :].astype(f32)
         pre_grad = (total * slope_ref[rows, :].astype(f32)).astype(bf16)
         agg_grad = mm_dims(pre_grad, gnn_ref[feat:, :], NT)
         agg_grad = (agg_grad * (1.0 / degree)).astype(bf16)
@@ -613,14 +614,14 @@
     (local_grad,) = call(
         functools.partial(local_grad_kernel, groups=groups, near=near),
         "local_grads",
-        out("H", f32, nets, feat),
+        out("H", bf16, nets, feat),
         [(rid, "S")]
         + v(pair_local)
         + h(pair_w1)
         + [(w1_parts, "A")]
         + v(*asked[:near], *sum(returned[:near], []))
         + h(*lin_grads),
-        [pltpu.VMEM((regions * slots, feat), bf16)],
+        [pltpu.VMEM((regions * slots, feat), bf16), pltpu.VMEM((nets, feat), f32)],
         flops=LOCAL,
     )
     order = [0, 1, *range(peers - 1, 1, -1)]

time: 109 us -> 108 us (level)
  no operation moved by 1% of the time
where the time goes in v6:
time: 108 us
  Pallas kernels  54.3 us (50%)
  starting transfers between devices  41.1 us (38%)
  waiting for transfers between devices  10.8 us (10%)
  between operations  1.1 us (1%)
    pallas_call x10, Pallas kernels, call(): pl.pallas_call(body, out_shape=[(in_hbm if kind == 'H' else shape)(dims,...  45.8 us
    all_to_all x4, starting transfers between devices, exchange(): return lax.all_to_all(value, axis, split_axis=0, concat_axis=0, tiled=True)  20.9 us
    ppermute x18, starting transfers between devices, permute(): return lax.ppermute(value, axis, [(i, i ^ k) for i in range(size)])  20.3 us
    pallas_call x1, Pallas kernels, local(): pl.pallas_call(adjacency_kernel, grid=(steps,), in_specs=[pl.BlockSpec((d...  8.57 us
    all_to_all x4, waiting for transfers between devices, exchange(): return lax.all_to_all(value, axis, split_axis=0, concat_axis=0, tiled=True)  6.41 us
    ppermute x18, waiting for transfers between devices, permute(): return lax.ppermute(value, axis, [(i, i ^ k) for i in range(size)])  4.4 us
  transfers between devices with their start and end apart: 22, of which 6 were waited for; matrix products, arithmetic and copies ran while one was open for 0% of the time, Pallas kernels for 46%

profile of v6, /device:TPU:0, one launch (start us, length us, event | category | flops | bytes accessed | tf_op | source)
XLA Modules:
  0.0 108.0 jit_solution(15840354980454960525)
XLA Ops:
  0.7 3.5 %halo_gather.1 = bf16[1024,256]{1,0:T(8,128)(2,1)} custom-call(s32[8,128]{1,0:T(8,128)} %refs_2_.9, bf16[2048,256]{1,0:T(8,128)(2,1)} %refs_4_.5), custom_call_target="tpu_custom_call" | custom-call | flops 1 | bytes 1 | tf_op jit(solution)/shard_map/halo_gather/pallas_call | solution.py:466
  4.2 7.3 %all-to-all-start = ((bf16[8,128,256]{2,1,0:T(8,128)(2,1)}), bf16[8,128,256]{2,1,0:T(8,128)(2,1)S(1)}, u32[]{:S(2)}, u32[]{:S(2)}) async-start(bf16[8,128,256]{2,1,0:T(8,128)(2,1)} %bitcast.3), calls=%async_computation | async-start | bytes 1048576 | tf_op jit(solution)/shard_map/all_to_all | solution.py:486
  11.5 1.6 %collective-permute-start = (s32[1,512]{1,0:T(1,128)S(1)}, s32[1,512]{1,0:T(1,128)S(1)}, u32[]{:S(2)}, u32[]{:S(2)}) collective-permute-start(s32[1,512]{1,0:T(1,128)S(1)} %get-tuple-element.97), channel_id=1, source_target_pairs={{0,16},{8,24},{16,0},{24,8},{1,17},{9,25},{17,1},{25,9},{2,18},{10... | collective-permute-start | bytes 6152 | tf_op jit(solution)/shard_map/ppermute | solution.py:517
  13.1 0.0 collective-permute-start.1
  13.1 0.6 collective-permute-start.2
  13.7 8.6 %adjacency.1 = (bf16[4,2048,512]{2,1,0:T(8,128)(2,1)}, bf16[4,1024,512]{2,1,0:T(8,128)(2,1)}, f32[2048,256]{1,0:T(8,128)}) custom-call(s32[8,2048]{1,0:T(8,128)S(1)} %bitcast.9, bf16[2048,256]{1,0:T(8,128)(2,1)S(1)} %copy-done), custom_call_target="tpu_custom_call" | custom-call | flops 1 | bytes 1 | tf_op jit(solution)/shard_map/adjacency/pallas_call | solution.py:540
  22.3 0.0 collective-permute-done.refs_5_.refs_7_
  22.3 0.0 collective-permute-done.1.refs_6_.refs_8_
  22.3 3.7 %all-to-all-done = bf16[8,128,256]{2,1,0:T(8,128)(2,1)S(1)} async-done(((bf16[8,128,256]{2,1,0:T(8,128)(2,1)}), bf16[8,128,256]{2,1,0:T(8,128)(2,1)S(1)}, u32[]{:S(2)}, u32[]{:S(2)}) %all-to-all-start) | async-done | bytes 524320 | tf_op jit(solution)/shard_map/all_to_all | solution.py:486
  26.0 6.2 %layer.1 = (f32[2048,256]{1,0:T(8,128)S(1)}, bf16[2048,256]{1,0:T(8,128)(2,1)}, bf16[2048,256]{1,0:T(8,128)(2,1)S(1)}, bf16[512,256]{1,0:T(8,128)(2,1)S(1)}, bf16[512,256]{1,0:T(8,128)(2,1)S(1)}) custom-call(bf16[4,1024,512]{2,1,0:T(8,128)(2,1)} %get-tuple-element.50.refs_0_.refs_6_, f32[2048,256]{1,0:T(8,128)} %get-tuple-element.51.refs_1_, ...), custom_call_target="tpu_custom_call" | custom-call | flops 1 | bytes 1 | tf_op jit(solution)/shard_map/layer/pallas_call | solution.py:466
  32.2 1.6 %collective-permute-start.4 = (bf16[512,256]{1,0:T(8,128)(2,1)S(1)}, bf16[512,256]{1,0:T(8,128)(2,1)S(1)}, u32[]{:S(2)}, u32[]{:S(2)}) collective-permute-start(bf16[512,256]{1,0:T(8,128)(2,1)S(1)} %get-tuple-element.58), channel_id=1, source_target_pairs={{0,16},{8,24},{16,0},{24,8},{1,17},{9,25},{17,1},{25,9},{2,18},{10... | collective-permute-start | bytes 786440 | tf_op jit(solution)/shard_map/ppermute | solution.py:517
  33.7 0.0 copy-start.11
  33.7 0.0 copy-start.2
  33.7 0.0 copy-start.8
  33.8 0.0 copy-start.9
  33.8 7.0 %victims.1 = (bf16[4,512,256]{2,1,0:T(8,128)(2,1)}, f32[4,512,256]{2,1,0:T(8,128)S(1)}, bf16[2048,256]{1,0:T(8,128)(2,1)}, bf16[512,256]{1,0:T(8,128)(2,1)S(1)}, bf16[512,256]{1,0:T(8,128)(2,1)S(1)}) custom-call(s32[1]{0:T(128)} %bitcast.1.refs_0_, s32[4,512]{1,0:T(4,128)S(1)} %copy-done.4, bf16[2048,256]{1,0:T(8,128)(2,1)S(1)} %get-tuple-element.52.refs_2_, ...), custom_call_target="tpu_custom_call" | custom-call | flops 10000000000 | bytes 1 | tf_op jit(solution)/shard_map/victims/pallas_call | solution.py:466
  40.8 0.7 collective-permute-start.3
  41.5 0.0 collective-permute-done.4.refs_6_.refs_9_
  41.5 2.0 %collective-permute-done.5.refs_7_.refs_10_ = bf16[512,256]{1,0:T(8,128)(2,1)S(1)} collective-permute-done((bf16[512,256]{1,0:T(8,128)(2,1)S(1)}, bf16[512,256]{1,0:T(8,128)(2,1)S(1)}, u32[]{:S(2)}, u32[]{:S(2)}) %collective-permute-start.5) | collective-permute-done | bytes 262176 | tf_op jit(solution)/shard_map/ppermute | solution.py:517
  43.6 2.5 %pairs.2 = (bf16[2,512,256]{2,1,0:T(8,128)(2,1)}, f32[8,256]{1,0:T(8,128)S(1)}, bf16[512,256]{1,0:T(8,128)(2,1)S(1)}, bf16[512,256]{1,0:T(8,128)(2,1)S(1)}) custom-call(s32[1]{0:T(128)} %bitcast.1.refs_0_, s32[1,4]{1,0:T(1,128)S(1)} %copy-done.9, f32[4,512]{1,0:T(4,128)S(1)} %copy-done.8, f32[4,512,256]{2,1,0:T(8,128)S(1)} %get-tuple-element.54.refs_3_, ...), custom_call_target="tpu_custom_call" | custom-call | flops 2000000000 | bytes 1 | tf_op jit(solution)/shard_map/pairs/pallas_call | solution.py:466
  46.1 0.6 collective-permute-start.8
  46.7 1.6 %collective-permute-start.9 = (bf16[512,256]{1,0:T(8,128)(2,1)S(1)}, bf16[512,256]{1,0:T(8,128)(2,1)S(1)}, u32[]{:S(2)}, u32[]{:S(2)}) collective-permute-start(bf16[512,256]{1,0:T(8,128)(2,1)S(1)} %get-tuple-element.71), channel_id=1, source_target_pairs={{0,24},{8,16},{16,8},{24,0},{1,25},{9,17},{17,9},{25,1},{2,26},{10... | collective-permute-start | bytes 786440 | tf_op jit(solution)/shard_map/ppermute | solution.py:517
  48.3 0.0 collective-permute-done.3.refs_7_
  48.3 4.6 %pairs.3 = (bf16[2,512,256]{2,1,0:T(8,128)(2,1)}, bf16[32,24,256]{2,1,0:T(8,128)(2,1)}, bf16[256,256]{1,0:T(8,128)(2,1)S(1)}, bf16[256,256]{1,0:T(8,128)(2,1)S(1...) custom-call(s32[1]{0:T(128)} %bitcast.1.refs_0_, s32[1,4]{1,0:T(1,128)S(1)} %copy-done.9, ...), custom_call_target="tpu_custom_call" | custom-call | flops 2000000000 | bytes 1 | tf_op jit(solution)/shard_map/pairs/pallas_call | solution.py:466
  52.9 0.1 collective-permute-start.6
  53.0 0.5 collective-permute-start.7
  53.5 5.2 %all-to-all-start.1 = ((bf16[32,24,256]{2,1,0:T(8,128)(2,1)}), bf16[32,24,256]{2,1,0:T(8,128)(2,1)S(1)}, u32[]{:S(2)}, u32[]{:S(2)}) async-start(bf16[32,24,256]{2,1,0:T(8,128)(2,1)} %get-tuple-element.62.refs_3_), calls=%async_computation.1 | async-start | bytes 786432 | tf_op jit(solution)/shard_map/all_to_all | solution.py:486
  58.7 0.0 collective-permute-done.6.refs_8_
  58.7 6.1 %local_grads.1.refs_1_ = bf16[2048,256]{1,0:T(8,128)(2,1)} custom-call(s32[1]{0:T(128)} %bitcast.1.refs_0_, s32[4,512]{1,0:T(4,128)S(1)} %copy-done.4, bf16[512,256]{1,0:T(8,128)(2,1)} %refs_2_.8, bf16[32,24,256]{2,1,0:T(8,128)(2,1)} %get-tuple-element.62.refs_3_, s32[1,512]{1,0:T(1,128)S(1)} %get-tuple-element.98.refs_5_.refs_4_, ...), custom_call_target="tpu_custom_call" | custom-call | flops 1 | bytes 1 | tf_op jit(solution)/shard_map/local_grads/pallas_call | solution.py:466
  64.8 0.0 copy-start.5
  64.8 5.9 %layer_grad.1 = (bf16[2048,256]{1,0:T(8,128)(2,1)}, bf16[2048,256]{1,0:T(8,128)(2,1)}, bf16[512,256]{1,0:T(8,128)(2,1)}, bf16[128,256]{1,0:T(8,128)(2,1)S(1)}, b...) custom-call(s32[1]{0:T(128)} %bitcast.refs_0_, ...), custom_call_target="tpu_custom_call" | custom-call | flops 10000000000 | bytes 1 | tf_op jit(solution)/shard_map/layer_grad/pallas_call | solution.py:466
  70.8 1.5 %all-to-all-done.1.refs_0_ = bf16[32,24,256]{2,1,0:T(8,128)(2,1)S(1)} async-done(((bf16[32,24,256]{2,1,0:T(8,128)(2,1)}), bf16[32,24,256]{2,1,0:T(8,128)(2,1)S(1)}, u32[]{:S(2)}, u32[]{:S(2)}) %all-to-all-start.1) | async-done | bytes 393248 | tf_op jit(solution)/shard_map/all_to_all | solution.py:486
  72.2 4.4 %all-to-all-start.2 = ((bf16[32,16,256]{2,1,0:T(8,128)(2,1)}), bf16[32,16,256]{2,1,0:T(8,128)(2,1)S(1)}, u32[]{:S(2)}, u32[]{:S(2)}) async-start(bf16[32,16,256]{2,1,0:T(8,128)(2,1)} %bitcast.10), calls=%async_computation.2 | async-start | bytes 524288 | tf_op jit(solution)/shard_map/all_to_all | solution.py:486
  76.6 1.8 %collective-permute-start.10 = (bf16[128,256]{1,0:T(8,128)(2,1)S(1)}, bf16[128,256]{1,0:T(8,128)(2,1)S(1)}, u32[]{:S(2)}, u32[]{:S(2)}) collective-permute-start(bf16[128,256]{1,0:T(8,128)(2,1)S(1)} %get-tuple-element.80), channel_id=1, source_target_pairs={{0,1},{1,0},{2,3},{3,2},{4,5},{5,4},{6,7},{7,6},{8,9},{9,8},{10,11... | collective-permute-start | bytes 196616 | tf_op jit(solution)/shard_map/ppermute | solution.py:517
  78.5 1.5 %collective-permute-start.11 = (bf16[128,256]{1,0:T(8,128)(2,1)S(1)}, bf16[128,256]{1,0:T(8,128)(2,1)S(1)}, u32[]{:S(2)}, u32[]{:S(2)}) collective-permute-start(bf16[128,256]{1,0:T(8,128)(2,1)S(1)} %get-tuple-element.81), channel_id=1, source_target_pairs={{0,2},{1,3},{2,0},{3,1},{4,6},{5,7},{6,4},{7,5},{8,10},{9,11},{10,... | collective-permute-start | bytes 196616 | tf_op jit(solution)/shard_map/ppermute | solution.py:517
  79.9 0.3 collective-permute-start.12
  80.2 2.7 %collective-permute-start.13 = (bf16[128,256]{1,0:T(8,128)(2,1)S(1)}, bf16[128,256]{1,0:T(8,128)(2,1)S(1)}, u32[]{:S(2)}, u32[]{:S(2)}) collective-permute-start(bf16[128,256]{1,0:T(8,128)(2,1)S(1)} %get-tuple-element.83), channel_id=1, source_target_pairs={{0,4},{1,5},{2,6},{3,7},{4,0},{5,1},{6,2},{7,3},{8,12},{9,13},{10,... | collective-permute-start | bytes 196616 | tf_op jit(solution)/shard_map/ppermute | solution.py:517
  82.8 1.5 %collective-permute-start.14 = (bf16[128,256]{1,0:T(8,128)(2,1)S(1)}, bf16[128,256]{1,0:T(8,128)(2,1)S(1)}, u32[]{:S(2)}, u32[]{:S(2)}) collective-permute-start(bf16[128,256]{1,0:T(8,128)(2,1)S(1)} %get-tuple-element.84), channel_id=1, source_target_pairs={{0,5},{1,4},{2,7},{3,6},{4,1},{5,0},{6,3},{7,2},{8,13},{9,12},{10,... | collective-permute-start | bytes 196616 | tf_op jit(solution)/shard_map/ppermute | solution.py:517
  84.3 3.3 %collective-permute-start.15 = (bf16[128,256]{1,0:T(8,128)(2,1)S(1)}, bf16[128,256]{1,0:T(8,128)(2,1)S(1)}, u32[]{:S(2)}, u32[]{:S(2)}) collective-permute-start(bf16[128,256]{1,0:T(8,128)(2,1)S(1)} %get-tuple-element.85), channel_id=1, source_target_pairs={{0,6},{1,7},{2,4},{3,5},{4,2},{5,3},{6,0},{7,1},{8,14},{9,15},{10,... | collective-permute-start | bytes 196616 | tf_op jit(solution)/shard_map/ppermute | solution.py:517
  87.7 2.0 %collective-permute-start.16 = (bf16[128,256]{1,0:T(8,128)(2,1)S(1)}, bf16[128,256]{1,0:T(8,128)(2,1)S(1)}, u32[]{:S(2)}, u32[]{:S(2)}) collective-permute-start(bf16[128,256]{1,0:T(8,128)(2,1)S(1)} %get-tuple-element.86), channel_id=1, source_target_pairs={{0,7},{1,6},{2,5},{3,4},{4,3},{5,2},{6,1},{7,0},{8,15},{9,14},{10,... | collective-permute-start | bytes 196616 | tf_op jit(solution)/shard_map/ppermute | solution.py:517
  89.7 0.8 shares.1
  90.5 4.0 %all-to-all-start.3 = ((bf16[32,16,256]{2,1,0:T(8,128)(2,1)}), bf16[32,16,256]{2,1,0:T(8,128)(2,1)S(1)}, u32[]{:S(2)}, u32[]{:S(2)}) async-start(bf16[32,16,256]{2,1,0:T(8,128)(2,1)} %get-tuple-element.88), calls=%async_computation.3 | async-start | bytes 524288 | tf_op jit(solution)/shard_map/all_to_all | solution.py:486
  94.5 1.3 %collective-permute-done.14.refs_11_ = bf16[128,256]{1,0:T(8,128)(2,1)S(1)} collective-permute-done((bf16[128,256]{1,0:T(8,128)(2,1)S(1)}, bf16[128,256]{1,0:T(8,128)(2,1)S(1)}, u32[]{:S(2)}, u32[]{:S(2)}) %collective-permute-start.14) | collective-permute-done | bytes 65568 | tf_op jit(solution)/shard_map/ppermute | solution.py:517
  95.8 8.0 %embeds_grads.1 = (bf16[2048,256]{1,0:T(8,128)(2,1)}, f32[1,256]{1,0:T(1,128)}, f32[1,256]{1,0:T(1,128)S(1)}) custom-call(s32[1]{0:T(128)} %bitcast.refs_0_, f32[8,256]{1,0:T(8,128)S(1)} %get-tuple-element.75.refs_1_, s32[8,128]{1,0:T(8,128)S(1)} %copy-done.5, bf16[2048,256]{1,0:T(8,128)(2,1)} %get-tuple-element.76.refs_3_, ...), custom_call_target="tpu_custom_call" | custom-call | flops 20000000000 | bytes 1 | tf_op jit(solution)/shard_map/embeds_grads/pallas_call | solution.py:466
  103.9 1.3 %all-to-all-done.3.refs_1_ = bf16[32,16,256]{2,1,0:T(8,128)(2,1)S(1)} async-done(((bf16[32,16,256]{2,1,0:T(8,128)(2,1)}), bf16[32,16,256]{2,1,0:T(8,128)(2,1)S(1)}, u32[]{:S(2)}, u32[]{:S(2)}) %all-to-all-start.3) | async-done | bytes 262176 | tf_op jit(solution)/shard_map/all_to_all | solution.py:486
  105.1 0.5 slice.3
  105.7 1.0 collective-permute-done.17.refs_2_
  106.7 1.1 %unpack.1 = (f32[512,256]{1,0:T(8,128)}, f32[512,256]{1,0:T(8,128)}) custom-call(s32[1]{0:T(128)} %bitcast.1.refs_0_, bf16[32,16,256]{2,1,0:T(8,128)(2,1)S(1)} %all-to-all-done.3.refs_1_, bf16[32,16,256]{2,1,0:T(8,128)(2,1)S(1)} %collective-permute-done.17.refs_2_), custom_call_target="tpu_custom_call" | custom-call | flops 1 | bytes 1 | tf_op jit(solution)/shard_map/unpack/pallas_call | solution.py:466
  (34 shorter events, 0.1 us)
Async XLA Ops:
  0.6 13.1 %copy-start = (bf16[2048,256]{1,0:T(8,128)(2,1)S(1)}, bf16[2048,256]{1,0:T(8,128)(2,1)}, u32[]{:S(2)}) copy-start(bf16[2048,256]{1,0:T(8,128)(2,1)} %refs_4_.5) | copy-start | bytes 3145732
  0.6 10.9 %copy-start.10 = (s32[4,512]{1,0:T(4,128)S(1)}, s32[4,512]{1,0:T(4,128)}, u32[]{:S(2)}) copy-start(s32[4,512]{1,0:T(4,128)} %param.15) | copy-start | bytes 24580
  0.7 13.1 %copy-start.3 = (s32[2048,8]{0,1:T(8,128)S(1)}, s32[2048,8]{0,1:T(8,128)}, u32[]{:S(2)}) copy-start(s32[2048,8]{0,1:T(8,128)} %param.11) | copy-start | bytes 196612
  0.7 25.3 %copy-start.1 = (bf16[512,256]{1,0:T(8,128)(2,1)S(1)}, bf16[512,256]{1,0:T(8,128)(2,1)}, u32[]{:S(2)}) copy-start(bf16[512,256]{1,0:T(8,128)(2,1)} %refs_3_.5) | copy-start | bytes 786436
  4.2 21.8 %all-to-all-start = ((bf16[8,128,256]{2,1,0:T(8,128)(2,1)}), bf16[8,128,256]{2,1,0:T(8,128)(2,1)S(1)}, u32[]{:S(2)}, u32[]{:S(2)}) async-start(bf16[8,128,256]{2,1,0:T(8,128)(2,1)} %bitcast.3), calls=%async_computation | async-start | bytes 1048576 | tf_op jit(solution)/shard_map/all_to_all | solution.py:486
  11.5 10.8 %collective-permute-start = (s32[1,512]{1,0:T(1,128)S(1)}, s32[1,512]{1,0:T(1,128)S(1)}, u32[]{:S(2)}, u32[]{:S(2)}) collective-permute-start(s32[1,512]{1,0:T(1,128)S(1)} %get-tuple-element.97), channel_id=1, source_target_pairs={{0,16},{8,24},{16,0},{24,8},{1,17},{9,25},{17,1},{25,9},{2,18},{10... | collective-permute-start | bytes 6152 | tf_op jit(solution)/shard_map/ppermute | solution.py:517
  13.1 9.2 %collective-permute-start.1 = (s32[1,512]{1,0:T(1,128)S(1)}, s32[1,512]{1,0:T(1,128)S(1)}, u32[]{:S(2)}, u32[]{:S(2)}) collective-permute-start(s32[1,512]{1,0:T(1,128)S(1)} %get-tuple-element.96), channel_id=1, source_target_pairs={{0,24},{8,16},{16,8},{24,0},{1,25},{9,17},{17,9},{25,1},{2,26},{10... | collective-permute-start | bytes 6152 | tf_op jit(solution)/shard_map/ppermute | solution.py:517
  13.1 20.6 %collective-permute-start.2 = (s32[1,512]{1,0:T(1,128)S(1)}, s32[1,512]{1,0:T(1,128)S(1)}, u32[]{:S(2)}, u32[]{:S(2)}) collective-permute-start(s32[1,512]{1,0:T(1,128)S(1)} %get-tuple-element.95), channel_id=1, source_target_pairs={{0,8},{8,0},{16,24},{24,16},{1,9},{9,1},{17,25},{25,17},{2,10},{10... | collective-permute-start | bytes 6152 | tf_op jit(solution)/shard_map/ppermute | solution.py:517
  26.0 7.7 %copy-start.4 = (s32[4,512]{1,0:T(4,128)S(1)}, s32[4,512]{1,0:T(4,128)}, u32[]{:S(2)}) copy-start(s32[4,512]{1,0:T(4,128)} %refs_1_.9) | copy-start | bytes 24580
  32.2 9.4 %collective-permute-start.4 = (bf16[512,256]{1,0:T(8,128)(2,1)S(1)}, bf16[512,256]{1,0:T(8,128)(2,1)S(1)}, u32[]{:S(2)}, u32[]{:S(2)}) collective-permute-start(bf16[512,256]{1,0:T(8,128)(2,1)S(1)} %get-tuple-element.58), channel_id=1, source_target_pairs={{0,16},{8,24},{16,0},{24,8},{1,17},{9,25},{17,1},{25,9},{2,18},{10... | collective-permute-start | bytes 786440 | tf_op jit(solution)/shard_map/ppermute | solution.py:517
  33.7 9.8 %collective-permute-start.5 = (bf16[512,256]{1,0:T(8,128)(2,1)S(1)}, bf16[512,256]{1,0:T(8,128)(2,1)S(1)}, u32[]{:S(2)}, u32[]{:S(2)}) collective-permute-start(bf16[512,256]{1,0:T(8,128)(2,1)S(1)} %get-tuple-element.59), channel_id=1, source_target_pairs={{0,24},{8,16},{16,8},{24,0},{1,25},{9,17},{17,9},{25,1},{2,26},{10... | collective-permute-start | bytes 786440 | tf_op jit(solution)/shard_map/ppermute | solution.py:517
  33.7 7.8 %copy-start.11 = (bf16[256]{0:T(256)(128)(2,1)S(1)}, bf16[256]{0:T(256)(128)(2,1)}, u32[]{:S(2)}) copy-start(bf16[256]{0:T(256)(128)(2,1)} %param.19) | copy-start | bytes 1540
  33.7 9.8 %copy-start.2 = (bf16[512,256]{1,0:T(8,128)(2,1)S(1)}, bf16[512,256]{1,0:T(8,128)(2,1)}, u32[]{:S(2)}) copy-start(bf16[512,256]{1,0:T(8,128)(2,1)} %refs_2_.8) | copy-start | bytes 786436
  33.7 9.8 %copy-start.8 = (f32[4,512]{1,0:T(4,128)S(1)}, f32[4,512]{1,0:T(4,128)}, u32[]{:S(2)}) copy-start(f32[4,512]{1,0:T(4,128)} %refs_2_.7) | copy-start | bytes 24580
  33.8 9.8 %copy-start.9 = (s32[1,4]{1,0:T(1,128)S(1)}, s32[1,4]{1,0:T(1,128)}, u32[]{:S(2)}) copy-start(s32[1,4]{1,0:T(1,128)} %refs_1_.8) | copy-start | bytes 52
  40.8 7.5 %collective-permute-start.3 = (bf16[512,256]{1,0:T(8,128)(2,1)S(1)}, bf16[512,256]{1,0:T(8,128)(2,1)S(1)}, u32[]{:S(2)}, u32[]{:S(2)}) collective-permute-start(bf16[512,256]{1,0:T(8,128)(2,1)S(1)} %get-tuple-element.56), channel_id=1, source_target_pairs={{0,8},{8,0},{16,24},{24,16},{1,9},{9,1},{17,25},{25,17},{2,10},{10... | collective-permute-start | bytes 786440 | tf_op jit(solution)/shard_map/ppermute | solution.py:517
  41.5 4.6 %copy-start.6 = (bf16[512,256]{1,0:T(8,128)(2,1)}, bf16[512,256]{1,0:T(8,128)(2,1)S(1)}, u32[]{:S(2)}) copy-start(bf16[512,256]{1,0:T(8,128)(2,1)S(1)} %collective-permute-done.4.refs_6_.refs_9_) | copy-start | bytes 786436
  43.6 2.5 %copy-start.7 = (bf16[512,256]{1,0:T(8,128)(2,1)}, bf16[512,256]{1,0:T(8,128)(2,1)S(1)}, u32[]{:S(2)}) copy-start(bf16[512,256]{1,0:T(8,128)(2,1)S(1)} %collective-permute-done.5.refs_7_.refs_10_) | copy-start | bytes 786436
  46.1 18.7 %collective-permute-start.8 = (bf16[512,256]{1,0:T(8,128)(2,1)S(1)}, bf16[512,256]{1,0:T(8,128)(2,1)S(1)}, u32[]{:S(2)}, u32[]{:S(2)}) collective-permute-start(bf16[512,256]{1,0:T(8,128)(2,1)S(1)} %get-tuple-element.70), channel_id=1, source_target_pairs={{0,16},{8,24},{16,0},{24,8},{1,17},{9,25},{17,1},{25,9},{2,18},{10... | collective-permute-start | bytes 786440 | tf_op jit(solution)/shard_map/ppermute | solution.py:517
  46.7 18.1 %collective-permute-start.9 = (bf16[512,256]{1,0:T(8,128)(2,1)S(1)}, bf16[512,256]{1,0:T(8,128)(2,1)S(1)}, u32[]{:S(2)}, u32[]{:S(2)}) collective-permute-start(bf16[512,256]{1,0:T(8,128)(2,1)S(1)} %get-tuple-element.71), channel_id=1, source_target_pairs={{0,24},{8,16},{16,8},{24,0},{1,25},{9,17},{17,9},{25,1},{2,26},{10... | collective-permute-start | bytes 786440 | tf_op jit(solution)/shard_map/ppermute | solution.py:517
  52.9 5.8 %collective-permute-start.6 = (bf16[256,256]{1,0:T(8,128)(2,1)}, bf16[256,256]{1,0:T(8,128)(2,1)S(1)}, u32[]{:S(2)}, u32[]{:S(2)}) collective-permute-start(bf16[256,256]{1,0:T(8,128)(2,1)} %get-tuple-element.65), channel_id=1, source_target_pairs={{0,8},{8,0},{16,24},{24,16},{1,9},{9,1},{17,25},{25,17},{2,10},{10... | collective-permute-start | bytes 393224 | tf_op jit(solution)/shard_map/ppermute | solution.py:517
  53.0 5.7 %collective-permute-start.7 = (bf16[256,256]{1,0:T(8,128)(2,1)S(1)}, bf16[256,256]{1,0:T(8,128)(2,1)S(1)}, u32[]{:S(2)}, u32[]{:S(2)}) collective-permute-start(bf16[256,256]{1,0:T(8,128)(2,1)S(1)} %get-tuple-element.66), channel_id=1, source_target_pairs={{0,8},{8,0},{16,24},{24,16},{1,9},{9,1},{17,25},{25,17},{2,10},{10... | collective-permute-start | bytes 393224 | tf_op jit(solution)/shard_map/ppermute | solution.py:517
  53.5 18.7 %all-to-all-start.1 = ((bf16[32,24,256]{2,1,0:T(8,128)(2,1)}), bf16[32,24,256]{2,1,0:T(8,128)(2,1)S(1)}, u32[]{:S(2)}, u32[]{:S(2)}) async-start(bf16[32,24,256]{2,1,0:T(8,128)(2,1)} %get-tuple-element.62.refs_3_), calls=%async_computation.1 | async-start | bytes 786432 | tf_op jit(solution)/shard_map/all_to_all | solution.py:486
  64.8 31.0 %copy-start.5 = (s32[8,128]{1,0:T(8,128)S(1)}, s32[8,128]{1,0:T(8,128)}, u32[]{:S(2)}) copy-start(s32[8,128]{1,0:T(8,128)} %refs_2_.9) | copy-start | bytes 12292
  72.2 17.4 %all-to-all-start.2 = ((bf16[32,16,256]{2,1,0:T(8,128)(2,1)}), bf16[32,16,256]{2,1,0:T(8,128)(2,1)S(1)}, u32[]{:S(2)}, u32[]{:S(2)}) async-start(bf16[32,16,256]{2,1,0:T(8,128)(2,1)} %bitcast.10), calls=%async_computation.2 | async-start | bytes 524288 | tf_op jit(solution)/shard_map/all_to_all | solution.py:486
  76.6 7.7 %collective-permute-start.10 = (bf16[128,256]{1,0:T(8,128)(2,1)S(1)}, bf16[128,256]{1,0:T(8,128)(2,1)S(1)}, u32[]{:S(2)}, u32[]{:S(2)}) collective-permute-start(bf16[128,256]{1,0:T(8,128)(2,1)S(1)} %get-tuple-element.80), channel_id=1, source_target_pairs={{0,1},{1,0},{2,3},{3,2},{4,5},{5,4},{6,7},{7,6},{8,9},{9,8},{10,11... | collective-permute-start | bytes 196616 | tf_op jit(solution)/shard_map/ppermute | solution.py:517
  78.5 9.2 %collective-permute-start.11 = (bf16[128,256]{1,0:T(8,128)(2,1)S(1)}, bf16[128,256]{1,0:T(8,128)(2,1)S(1)}, u32[]{:S(2)}, u32[]{:S(2)}) collective-permute-start(bf16[128,256]{1,0:T(8,128)(2,1)S(1)} %get-tuple-element.81), channel_id=1, source_target_pairs={{0,2},{1,3},{2,0},{3,1},{4,6},{5,7},{6,4},{7,5},{8,10},{9,11},{10,... | collective-permute-start | bytes 196616 | tf_op jit(solution)/shard_map/ppermute | solution.py:517
  79.9 14.6 %collective-permute-start.12 = (bf16[128,256]{1,0:T(8,128)(2,1)S(1)}, bf16[128,256]{1,0:T(8,128)(2,1)S(1)}, u32[]{:S(2)}, u32[]{:S(2)}) collective-permute-start(bf16[128,256]{1,0:T(8,128)(2,1)S(1)} %get-tuple-element.82), channel_id=1, source_target_pairs={{0,3},{1,2},{2,1},{3,0},{4,7},{5,6},{6,5},{7,4},{8,11},{9,10},{10,... | collective-permute-start | bytes 196616 | tf_op jit(solution)/shard_map/ppermute | solution.py:517
  80.2 14.3 %collective-permute-start.13 = (bf16[128,256]{1,0:T(8,128)(2,1)S(1)}, bf16[128,256]{1,0:T(8,128)(2,1)S(1)}, u32[]{:S(2)}, u32[]{:S(2)}) collective-permute-start(bf16[128,256]{1,0:T(8,128)(2,1)S(1)} %get-tuple-element.83), channel_id=1, source_target_pairs={{0,4},{1,5},{2,6},{3,7},{4,0},{5,1},{6,2},{7,3},{8,12},{9,13},{10,... | collective-permute-start | bytes 196616 | tf_op jit(solution)/shard_map/ppermute | solution.py:517
  82.8 13.0 %collective-permute-start.14 = (bf16[128,256]{1,0:T(8,128)(2,1)S(1)}, bf16[128,256]{1,0:T(8,128)(2,1)S(1)}, u32[]{:S(2)}, u32[]{:S(2)}) collective-permute-start(bf16[128,256]{1,0:T(8,128)(2,1)S(1)} %get-tuple-element.84), channel_id=1, source_target_pairs={{0,5},{1,4},{2,7},{3,6},{4,1},{5,0},{6,3},{7,2},{8,13},{9,12},{10,... | collective-permute-start | bytes 196616 | tf_op jit(solution)/shard_map/ppermute | solution.py:517
  84.3 11.5 %collective-permute-start.15 = (bf16[128,256]{1,0:T(8,128)(2,1)S(1)}, bf16[128,256]{1,0:T(8,128)(2,1)S(1)}, u32[]{:S(2)}, u32[]{:S(2)}) collective-permute-start(bf16[128,256]{1,0:T(8,128)(2,1)S(1)} %get-tuple-element.85), channel_id=1, source_target_pairs={{0,6},{1,7},{2,4},{3,5},{4,2},{5,3},{6,0},{7,1},{8,14},{9,15},{10,... | collective-permute-start | bytes 196616 | tf_op jit(solution)/shard_map/ppermute | solution.py:517
  87.7 8.2 %collective-permute-start.16 = (bf16[128,256]{1,0:T(8,128)(2,1)S(1)}, bf16[128,256]{1,0:T(8,128)(2,1)S(1)}, u32[]{:S(2)}, u32[]{:S(2)}) collective-permute-start(bf16[128,256]{1,0:T(8,128)(2,1)S(1)} %get-tuple-element.86), channel_id=1, source_target_pairs={{0,7},{1,6},{2,5},{3,4},{4,3},{5,2},{6,1},{7,0},{8,15},{9,14},{10,... | collective-permute-start | bytes 196616 | tf_op jit(solution)/shard_map/ppermute | solution.py:517
  90.5 14.7 %all-to-all-start.3 = ((bf16[32,16,256]{2,1,0:T(8,128)(2,1)}), bf16[32,16,256]{2,1,0:T(8,128)(2,1)S(1)}, u32[]{:S(2)}, u32[]{:S(2)}) async-start(bf16[32,16,256]{2,1,0:T(8,128)(2,1)} %get-tuple-element.88), calls=%async_computation.3 | async-start | bytes 524288 | tf_op jit(solution)/shard_map/all_to_all | solution.py:486
  105.1 1.5 %collective-permute-start.17 = (bf16[32,16,256]{2,1,0:T(8,128)(2,1)S(1)}, bf16[32,16,256]{2,1,0:T(8,128)(2,1)S(1)}, u32[]{:S(2)}, u32[]{:S(2)}) collective-permute-start(bf16[32,16,256]{2,1,0:T(8,128)(2,1)S(1)} %all-to-all-done.3.refs_1_), channel_id=1, source_target_pairs={{0,8},{8,0},{16,24},{24,16},{1,9},{9,1},{17,25},{25,17},{2,10},{10... | collective-permute-start | bytes 786440 | tf_op jit(solution)/shard_map/ppermute | solution.py:517
